TPU v7x, 256 devices: a whole 4x4x8 slice. The times are simulated.
256 devices in a mesh: lat: 8 (over y, x_hi), lon: 32 (over x_lo, z, core).
Axes of the slice: x: 4 (x_hi: 2, x_lo: 2; x = x_hi * 2 + x_lo), y: 4, z: 8, core: 2. Of those that a mesh axis runs over, the one named last changes fastest.
Arguments:
- tokens: bfloat16 [192, 768, 512], P('lat', 'lon'), may hold values from -6 to 6
- cotangent: bfloat16 [192, 768, 512], P('lat', 'lon'), may hold values from -6 to 6
- norm_gain: float32 [512], replicated, may hold values from 0.5 to 1.5
- w_qkv: bfloat16 [512, 1536], replicated, may hold values from -8 to 8
- w_proj: bfloat16 [512, 512], replicated, may hold values from -0.25 to 0.25
- merge_gain: float32 [2048], replicated, may hold values from 0.5 to 1.5
- w_merge: bfloat16 [2048, 1024], replicated, may hold values from -0.125 to 0.125
- w_expand: bfloat16 [1024, 2048], replicated, may hold values from -0.1875 to 0.1875
- expand_gain: float32 [512], replicated, may hold values from 0.5 to 1.5
Outputs:
- d_tokens: bfloat16 [192, 768, 512], P('lat', 'lon')
- grad_qkv: float32 [512, 1536], P('lon')
- grad_proj: float32 [512, 512], P('lon')
All inputs are finite; a program needn't handle non-finite values.
Results may differ from a plain program's by a relative error of at most 0.04.
Values may be sent and summed in bfloat16 or wider, within the bound.
No kernel may reach another device: no remote copies, remote signals or barrier semaphores. Data moves between devices by JAX's collectives and lax.ppermute only.
A program may use at most 128 MiB of HBM per device.

v0:
```python
import functools

import jax
import jax.numpy as jnp
import numpy as np
from jax import lax
from jax.experimental import pallas as pl
from jax.experimental.pallas import tpu as pltpu
from jax.sharding import Mesh, PartitionSpec as P

HEADS = 8
HEAD = 64
WLAT = 6
WLON = 12
SLAT = 3
SLON = 6
D = 512
ROWS = 24
COLS = 24
WR = WLAT * COLS
NWR = 6
XROWS = WLAT * NWR
CROWS = 28
PAIRS = 13
QROWS = 160

EPSILON = 1e-05
MASKED = -1000000000.0
OUTSIDE = -3.0e38
BF = jnp.bfloat16
F32 = jnp.float32


def to_offsets(pairs, lead, span, padded):
    out = np.zeros((4 * padded, span), np.float32)
    for a in range(pairs):
        for rp in range(2):
            for col in range(COLS):
                q = (col % 2) * 2 + rp
                out[q * padded + a * 12 + col // 2, lead + (2 * a + rp) * COLS + col] = 1
    return out.astype(jnp.bfloat16)


def from_offsets():
    out = np.zeros((4, WR, 256), np.float32)
    for k in range(1, 5):
        for t in range(WR):
            f = WLAT * k + t // COLS
            col = t % COLS
            a, rp = divmod(f - 5, 2)
            q = (col % 2) * 2 + rp
            out[k - 1, t, q * 64 + 12 * a + col // 2 - 32 * (k - 1)] = 1
    return out.astype(jnp.bfloat16)


def dot(a, b):
    return jnp.dot(a, b, preferred_element_type=F32)


def dot_nt(a, b):
    return lax.dot_general(a, b, (((1,), (1,)), ((), ())), preferred_element_type=F32)


def dot_tn(a, b):
    return lax.dot_general(a, b, (((0,), (0,)), ((), ())), preferred_element_type=F32)


def norm_parts(values):
    average = jnp.mean(values, axis=-1, keepdims=True)
    centred = values - average
    spread = jnp.mean(centred * centred, axis=-1, keepdims=True)
    scale = lax.rsqrt(spread + EPSILON)
    return centred * scale, scale


def norm_back(hat, scale, dy):
    mean_dy = jnp.mean(dy, axis=-1, keepdims=True)
    mean_dyh = jnp.mean(dy * hat, axis=-1, keepdims=True)
    return scale * (dy - mean_dy - hat * mean_dyh)


def kernel(
    place, x_ref, c_ref, ng_ref, mg_ref, eg_ref, pf_ref, pf3_ref, pc_ref, pc3_ref, pi_ref,
    wqkv_hbm, wproj_hbm, wm_hbm, we_hbm,
    dwork_ref, mine_ref, other_ref,
    wqkv, wproj, wm, we, normed, qkv, probs, attn, fine, fq, cq, mg, dw, gq, gn, dqkv, sems,
):
    lat = place[0]
    lat_size = place[1]
    core = place[2]
    loads = [
        pltpu.make_async_copy(src, dst, sems.at[i])
        for i, (src, dst) in enumerate(
            ((wqkv_hbm, wqkv), (wproj_hbm, wproj), (wm_hbm, wm), (we_hbm, we))
        )
    ]
    for load in loads:
        load.start()

    tq = lax.broadcasted_iota(jnp.int32, (WR, WR), 0)
    tk = lax.broadcasted_iota(jnp.int32, (WR, WR), 1)
    cross = ((tq % COLS) >= WLON) != ((tk % COLS) >= WLON)
    halves = (tq >= WR // 2) != (tk >= WR // 2)
    plain = jnp.where(cross, OUTSIDE, 0.0)
    edged = jnp.where(cross, OUTSIDE, jnp.where(halves, MASKED, 0.0))
    lane = lax.broadcasted_iota(jnp.int32, (1, 2 * HEAD), 1)
    low = (lane < HEAD).astype(F32)
    first_lane = lane < HEAD

    def bias_of(k):
        edge = ((k == 0) & (lat == 0)) | ((k == 4) & (lat == lat_size - 1))
        return jnp.where(edge, edged, plain)

    loads[0].wait()
    loads[1].wait()

    def forward(k, carry):
        start = pl.multiple_of(k * WR, 16)
        span = pl.ds(start, WR)
        bias = bias_of(k)
        x = x_ref[span, :].astype(F32)
        hat, _ = norm_parts(x)
        nrm = (hat * ng_ref[...]).astype(BF)
        normed[span, :] = nrm
        qkv[span, :] = dot(nrm, wqkv[...]).astype(BF)
        for hp in range(HEADS // 2):
            q2 = qkv[span, 128 * hp : 128 * hp + 128]
            k2 = qkv[span, D + 128 * hp : D + 128 * hp + 128]
            v2 = qkv[span, 2 * D + 128 * hp : 2 * D + 128 * hp + 128]
            outs = []
            for half in range(2):
                keep = (low if half == 0 else 1.0 - low) * 0.125
                s = dot_nt(q2 * keep.astype(BF), k2)
                s = jnp.where(bias == 0.0, s, bias)
                e = jnp.exp(s - jnp.max(s, axis=-1, keepdims=True))
                p = e * (1.0 / jnp.sum(e, axis=-1, keepdims=True))
                probs[k, 2 * hp + half] = p
                outs.append(dot(p.astype(BF), v2))
            attn[span, 128 * hp : 128 * hp + 128] = jnp.where(first_lane, outs[0], outs[1]).astype(BF)
        fine[span, :] = (x + dot(attn[span, :], wproj[...])).astype(BF)
        return carry

    lax.fori_loop(0, NWR, forward, 0)

    for g in range(4):
        if g < 3:
            f = dot(pf_ref[...], fine[112 + 192 * g : 112 + 192 * g + 208, :]).astype(BF)
            c = dot(pc_ref[...], c_ref[48 + 192 * g : 48 + 192 * g + 192, :]).astype(BF)
            n = 48
        else:
            f = dot(pf3_ref[...], fine[688:752, :]).astype(BF)
            c = dot(pc3_ref[...], c_ref[624:672, :]).astype(BF)
            n = 16
        for q in range(4):
            fq[q, 48 * g : 48 * g + n, :] = f[n * q : n * q + n]
            cq[q, 48 * g : 48 * g + n, :] = c[n * q : n * q + n]

    def merge_stats(rows):
        total = jnp.zeros((32, 1), F32)
        for q in range(4):
            total = total + jnp.sum(fq[q, rows, :].astype(F32), axis=-1, keepdims=True)
        average = total * (1.0 / (4 * D))
        total = jnp.zeros((32, 1), F32)
        for q in range(4):
            centred = fq[q, rows, :].astype(F32) - average
            total = total + jnp.sum(centred * centred, axis=-1, keepdims=True)
        return average, lax.rsqrt(total * (1.0 / (4 * D)) + EPSILON)

    for r in range(QROWS // 32):
        rows = slice(32 * r, 32 * r + 32)
        average, scale = merge_stats(rows)
        for q in range(4):
            hat = (fq[q, rows, :].astype(F32) - average) * scale
            mg[rows, D * q : D * q + D] = (hat * mg_ref[:, D * q : D * q + D]).astype(BF)

    loads[2].wait()
    loads[3].wait()
    coarse = dot(mg[...], wm[...]).astype(BF)
    for q in range(4):
        qq = (0, 2, 1, 3)[q]
        wide = dot(coarse, we[:, D * qq : D * qq + D])
        hat, scale = norm_parts(wide)
        dy = cq[q].astype(F32) * eg_ref[...]
        dw[:, D * qq : D * qq + D] = norm_back(hat, scale, dy).astype(BF)
    d_coarse = dot_nt(dw[...], we[...]).astype(BF)
    mg[...] = dot_nt(d_coarse, wm[...]).astype(BF)

    for r in range(QROWS // 32):
        rows = slice(32 * r, 32 * r + 32)
        average, scale = merge_stats(rows)
        sum_dy = jnp.zeros((32, 1), F32)
        sum_dyh = jnp.zeros((32, 1), F32)
        for q in range(4):
            hat = (fq[q, rows, :].astype(F32) - average) * scale
            dy = mg[rows, D * q : D * q + D].astype(F32) * mg_ref[:, D * q : D * q + D]
            sum_dy = sum_dy + jnp.sum(dy, axis=-1, keepdims=True)
            sum_dyh = sum_dyh + jnp.sum(dy * hat, axis=-1, keepdims=True)
        mean_dy = sum_dy * (1.0 / (4 * D))
        mean_dyh = sum_dyh * (1.0 / (4 * D))
        for q in range(4):
            hat = (fq[q, rows, :].astype(F32) - average) * scale
            dy = mg[rows, D * q : D * q + D].astype(F32) * mg_ref[:, D * q : D * q + D]
            back = (scale * (dy - mean_dy - hat * mean_dyh)).astype(BF)
            gq[q, rows, :] = (cq[q, rows, :].astype(F32) + back.astype(F32)).astype(BF)

    for k in range(4):
        parts = jnp.concatenate([gq[q, 32 * k : 32 * k + 64, :] for q in range(4)], axis=0)
        gn[WR * k : WR * k + WR, :] = dot(pi_ref[k], parts).astype(BF)

    def backward(k, carry):
        xspan = pl.ds(pl.multiple_of(k * WR, 16), WR)
        gspan = pl.ds(pl.multiple_of((k - 1) * WR, 16), WR)
        bias = bias_of(k)
        g = gn[gspan, :]
        d_attn = dot_nt(g, wproj[...]).astype(BF)
        for hp in range(HEADS // 2):
            q2 = qkv[xspan, 128 * hp : 128 * hp + 128]
            k2 = qkv[xspan, D + 128 * hp : D + 128 * hp + 128]
            v2 = qkv[xspan, 2 * D + 128 * hp : 2 * D + 128 * hp + 128]
            do2 = d_attn[:, 128 * hp : 128 * hp + 128]
            dqs, dks, dvs = [], [], []
            for half in range(2):
                keep = (low if half == 0 else 1.0 - low).astype(BF)
                p = probs[k, 2 * hp + half]
                dp = dot_nt(do2 * keep, v2).astype(BF).astype(F32)
                ds = p * (dp - jnp.sum(dp * p, axis=-1, keepdims=True))
                ds = jnp.where(bias == 0.0, ds, 0.0).astype(BF)
                dqs.append(dot(ds, k2))
                dks.append(dot_tn(ds, q2))
                dvs.append(dot_tn(p.astype(BF), do2))
            for part, two in enumerate((dqs, dks, dvs)):
                both = jnp.where(first_lane, two[0], two[1])
                if part < 2:
                    both = both * 0.125
                dqkv[gspan, D * part + 128 * hp : D * part + 128 * hp + 128] = both.astype(BF)
        d_normed = dot_nt(dqkv[gspan, :], wqkv[...]).astype(BF).astype(F32)
        hat, scale = norm_parts(x_ref[xspan, :].astype(F32))
        back = norm_back(hat, scale, d_normed * ng_ref[...])
        dwork_ref[gspan, :] = (g.astype(F32) + back).astype(BF)
        return carry

    lax.fori_loop(1, 5, backward, 0)

    def put(columns, block):
        pairs = block.astype(BF).reshape(mine_ref.shape[0], 2, mine_ref.shape[1], block.shape[1])
        even, odd = pairs[:, 0], pairs[:, 1]
        mine_ref[:, :, columns] = jnp.where(core == 0, even, odd)
        other_ref[:, :, columns] = jnp.where(core == 0, odd, even)

    inner = slice(WR, 5 * WR)
    for j in range(3):
        put(slice(D * j, D * j + D), dot_tn(normed[inner, :], dqkv[:, D * j : D * j + D]))
    put(slice(3 * D, 4 * D), dot_tn(attn[inner, :], gn[...]))


def compute(tiles, place, x, c, norm_gain, w_qkv, w_proj, merge_gain, w_merge, w_expand, expand_gain):
    vmem = pl.BlockSpec(memory_space=pltpu.VMEM)
    hbm = pl.BlockSpec(memory_space=pl.ANY)
    bf = lambda *shape: pltpu.VMEM(shape, BF)
    return pl.pallas_call(
        kernel,
        out_shape=(
            jax.ShapeDtypeStruct((4 * WR, D), BF),
            jax.ShapeDtypeStruct((tiles, D // (2 * tiles), 4 * D), BF),
            jax.ShapeDtypeStruct((tiles, D // (2 * tiles), 4 * D), BF),
        ),
        in_specs=[pl.BlockSpec(memory_space=pltpu.SMEM)] + [vmem] * 10 + [hbm] * 4,
        out_specs=(vmem, vmem, vmem),
        scratch_shapes=[
            bf(D, 3 * D), bf(D, D), bf(4 * D, 2 * D), bf(2 * D, 4 * D),
            bf(NWR * WR, D), bf(NWR * WR, 3 * D), pltpu.VMEM((NWR, HEADS, WR, WR), F32),
            bf(NWR * WR, D), bf(NWR * WR, D),
            bf(4, QROWS, D), bf(4, QROWS, D), bf(QROWS, 4 * D), bf(QROWS, 4 * D), bf(4, QROWS, D),
            bf(4 * WR, D), bf(4 * WR, 3 * D),
            pltpu.SemaphoreType.DMA((4,)),
        ],
        compiler_params=pltpu.CompilerParams(vmem_limit_bytes=58 * 1024 * 1024),
        name="block",
    )(
        place, x, c, norm_gain[None], merge_gain[None], expand_gain[None],
        jnp.asarray(to_offsets(4, 8, 208, 48)), jnp.asarray(to_offsets(1, 8, 64, 16)),
        jnp.asarray(to_offsets(4, 0, 192, 48)), jnp.asarray(to_offsets(1, 0, 48, 16)),
        jnp.asarray(from_offsets()),
        w_qkv, w_proj, w_merge, w_expand,
    )


def body(tokens, cotangent, norm_gain, w_qkv, w_proj, merge_gain, w_merge, w_expand, expand_gain):
    lats, tiles, cores = lax.axis_size("lat"), lax.axis_size("tile"), lax.axis_size("core")
    lons = tiles * cores
    names = ("lat", "tile", "core")

    def moved(value, dlat, dlon):
        pairs = []
        for a in range(lats):
            for b in range(lons):
                pairs.append((a * lons + b, ((a + dlat) % lats) * lons + (b + dlon) % lons))
        return lax.ppermute(value, names, pairs)

    lat = lax.axis_index("lat")
    core = lax.axis_index("core")
    place = jnp.stack([lat, jnp.int32(lats), core]).astype(jnp.int32)

    edge = moved(jnp.concatenate([tokens[:, :SLON], cotangent[:, :SLON]], axis=0), 0, -1)
    work = jnp.concatenate([tokens[:, SLON:], edge[:ROWS]], axis=1)
    cwork = jnp.concatenate([cotangent[:, SLON:], edge[ROWS:]], axis=1)
    below = moved(jnp.concatenate([work[:9], cwork[:4]], axis=0), -1, 0)
    above = moved(work[ROWS - 3 :], 1, 0)
    x = jnp.concatenate([above, work, below[:9]], axis=0).reshape(XROWS * COLS, D)
    c = jnp.concatenate([cwork, below[9:]], axis=0).reshape(CROWS * COLS, D)

    d_work, mine, other = compute(
        tiles, place, x, c, norm_gain, w_qkv, w_proj, merge_gain, w_merge, w_expand, expand_gain
    )

    theirs = lax.ppermute(other, "core", [(i, cores - 1 - i) for i in range(cores)])
    d_work = d_work.reshape(ROWS, COLS, D)
    arrived = moved(d_work[ROWS - SLAT :], 1, 0)
    d_rows = jnp.concatenate([arrived, d_work[: ROWS - SLAT]], axis=0)
    arrived = moved(d_rows[:, COLS - SLON :], 0, 1)
    d_tokens = jnp.concatenate([arrived, d_rows[:, : COLS - SLON]], axis=1)

    pair = (mine.astype(F32) + theirs.astype(F32)).astype(BF)
    spread = lax.all_to_all(pair, "tile", 0, 0, tiled=True)
    share = jnp.sum(spread.astype(F32), axis=0).astype(BF)
    copies = jnp.broadcast_to(share[None], (lats,) + share.shape)
    gathered = lax.all_to_all(copies, "lat", 0, 0, tiled=True)
    total = jnp.sum(gathered.astype(F32), axis=0)
    return (d_tokens, total[:, : 3 * D], total[:, 3 * D :])


def solution(mesh):
    lats, lons = mesh.shape["lat"], mesh.shape["lon"]
    fine_mesh = Mesh(mesh.devices.reshape(lats, lons // 2, 2), ("lat", "tile", "core"))
    lon = ("tile", "core")
    in_specs = (P("lat", lon, None), P("lat", lon, None), P(), P(), P(), P(), P(), P(), P())
    out_specs = (P("lat", lon, None), P(lon, None), P(lon, None))
    return jax.shard_map(body, mesh=fine_mesh, in_specs=in_specs, out_specs=out_specs, check_vma=False)
```

profile of v0, /device:TPU:0, one launch (start us, length us, event | category | flops | bytes accessed | tf_op | source)
XLA Modules:
  0.0 123.6 jit_solution(15397001054693876088)
XLA Ops:
  0.7 1.0 slice.58
  1.7 0.9 slice.59
  2.7 4.6 %collective-permute-start = (bf16[48,6,512]{2,1,0:T(8,128)(2,1)S(1)}, bf16[48,6,512]{2,1,0:T(8,128)(2,1)S(1)}, u32[]{:S(2)}, u32[]{:S(2)}) collective-permute-start(bf16[48,6,512]{2,1,0:T(8,128)(2,1)S(1)} %pad_maximum_fusion.3), channel_id=1, source_target_pairs={{0,31},{1,0},{2,1},{3,2},{4,3},{5,4},{6,5},{7,6},{8,7},{9,8},{10,9... | collective-permute-start | bytes 884744 | tf_op jit(solution)/shard_map/ppermute | solution.py:298
  7.6 5.0 %collective-permute-done = bf16[48,6,512]{2,1,0:T(8,128)(2,1)S(1)} collective-permute-done((bf16[48,6,512]{2,1,0:T(8,128)(2,1)S(1)}, bf16[48,6,512]{2,1,0:T(8,128)(2,1)S(1)}, u32[]{:S(2)}, u32[]{:S(2)}) %collective-permute-start) | collective-permute-done | bytes 294944 | tf_op jit(solution)/shard_map/ppermute | solution.py:298
  12.7 5.3 %collective-permute-start.2 = (bf16[13,24,512]{2,1,0:T(8,128)(2,1)S(1)}, bf16[13,24,512]{2,1,0:T(8,128)(2,1)S(1)}, u32[]{:S(2)}, u32[]{:S(2)}) collective-permute-start(bf16[13,24,512]{2,1,0:T(8,128)(2,1)S(1)} %fusion.4), channel_id=1, source_target_pairs={{0,224},{1,225},{2,226},{3,227},{4,228},{5,229},{6,230},{7,231},{8... | collective-permute-start | bytes 958472 | tf_op jit(solution)/shard_map/ppermute | solution.py:298
  17.9 0.7 pad_add_fusion.place
  18.6 0.3 collective-permute-start.1
  18.9 3.5 %collective-permute-done.2 = bf16[13,24,512]{2,1,0:T(8,128)(2,1)S(1)} collective-permute-done((bf16[13,24,512]{2,1,0:T(8,128)(2,1)S(1)}, bf16[13,24,512]{2,1,0:T(8,128)(2,1)S(1)}, u32[]{:S(2)}, u32[]{:S(2)}) %collective-permute-start.2) | collective-permute-done | bytes 319520 | tf_op jit(solution)/shard_map/ppermute | solution.py:298
  22.5 1.0 pad_maximum_fusion.1
  23.4 3.4 %collective-permute-done.1 = bf16[3,24,512]{2,1,0:T(8,128)(2,1)S(1)} collective-permute-done((bf16[3,24,512]{2,1,0:T(8,128)(2,1)S(1)}, bf16[3,24,512]{2,1,0:T(8,128)(2,1)S(1)}, u32[]{:S(2)}, u32[]{:S(2)}) %collective-permute-start.1) | collective-permute-done | bytes 73760 | tf_op jit(solution)/shard_map/ppermute | solution.py:298
  26.9 1.0 pad_maximum_fusion
  27.9 36.8 %block.1 = (bf16[576,512]{1,0:T(8,128)(2,1)}, bf16[16,16,2048]{2,1,0:T(8,128)(2,1)}, bf16[16,16,2048]{2,1,0:T(8,128)(2,1)}) custom-call(s32[3]{0:T(128)} %pad_add_fusion.place, bf16[864,512]{1,0:T(8,128)(2,1)} %bitcast.11, bf16[672,512]{1,0:T(8,128)(2,1)} %bitcast.12, f32[1,512]{1,0:T(1,128)} %bitcast.15, f32[1,2048]{1,0:T(1,128)} %bitcast.14, ...), custom_call_target="tpu_custom_call" | custom-call | tf_op jit(solution)/shard_map/block/pallas_call | solution.py:260
  64.8 2.9 %collective-permute-done.5 = bf16[16,16,2048]{2,1,0:T(8,128)(2,1)S(1)} collective-permute-done((bf16[16,16,2048]{2,1,0:T(8,128)(2,1)}, bf16[16,16,2048]{2,1,0:T(8,128)(2,1)S(1)}, u32[]{:S(2)}, u32[]{:S(2)}) %collective-permute-start.5) | collective-permute-done | bytes 1048608 | tf_op jit(solution)/shard_map/ppermute | solution.py:316
  67.7 2.6 %add_convert_fusion = bf16[16,16,2048]{2,1,0:T(8,128)(2,1)} fusion(bf16[16,16,2048]{2,1,0:T(8,128)(2,1)S(1)} %collective-permute-done.5, bf16[16,16,2048]{2,1,0:T(8,128)(2,1)} %get-tuple-element.7), kind=kLoop, calls=%fused_computation | loop fusion | flops 2097152 | bytes 3145728 | tf_op jit(solution)/shard_map/convert_element_type | solution.py:323
  70.3 4.9 %all-to-all-start = ((bf16[16,16,2048]{2,1,0:T(8,128)(2,1)}), bf16[16,16,2048]{2,1,0:T(8,128)(2,1)S(1)}, u32[]{:S(2)}, u32[]{:S(2)}) async-start(bf16[16,16,2048]{2,1,0:T(8,128)(2,1)} %add_convert_fusion), calls=%async_computation | async-start | bytes 2097152 | tf_op jit(solution)/shard_map/all_to_all | solution.py:324
  75.3 2.8 %collective-permute-start.3 = (bf16[3,24,512]{2,1,0:T(8,128)(2,1)S(1)}, bf16[3,24,512]{2,1,0:T(8,128)(2,1)S(1)}, u32[]{:S(2)}, u32[]{:S(2)}) collective-permute-start(bf16[3,24,512]{2,1,0:T(8,128)(2,1)S(1)} %bitcast.13), channel_id=1, source_target_pairs={{0,32},{1,33},{2,34},{3,35},{4,36},{5,37},{6,38},{7,39},{8,40},{9,... | collective-permute-start | bytes 221192 | tf_op jit(solution)/shard_map/ppermute | solution.py:298
  78.1 24.6 %all-to-all-done = bf16[16,16,2048]{2,1,0:T(8,128)(2,1)S(1)} async-done(((bf16[16,16,2048]{2,1,0:T(8,128)(2,1)}), bf16[16,16,2048]{2,1,0:T(8,128)(2,1)S(1)}, u32[]{:S(2)}, u32[]{:S(2)}) %all-to-all-start) | async-done | bytes 1048608 | tf_op jit(solution)/shard_map/all_to_all | solution.py:324
  102.8 0.8 broadcast_in_dim.18
  103.7 6.3 %all-to-all-start.1 = ((bf16[8,16,2048]{2,1,0:T(8,128)(2,1)}), bf16[8,16,2048]{2,1,0:T(8,128)(2,1)S(1)}, u32[]{:S(2)}, u32[]{:S(2)}) async-start(bf16[8,16,2048]{2,1,0:T(8,128)(2,1)} %broadcast_in_dim.18), calls=%async_computation.1 | async-start | bytes 1048576 | tf_op jit(solution)/shard_map/all_to_all | solution.py:327
  110.1 7.2 %collective-permute-done.4 = bf16[24,6,512]{2,1,0:T(8,128)(2,1)S(1)} collective-permute-done((bf16[24,6,512]{2,1,0:T(8,128)(2,1)S(1)}, bf16[24,6,512]{2,1,0:T(8,128)(2,1)S(1)}, u32[]{:S(2)}, u32[]{:S(2)}) %collective-permute-start.4) | collective-permute-done | bytes 147488 | tf_op jit(solution)/shard_map/ppermute | solution.py:298
  117.3 1.0 fusion.2
  118.3 3.9 %all-to-all-done.1 = bf16[8,16,2048]{2,1,0:T(8,128)(2,1)S(1)} async-done(((bf16[8,16,2048]{2,1,0:T(8,128)(2,1)}), bf16[8,16,2048]{2,1,0:T(8,128)(2,1)S(1)}, u32[]{:S(2)}, u32[]{:S(2)}) %all-to-all-start.1) | async-done | bytes 524320 | tf_op jit(solution)/shard_map/all_to_all | solution.py:327
  122.3 0.6 slice.81
  122.9 0.6 slice.80
  (22 shorter events, 1.0 us)
Async XLA Ops:
  0.6 6.7 %copy-start = (bf16[24,24,512]{2,1,0:T(8,128)(2,1)S(1)}, bf16[24,24,512]{2,1,0:T(8,128)(2,1)}, u32[]{:S(2)}) copy-start(bf16[24,24,512]{2,1,0:T(8,128)(2,1)} %param.14) | copy-start | bytes 1769476
  0.6 6.8 %copy-start.1 = (bf16[24,24,512]{2,1,0:T(8,128)(2,1)S(1)}, bf16[24,24,512]{2,1,0:T(8,128)(2,1)}, u32[]{:S(2)}) copy-start(bf16[24,24,512]{2,1,0:T(8,128)(2,1)} %param.15) | copy-start | bytes 1769476
  2.7 9.9 %collective-permute-start = (bf16[48,6,512]{2,1,0:T(8,128)(2,1)S(1)}, bf16[48,6,512]{2,1,0:T(8,128)(2,1)S(1)}, u32[]{:S(2)}, u32[]{:S(2)}) collective-permute-start(bf16[48,6,512]{2,1,0:T(8,128)(2,1)S(1)} %pad_maximum_fusion.3), channel_id=1, source_target_pairs={{0,31},{1,0},{2,1},{3,2},{4,3},{5,4},{6,5},{7,6},{8,7},{9,8},{10,9... | collective-permute-start | bytes 884744 | tf_op jit(solution)/shard_map/ppermute | solution.py:298
  12.7 9.8 %collective-permute-start.2 = (bf16[13,24,512]{2,1,0:T(8,128)(2,1)S(1)}, bf16[13,24,512]{2,1,0:T(8,128)(2,1)S(1)}, u32[]{:S(2)}, u32[]{:S(2)}) collective-permute-start(bf16[13,24,512]{2,1,0:T(8,128)(2,1)S(1)} %fusion.4), channel_id=1, source_target_pairs={{0,224},{1,225},{2,226},{3,227},{4,228},{5,229},{6,230},{7,231},{8... | collective-permute-start | bytes 958472 | tf_op jit(solution)/shard_map/ppermute | solution.py:298
  18.6 8.2 %collective-permute-start.1 = (bf16[3,24,512]{2,1,0:T(8,128)(2,1)S(1)}, bf16[3,24,512]{2,1,0:T(8,128)(2,1)S(1)}, u32[]{:S(2)}, u32[]{:S(2)}) collective-permute-start(bf16[3,24,512]{2,1,0:T(8,128)(2,1)S(1)} %pad_maximum_fusion.6), channel_id=1, source_target_pairs={{0,32},{1,33},{2,34},{3,35},{4,36},{5,37},{6,38},{7,39},{8,40},{9,... | collective-permute-start | bytes 221192 | tf_op jit(solution)/shard_map/ppermute | solution.py:298
  64.7 3.0 %collective-permute-start.5 = (bf16[16,16,2048]{2,1,0:T(8,128)(2,1)}, bf16[16,16,2048]{2,1,0:T(8,128)(2,1)S(1)}, u32[]{:S(2)}, u32[]{:S(2)}) collective-permute-start(bf16[16,16,2048]{2,1,0:T(8,128)(2,1)} %get-tuple-element.8), channel_id=1, source_target_pairs={{0,1},{1,0},{2,3},{3,2},{4,5},{5,4},{6,7},{7,6},{8,9},{9,8},{10,11... | collective-permute-start | bytes 3145736 | tf_op jit(solution)/shard_map/ppermute | solution.py:316
  70.3 4.9 %copy-start.2 = (bf16[576,512]{1,0:T(8,128)(2,1)S(1)}, bf16[576,512]{1,0:T(8,128)(2,1)}, u32[]{:S(2)}) copy-start(bf16[576,512]{1,0:T(8,128)(2,1)} %get-tuple-element.6) | copy-start | bytes 1769476
  70.3 32.4 %all-to-all-start = ((bf16[16,16,2048]{2,1,0:T(8,128)(2,1)}), bf16[16,16,2048]{2,1,0:T(8,128)(2,1)S(1)}, u32[]{:S(2)}, u32[]{:S(2)}) async-start(bf16[16,16,2048]{2,1,0:T(8,128)(2,1)} %add_convert_fusion), calls=%async_computation | async-start | bytes 2097152 | tf_op jit(solution)/shard_map/all_to_all | solution.py:324
  75.3 34.7 %collective-permute-start.3 = (bf16[3,24,512]{2,1,0:T(8,128)(2,1)S(1)}, bf16[3,24,512]{2,1,0:T(8,128)(2,1)S(1)}, u32[]{:S(2)}, u32[]{:S(2)}) collective-permute-start(bf16[3,24,512]{2,1,0:T(8,128)(2,1)S(1)} %bitcast.13), channel_id=1, source_target_pairs={{0,32},{1,33},{2,34},{3,35},{4,36},{5,37},{6,38},{7,39},{8,40},{9,... | collective-permute-start | bytes 221192 | tf_op jit(solution)/shard_map/ppermute | solution.py:298
  103.7 18.6 %all-to-all-start.1 = ((bf16[8,16,2048]{2,1,0:T(8,128)(2,1)}), bf16[8,16,2048]{2,1,0:T(8,128)(2,1)S(1)}, u32[]{:S(2)}, u32[]{:S(2)}) async-start(bf16[8,16,2048]{2,1,0:T(8,128)(2,1)} %broadcast_in_dim.18), calls=%async_computation.1 | async-start | bytes 1048576 | tf_op jit(solution)/shard_map/all_to_all | solution.py:327
  110.0 7.3 %collective-permute-start.4 = (bf16[24,6,512]{2,1,0:T(8,128)(2,1)S(1)}, bf16[24,6,512]{2,1,0:T(8,128)(2,1)S(1)}, u32[]{:S(2)}, u32[]{:S(2)}) collective-permute-start(bf16[24,6,512]{2,1,0:T(8,128)(2,1)S(1)} %pad_maximum_fusion.5), channel_id=1, source_target_pairs={{0,1},{1,2},{2,3},{3,4},{4,5},{5,6},{6,7},{7,8},{8,9},{9,10},{10,1... | collective-permute-start | bytes 442376 | tf_op jit(solution)/shard_map/ppermute | solution.py:298
where the time goes:
time: 124 us
  waiting for transfers between devices  50.5 us (41%)
  Pallas kernels  36.8 us (30%)
  starting transfers between devices  24.3 us (20%)
  other arithmetic  6.74 us (5%)
  local copies, waits for them, and re-layouts  4.51 us (4%)
    pallas_call x1, Pallas kernels, compute(): pl.pallas_call(kernel, out_shape=(jax.ShapeDtypeStruct((4 * WR, D), BF),...  36.8 us
    all_to_all x1, waiting for transfers between devices, body(): spread = lax.all_to_all(pair, 'tile', 0, 0, tiled=True)  24.6 us
    ppermute x5, waiting for transfers between devices, moved(): return lax.ppermute(value, names, pairs)  19.1 us
    ppermute x5, starting transfers between devices, moved(): return lax.ppermute(value, names, pairs)  13 us
    all_to_all x1, starting transfers between devices, body(): gathered = lax.all_to_all(copies, 'lat', 0, 0, tiled=True)  6.27 us
    all_to_all x1, starting transfers between devices, body(): spread = lax.all_to_all(pair, 'tile', 0, 0, tiled=True)  4.93 us
    all_to_all x1, waiting for transfers between devices, body(): gathered = lax.all_to_all(copies, 'lat', 0, 0, tiled=True)  3.89 us
    ppermute x1, waiting for transfers between devices, body(): lax.ppermute(other, 'core', [(i, cores - 1 - i) for i in range(cores)])  2.86 us
  transfers between devices with their start and end apart: 8, of which 7 were waited for; matrix products, arithmetic and copies ran while one was open for 3% of the time, Pallas kernels for 0%

commit v1 on v0

v1 whole, which is shorter than its diff:
```python
import functools

import jax
import jax.numpy as jnp
import numpy as np
from jax import lax
from jax.experimental import pallas as pl
from jax.experimental.pallas import tpu as pltpu
from jax.sharding import Mesh, PartitionSpec as P

HEADS = 8
HEAD = 64
WLAT = 6
WLON = 12
SLAT = 3
SLON = 6
D = 512
ROWS = 24
COLS = 24
WR = WLAT * COLS
WIN = WLAT * WLON
WP = 80
WRP = 2 * WP
NWR = 6
XROWS = WLAT * NWR
CROWS = 28
PAIRS = 13
QROWS = 160

EPSILON = 1e-05
MASKED = -1000000000.0
OUTSIDE = -3.0e38
BF = jnp.bfloat16
F32 = jnp.float32


def window_row(i, col):
    return (col // WLON) * WP + i * WLON + col % WLON


def to_windows():
    out = np.zeros((WRP, WR), np.float32)
    for t in range(WR):
        out[window_row(t // COLS, t % COLS), t] = 1
    return out.astype(jnp.bfloat16)


def cot_offsets(pairs, padded):
    out = np.zeros((4 * padded, pairs * 2 * COLS), np.float32)
    for a in range(pairs):
        for rp in range(2):
            for col in range(COLS):
                q = (col % 2) * 2 + rp
                out[q * padded + a * 12 + col // 2, (2 * a + rp) * COLS + col] = 1
    return out.astype(jnp.bfloat16)


FINE_PARTS = ((0, 0), (0, 1), (0, 2), (1, 2), (1, 3), (2, 3), (2, 4), (3, 4), (3, 5))


def fine_offsets():
    out = np.zeros((len(FINE_PARTS), 4 * 48, WRP), np.float32)
    for n, (g, k) in enumerate(FINE_PARTS):
        padded = 48 if g < 3 else 16
        for a in range(4 * g, min(4 * g + 4, PAIRS)):
            for rp in range(2):
                f = 5 + 2 * a + rp
                if f // WLAT != k:
                    continue
                for col in range(COLS):
                    q = (col % 2) * 2 + rp
                    out[n, q * padded + (a - 4 * g) * 12 + col // 2, window_row(f % WLAT, col)] = 1
    return out.astype(jnp.bfloat16)


def from_offsets():
    out = np.zeros((4, WRP, 256), np.float32)
    for k in range(1, 5):
        for t in range(WR):
            f = WLAT * k + t // COLS
            col = t % COLS
            a, rp = divmod(f - 5, 2)
            q = (col % 2) * 2 + rp
            out[k - 1, window_row(t // COLS, col), q * 64 + 12 * a + col // 2 - 32 * (k - 1)] = 1
    return out.astype(jnp.bfloat16)


def dot(a, b):
    return jnp.dot(a, b, preferred_element_type=F32)


def dot_nt(a, b):
    return lax.dot_general(a, b, (((1,), (1,)), ((), ())), preferred_element_type=F32)


def dot_tn(a, b):
    return lax.dot_general(a, b, (((0,), (0,)), ((), ())), preferred_element_type=F32)


def norm_parts(values):
    average = jnp.mean(values, axis=-1, keepdims=True)
    centred = values - average
    spread = jnp.mean(centred * centred, axis=-1, keepdims=True)
    scale = lax.rsqrt(spread + EPSILON)
    return centred * scale, scale


def norm_back(hat, scale, dy):
    mean_dy = jnp.mean(dy, axis=-1, keepdims=True)
    mean_dyh = jnp.mean(dy * hat, axis=-1, keepdims=True)
    return scale * (dy - mean_dy - hat * mean_dyh)


def stacked(two, low):
    gap = jnp.zeros((128 - WP, 2 * HEAD), BF)
    return jnp.concatenate([two * low, gap, two * (1 - low), gap], axis=0)


def over_queries(keys_by_queries, rows, first_lane):
    both = [dot_tn(keys_by_queries[:, 128 * i : 128 * i + WP], rows) for i in range(2)]
    return jnp.where(first_lane, both[0], both[1])


def padded_keys(values):
    return jnp.concatenate([values, jnp.zeros((WP - WIN, 256), F32)], axis=0).astype(BF)


UNITS = [(w, hp) for w in range(2) for hp in range(HEADS // 2)]
GROUP = 8


def kernel(
    lat_size, x_ref, c_ref, ng_ref, mg_ref, eg_ref, px_ref, pxt_ref, pf_ref, pc_ref, pc3_ref, pi_ref,
    wqkv_hbm, wproj_hbm, wm_hbm, we_hbm,
    mine_hbm, other_hbm, gn_hbm, dqkv_hbm,
    wqkv, wproj, wm, we, xw, normed, qkv, probs, attn, fine, fq, cq, mg, dw, gq, gn, d_attn, dqkv, mine, other, sems,
):
    lat = lax.axis_index("lat")
    core = lax.axis_index("core")
    loads = [
        pltpu.make_async_copy(src, dst, sems.at[i])
        for i, (src, dst) in enumerate(
            ((wqkv_hbm, wqkv), (wproj_hbm, wproj), (wm_hbm, wm), (we_hbm, we))
        )
    ]
    for load in loads:
        load.start()

    key = lax.broadcasted_iota(jnp.int32, (WIN, 256), 0)
    query = lax.broadcasted_iota(jnp.int32, (WIN, 256), 1) % 128
    apart = (key >= WIN // 2) != (query >= WIN // 2)
    lane = lax.broadcasted_iota(jnp.int32, (1, 2 * HEAD), 1)
    first_lane = lane < HEAD
    low = first_lane.astype(F32).astype(BF)

    def masked_at(k):
        edge = ((k == 0) & (lat == 0)) | ((k == 4) & (lat == lat_size - 1))
        return apart & edge

    loads[0].wait()
    loads[1].wait()

    def prepare(k, carry):
        span = pl.ds(pl.multiple_of(k * WRP, 16), WRP)
        x = dot(px_ref[...], x_ref[pl.ds(pl.multiple_of(k * WR, 16), WR), :])
        xw[span, :] = x.astype(BF)
        hat, _ = norm_parts(x)
        normed[span, :] = (hat * ng_ref[...]).astype(BF)
        return carry

    lax.fori_loop(0, NWR, prepare, 0, unroll=3)
    for j in range(6):
        columns = slice(256 * j, 256 * j + 256)
        qkv[:, columns] = dot(normed[...], wqkv[:, columns]).astype(BF)

    def heads(base, w, hp):
        win = pl.ds(pl.multiple_of(base + WP * w, 16), WP)
        q2 = qkv[win, 128 * hp : 128 * hp + 128]
        k2 = qkv[win, D + 128 * hp : D + 128 * hp + 128]
        v2 = qkv[win, 2 * D + 128 * hp : 2 * D + 128 * hp + 128]
        return stacked(q2 * 0.125, low), k2, v2, win

    def forward(k, carry):
        start = pl.multiple_of(k * WRP, 16)
        masked = masked_at(k)
        for first in range(0, len(UNITS), GROUP):
            group = UNITS[first : first + GROUP]
            parts = [heads(start, w, hp) for w, hp in group]
            s = [dot_nt(k2, qs)[:WIN] for qs, k2, _, _ in parts]
            s = [jnp.where(masked, MASKED, v) for v in s]
            top = [jnp.max(v, axis=0, keepdims=True) for v in s]
            e = [jnp.exp(v - t) for v, t in zip(s, top)]
            total = [jnp.sum(v, axis=0, keepdims=True) for v in e]
            p = [v * (1.0 / t) for v, t in zip(e, total)]
            for (w, hp), v in zip(group, p):
                probs[k, 4 * w + hp] = v
            o = [over_queries(padded_keys(v), v2, first_lane) for v, (_, _, v2, _) in zip(p, parts)]
            for (w, hp), v, (_, _, _, win) in zip(group, o, parts):
                attn[win, 128 * hp : 128 * hp + 128] = v.astype(BF)
        return carry

    lax.fori_loop(0, NWR, forward, 0)
    for j in range(2):
        columns = slice(256 * j, 256 * j + 256)
        fine[:, columns] = (
            xw[:, columns].astype(F32) + dot(attn[...], wproj[:, columns])
        ).astype(BF)

    for g in range(4):
        n = 48 if g < 3 else 16
        f = sum(
            dot(pf_ref[m, : 4 * n, :], fine[WRP * k : WRP * k + WRP, :])
            for m, (gg, k) in enumerate(FINE_PARTS)
            if gg == g
        ).astype(BF)
        if g < 3:
            c = dot(pc_ref[...], c_ref[48 + 192 * g : 48 + 192 * g + 192, :]).astype(BF)
        else:
            c = dot(pc3_ref[...], c_ref[624:672, :]).astype(BF)
        for q in range(4):
            fq[q, 48 * g : 48 * g + n, :] = f[n * q : n * q + n]
            cq[q, 48 * g : 48 * g + n, :] = c[n * q : n * q + n]

    def merge_stats(rows):
        total = jnp.zeros((32, 1), F32)
        for q in range(4):
            total = total + jnp.sum(fq[q, rows, :].astype(F32), axis=-1, keepdims=True)
        average = total * (1.0 / (4 * D))
        total = jnp.zeros((32, 1), F32)
        for q in range(4):
            centred = fq[q, rows, :].astype(F32) - average
            total = total + jnp.sum(centred * centred, axis=-1, keepdims=True)
        return average, lax.rsqrt(total * (1.0 / (4 * D)) + EPSILON)

    for r in range(QROWS // 32):
        rows = slice(32 * r, 32 * r + 32)
        average, scale = merge_stats(rows)
        for q in range(4):
            hat = (fq[q, rows, :].astype(F32) - average) * scale
            mg[rows, D * q : D * q + D] = (hat * mg_ref[:, D * q : D * q + D]).astype(BF)

    loads[2].wait()
    loads[3].wait()
    coarse = dot(mg[...], wm[...]).astype(BF)
    for q in range(4):
        qq = (0, 2, 1, 3)[q]
        wide = dot(coarse, we[:, D * qq : D * qq + D])
        hat, scale = norm_parts(wide)
        dy = cq[q].astype(F32) * eg_ref[...]
        dw[:, D * qq : D * qq + D] = norm_back(hat, scale, dy).astype(BF)
    d_coarse = dot_nt(dw[...], we[...]).astype(BF)
    mg[...] = dot_nt(d_coarse, wm[...]).astype(BF)

    for r in range(QROWS // 32):
        rows = slice(32 * r, 32 * r + 32)
        average, scale = merge_stats(rows)
        sum_dy = jnp.zeros((32, 1), F32)
        sum_dyh = jnp.zeros((32, 1), F32)
        for q in range(4):
            hat = (fq[q, rows, :].astype(F32) - average) * scale
            dy = mg[rows, D * q : D * q + D].astype(F32) * mg_ref[:, D * q : D * q + D]
            sum_dy = sum_dy + jnp.sum(dy, axis=-1, keepdims=True)
            sum_dyh = sum_dyh + jnp.sum(dy * hat, axis=-1, keepdims=True)
        mean_dy = sum_dy * (1.0 / (4 * D))
        mean_dyh = sum_dyh * (1.0 / (4 * D))
        for q in range(4):
            hat = (fq[q, rows, :].astype(F32) - average) * scale
            dy = mg[rows, D * q : D * q + D].astype(F32) * mg_ref[:, D * q : D * q + D]
            back = (scale * (dy - mean_dy - hat * mean_dyh)).astype(BF)
            gq[q, rows, :] = (cq[q, rows, :].astype(F32) + back.astype(F32)).astype(BF)

    for k in range(4):
        parts = jnp.concatenate([gq[q, 32 * k : 32 * k + 64, :] for q in range(4)], axis=0)
        gn[WRP * k : WRP * k + WRP, :] = dot(pi_ref[k], parts).astype(BF)

    stores = []

    def store(src, dst):
        copy = pltpu.make_async_copy(src, dst, sems.at[4 + len(stores)])
        copy.start()
        stores.append(copy)

    def put(j, block):
        columns = slice(D * j, D * j + D)
        pairs = block.astype(BF).reshape(mine.shape[0], 2, mine.shape[1], D)
        even, odd = pairs[:, 0], pairs[:, 1]
        mine[:, :, columns] = jnp.where(core == 0, even, odd)
        other[:, :, columns] = jnp.where(core == 0, odd, even)
        store(other.at[:, :, columns], other_hbm.at[:, :, columns])
        store(mine.at[:, :, columns], mine_hbm.at[:, :, columns])

    inner = slice(WRP, 5 * WRP)
    store(gn, gn_hbm)
    put(3, dot_tn(attn[inner, :], gn[...]))

    for j in range(2):
        columns = slice(256 * j, 256 * j + 256)
        d_attn[:, columns] = dot_nt(gn[...], wproj[columns, :]).astype(BF)

    def backward(k, carry):
        start = pl.multiple_of(k * WRP, 16)
        gstart = pl.multiple_of((k - 1) * WRP, 16)
        masked = masked_at(k)
        for first in range(0, len(UNITS), GROUP):
            group = UNITS[first : first + GROUP]
            parts = [heads(start, w, hp) for w, hp in group]
            gwins = [pl.ds(pl.multiple_of(gstart + WP * w, 16), WP) for w, _ in group]
            do = [
                stacked(d_attn[gwin, 128 * hp : 128 * hp + 128], low)
                for gwin, (_, hp) in zip(gwins, group)
            ]
            dp = [dot_nt(v2, d)[:WIN] for d, (_, _, v2, _) in zip(do, parts)]
            p = [probs[k, 4 * w + hp] for w, hp in group]
            dv = [dot(padded_keys(v), d) for v, d in zip(p, do)]
            dp = [v.astype(BF).astype(F32) for v in dp]
            inner = [jnp.sum(a * b, axis=0, keepdims=True) for a, b in zip(dp, p)]
            ds = [b * (a - c) for a, b, c in zip(dp, p, inner)]
            ds = [padded_keys(jnp.where(masked, 0.0, v)) for v in ds]
            dk = [dot(v, qs) for v, (qs, _, _, _) in zip(ds, parts)]
            dq = [over_queries(v, k2, first_lane) * 0.125 for v, (_, k2, _, _) in zip(ds, parts)]
            for i, (gwin, (w, hp)) in enumerate(zip(gwins, group)):
                lanes = slice(128 * hp, 128 * hp + 128)
                dqkv[gwin, lanes] = dq[i].astype(BF)
                dqkv[gwin, D + lanes.start : D + lanes.stop] = dk[i].astype(BF)
                dqkv[gwin, 2 * D + lanes.start : 2 * D + lanes.stop] = dv[i].astype(BF)
        return carry

    lax.fori_loop(1, 5, backward, 0)
    store(dqkv, dqkv_hbm)
    for j in range(3):
        put(j, dot_tn(normed[inner, :], dqkv[:, D * j : D * j + D]))
    for copy in stores:
        copy.wait()


def finish_kernel(x_ref, gn_ref, dqkv_ref, wqkv_ref, ng_ref, px_ref, pxt_ref, dwork_ref, d_normed):
    for j in range(2):
        columns = slice(256 * j, 256 * j + 256)
        d_normed[:, columns] = dot_nt(dqkv_ref[...], wqkv_ref[columns, :]).astype(BF)

    def finish(k, carry):
        span = pl.ds(pl.multiple_of((k + 1) * WR, 16), WR)
        gspan = pl.ds(pl.multiple_of(k * WRP, 16), WRP)
        hat, scale = norm_parts(dot(px_ref[...], x_ref[span, :]))
        back = norm_back(hat, scale, d_normed[gspan, :].astype(F32) * ng_ref[...])
        d_work = (gn_ref[gspan, :].astype(F32) + back).astype(BF)
        dwork_ref[pl.ds(pl.multiple_of(k * WR, 16), WR), :] = dot(pxt_ref[...], d_work).astype(BF)
        return carry

    lax.fori_loop(0, 4, finish, 0, unroll=2)


VMEM = pl.BlockSpec(memory_space=pltpu.VMEM)
HBM = pl.BlockSpec(memory_space=pl.ANY)


def compute(tiles, lats, x, c, norm_gain, w_qkv, w_proj, merge_gain, w_merge, w_expand, expand_gain):
    bf = lambda *shape: pltpu.VMEM(shape, BF)
    share = (tiles, D // (2 * tiles), 4 * D)
    return pl.pallas_call(
        functools.partial(kernel, lats),
        out_shape=tuple(
            jax.ShapeDtypeStruct(shape, BF) for shape in (share, share, (4 * WRP, D), (4 * WRP, 3 * D))
        ),
        in_specs=[VMEM] * 11 + [HBM] * 4,
        out_specs=(HBM,) * 4,
        scratch_shapes=[
            bf(D, 3 * D), bf(D, D), bf(4 * D, 2 * D), bf(2 * D, 4 * D),
            bf(NWR * WRP, D), bf(NWR * WRP, D), bf(NWR * WRP, 3 * D), pltpu.VMEM((NWR, HEADS, WIN, 256), F32),
            bf(NWR * WRP, D), bf(NWR * WRP, D),
            bf(4, QROWS, D), bf(4, QROWS, D), bf(QROWS, 4 * D), bf(QROWS, 4 * D), bf(4, QROWS, D),
            bf(4 * WRP, D), bf(4 * WRP, D), bf(4 * WRP, 3 * D), bf(*share), bf(*share),
            pltpu.SemaphoreType.DMA((14,)),
        ],
        compiler_params=pltpu.CompilerParams(vmem_limit_bytes=58 * 1024 * 1024),
        cost_estimate=pl.CostEstimate(flops=7_000_000_000, bytes_accessed=18_000_000, transcendentals=0),
        name="block",
    )(
        x, c, norm_gain[None], merge_gain[None], expand_gain[None],
        jnp.asarray(to_windows()), jnp.asarray(to_windows().T), jnp.asarray(fine_offsets()),
        jnp.asarray(cot_offsets(4, 48)), jnp.asarray(cot_offsets(1, 16)), jnp.asarray(from_offsets()),
        w_qkv, w_proj, w_merge, w_expand,
    )


def finish_tokens(x, gn, dqkv, w_qkv, norm_gain):
    return pl.pallas_call(
        finish_kernel,
        out_shape=jax.ShapeDtypeStruct((4 * WR, D), BF),
        in_specs=[VMEM] * 7,
        out_specs=VMEM,
        scratch_shapes=[pltpu.VMEM((4 * WRP, D), BF)],
        compiler_params=pltpu.CompilerParams(vmem_limit_bytes=40 * 1024 * 1024),
        cost_estimate=pl.CostEstimate(flops=1_200_000_000, bytes_accessed=6_000_000, transcendentals=0),
        name="block_tokens",
    )(x, gn, dqkv, w_qkv, norm_gain[None], jnp.asarray(to_windows()), jnp.asarray(to_windows().T))


def body(tokens, cotangent, norm_gain, w_qkv, w_proj, merge_gain, w_merge, w_expand, expand_gain):
    lats, tiles, cores = lax.axis_size("lat"), lax.axis_size("tile"), lax.axis_size("core")
    lons = tiles * cores
    names = ("lat", "tile", "core")

    def moved(value, dlat, dlon):
        pairs = []
        for a in range(lats):
            for b in range(lons):
                pairs.append((a * lons + b, ((a + dlat) % lats) * lons + (b + dlon) % lons))
        return lax.ppermute(value, names, pairs)

    edge = moved(jnp.concatenate([tokens[:, :SLON], cotangent[:, :SLON]], axis=0), 0, -1)
    work = jnp.concatenate([tokens[:, SLON:], edge[:ROWS]], axis=1)
    cwork = jnp.concatenate([cotangent[:, SLON:], edge[ROWS:]], axis=1)
    below = moved(jnp.concatenate([work[:9], cwork[:4]], axis=0), -1, 0)
    above = moved(work[ROWS - 3 :], 1, 0)
    x = jnp.concatenate([above, work, below[:9]], axis=0).reshape(XROWS * COLS, D)
    c = jnp.concatenate([cwork, below[9:]], axis=0).reshape(CROWS * COLS, D)

    mine, other, gn, dqkv = compute(
        tiles, lats, x, c, norm_gain, w_qkv, w_proj, merge_gain, w_merge, w_expand, expand_gain
    )

    theirs = lax.ppermute(other, "core", [(i, cores - 1 - i) for i in range(cores)])
    pair, dqkv = lax.optimization_barrier((mine + theirs, dqkv))
    spread = lax.all_to_all(pair, "tile", 0, 0, tiled=True)

    d_work = finish_tokens(x, gn, dqkv, w_qkv, norm_gain).reshape(ROWS, COLS, D)
    arrived = moved(d_work[ROWS - SLAT :], 1, 0)
    d_rows = jnp.concatenate([arrived, d_work[: ROWS - SLAT]], axis=0)
    arrived = moved(d_rows[:, COLS - SLON :], 0, 1)
    d_tokens = jnp.concatenate([arrived, d_rows[:, : COLS - SLON]], axis=1)
    spread, d_tokens = lax.optimization_barrier((spread, d_tokens))

    share = jnp.sum(spread.astype(F32), axis=0).astype(BF)
    copies = jnp.broadcast_to(share[None], (lats,) + share.shape)
    gathered = lax.all_to_all(copies, "lat", 0, 0, tiled=True)
    grad_qkv = jnp.sum(gathered[:, :, : 3 * D].astype(F32), axis=0)
    grad_proj = jnp.sum(gathered[:, :, 3 * D :].astype(F32), axis=0)
    return (d_tokens, grad_qkv, grad_proj)


def solution(mesh):
    lats, lons = mesh.shape["lat"], mesh.shape["lon"]
    fine_mesh = Mesh(mesh.devices.reshape(lats, lons // 2, 2), ("lat", "tile", "core"))
    lon = ("tile", "core")
    in_specs = (P("lat", lon, None), P("lat", lon, None), P(), P(), P(), P(), P(), P(), P())
    out_specs = (P("lat", lon, None), P(lon, None), P(lon, None))
    return jax.shard_map(body, mesh=fine_mesh, in_specs=in_specs, out_specs=out_specs, check_vma=False)
```

time: 124 us -> 112 us (0.903)
  blocking collectives: 0 us -> 16.3 us
  waiting for transfers between devices: 50.5 us -> 34.3 us
  Pallas kernels: 36.8 us -> 27.2 us
  starting transfers between devices: 24.3 us -> 18.7 us
  other arithmetic: 6.74 us -> 8.68 us
    all_to_all x1, waiting for transfers between devices: 24.6 us -> 0.01 us  [body(): spread = lax.all_to_all(pair, 'tile', 0, 0, tiled=True)]
    all_to_all x0 -> x1, blocking collectives: none -> 16.3 us  [body(): gathered = lax.all_to_all(copies, 'lat', 0, 0, tiled=True)]
    ppermute x5, waiting for transfers between devices: 19.1 us -> 31.4 us  [moved(): return lax.ppermute(value, names, pairs)]
    pallas_call x1 -> x2, Pallas kernels: 36.8 us -> 27.2 us  [the longest x1 23.8 us: compute(): pl.pallas_call(functools.partial(kernel, lats), out_shape=tuple((jax.Shap...]
    all_to_all x1 -> x0, starting transfers between devices: 6.27 us -> none  [body(): gathered = lax.all_to_all(copies, 'lat', 0, 0, tiled=True)]
    all_to_all x1 -> x0, waiting for transfers between devices: 3.89 us -> none  [body(): gathered = lax.all_to_all(copies, 'lat', 0, 0, tiled=True)]
    unnamed x6 -> x18, local copies, waits for them, and re-layouts: 0.01 us -> 3.2 us
    add x0 -> x1, other arithmetic: none -> 2.73 us  [body(): pair, dqkv = lax.optimization_barrier((mine + theirs, dqkv))]
  transfers between devices with their start and end apart: 8 -> 7, of which waited for: 7 -> 6; matrix products, arithmetic and copies ran while one was open for 3% -> 2% of each run, Pallas kernels for 0% -> 3%
where the time goes in v1:
time: 112 us
  waiting for transfers between devices  34.3 us (31%)
  Pallas kernels  27.2 us (24%)
  starting transfers between devices  18.7 us (17%)
  blocking collectives  16.3 us (15%)
  other arithmetic  8.68 us (8%)
  local copies, waits for them, and re-layouts  5.63 us (5%)
    ppermute x5, waiting for transfers between devices, moved(): return lax.ppermute(value, names, pairs)  31.4 us
    pallas_call x1, Pallas kernels, compute(): pl.pallas_call(functools.partial(kernel, lats), out_shape=tuple((jax.Shap...  23.8 us
    all_to_all x1, blocking collectives, body(): gathered = lax.all_to_all(copies, 'lat', 0, 0, tiled=True)  16.3 us
    ppermute x5, starting transfers between devices, moved(): return lax.ppermute(value, names, pairs)  13 us
    all_to_all x1, starting transfers between devices, body(): spread = lax.all_to_all(pair, 'tile', 0, 0, tiled=True)  5.67 us
    pallas_call x1, Pallas kernels, finish_tokens(): pl.pallas_call(finish_kernel, out_shape=jax.ShapeDtypeStruct((4 * WR, D),...  3.42 us
    unnamed x18, local copies, waits for them, and re-layouts  3.2 us
    ppermute x1, waiting for transfers between devices, body(): lax.ppermute(other, 'core', [(i, cores - 1 - i) for i in range(cores)])  2.86 us
  transfers between devices with their start and end apart: 7, of which 6 were waited for; matrix products, arithmetic and copies ran while one was open for 2% of the time, Pallas kernels for 3%

profile of v1, /device:TPU:0, one launch (start us, length us, event | category | flops | bytes accessed | tf_op | source)
XLA Modules:
  0.0 111.6 jit_solution(6269456243804433246)
XLA Ops:
  0.7 1.0 slice.58
  1.7 0.9 slice.59
  2.7 4.6 %collective-permute-start = (bf16[48,6,512]{2,1,0:T(8,128)(2,1)S(1)}, bf16[48,6,512]{2,1,0:T(8,128)(2,1)S(1)}, u32[]{:S(2)}, u32[]{:S(2)}) collective-permute-start(bf16[48,6,512]{2,1,0:T(8,128)(2,1)S(1)} %pad_maximum_fusion.3), channel_id=1, source_target_pairs={{0,31},{1,0},{2,1},{3,2},{4,3},{5,4},{6,5},{7,6},{8,7},{9,8},{10,9... | collective-permute-start | bytes 884744 | tf_op jit(solution)/shard_map/ppermute | solution.py:409
  7.6 5.0 %collective-permute-done = bf16[48,6,512]{2,1,0:T(8,128)(2,1)S(1)} collective-permute-done((bf16[48,6,512]{2,1,0:T(8,128)(2,1)S(1)}, bf16[48,6,512]{2,1,0:T(8,128)(2,1)S(1)}, u32[]{:S(2)}, u32[]{:S(2)}) %collective-permute-start) | collective-permute-done | bytes 294944 | tf_op jit(solution)/shard_map/ppermute | solution.py:409
  12.7 5.3 %collective-permute-start.2 = (bf16[13,24,512]{2,1,0:T(8,128)(2,1)S(1)}, bf16[13,24,512]{2,1,0:T(8,128)(2,1)S(1)}, u32[]{:S(2)}, u32[]{:S(2)}) collective-permute-start(bf16[13,24,512]{2,1,0:T(8,128)(2,1)S(1)} %fusion.4), channel_id=1, source_target_pairs={{0,224},{1,225},{2,226},{3,227},{4,228},{5,229},{6,230},{7,231},{8... | collective-permute-start | bytes 958472 | tf_op jit(solution)/shard_map/ppermute | solution.py:409
  18.2 4.2 %collective-permute-done.2 = bf16[13,24,512]{2,1,0:T(8,128)(2,1)S(1)} collective-permute-done((bf16[13,24,512]{2,1,0:T(8,128)(2,1)S(1)}, bf16[13,24,512]{2,1,0:T(8,128)(2,1)S(1)}, u32[]{:S(2)}, u32[]{:S(2)}) %collective-permute-start.2) | collective-permute-done | bytes 319520 | tf_op jit(solution)/shard_map/ppermute | solution.py:409
  22.5 1.0 pad_maximum_fusion.1
  23.5 2.7 %collective-permute-done.1 = bf16[3,24,512]{2,1,0:T(8,128)(2,1)S(1)} collective-permute-done((bf16[3,24,512]{2,1,0:T(8,128)(2,1)S(1)}, bf16[3,24,512]{2,1,0:T(8,128)(2,1)S(1)}, u32[]{:S(2)}, u32[]{:S(2)}) %collective-permute-start.1) | collective-permute-done | bytes 73760 | tf_op jit(solution)/shard_map/ppermute | solution.py:409
  26.2 1.0 pad_maximum_fusion
  27.2 23.8 %block.1 = (bf16[16,16,2048]{2,1,0:T(8,128)(2,1)}, bf16[16,16,2048]{2,1,0:T(8,128)(2,1)}, bf16[640,512]{1,0:T(8,128)(2,1)}, bf16[640,1536]{1,0:T(8,128)(2,1)}) custom-call(bf16[864,512]{1,0:T(8,128)(2,1)} %bitcast.7, bf16[672,512]{1,0:T(8,128)(2,1)} %bitcast.13, f32[1,512]{1,0:T(1,128)} %bitcast.9, f32[1,2048]{1,0:T(1,128)} %bitcast.15, f32[1,512]{1,0:T(1,128)} %bitcast.16, ...), custom_call_target="tpu_custom_call" | custom-call | flops 7000000000 | bytes 18000000 | tf_op jit(solution)/shard_map/block/pallas_call | solution.py:360
  51.1 2.9 %collective-permute-done.3 = bf16[16,16,2048]{2,1,0:T(8,128)(2,1)S(1)} collective-permute-done((bf16[16,16,2048]{2,1,0:T(8,128)(2,1)}, bf16[16,16,2048]{2,1,0:T(8,128)(2,1)S(1)}, u32[]{:S(2)}, u32[]{:S(2)}) %collective-permute-start.3) | collective-permute-done | bytes 1048608 | tf_op jit(solution)/shard_map/ppermute | solution.py:423
  53.9 2.7 %add.3 = bf16[16,16,2048]{2,1,0:T(8,128)(2,1)} add(bf16[16,16,2048]{2,1,0:T(8,128)(2,1)} %get-tuple-element.11, bf16[16,16,2048]{2,1,0:T(8,128)(2,1)S(1)} %collective-permute-done.3) | non-fusion elementwise | flops 524288 | bytes 3145728 | tf_op jit(solution)/shard_map/add | solution.py:424
  56.7 5.7 %all-to-all-start = ((bf16[16,16,2048]{2,1,0:T(8,128)(2,1)}), bf16[16,16,2048]{2,1,0:T(8,128)(2,1)}, u32[]{:S(2)}, u32[]{:S(2)}) async-start(bf16[16,16,2048]{2,1,0:T(8,128)(2,1)} %add.3), calls=%async_computation | async-start | bytes 2097152 | tf_op jit(solution)/shard_map/all_to_all | solution.py:425
  62.4 1.4 %copy-done.2 = bf16[512,1536]{1,0:T(8,128)(2,1)S(1)} copy-done((bf16[512,1536]{1,0:T(8,128)(2,1)S(1)}, bf16[512,1536]{1,0:T(8,128)(2,1)}, u32[]{:S(2)}) %copy-start.2) | copy-done | bytes 1572888
  63.8 0.9 copy-done.4
  64.7 0.9 copy-done.5
  65.6 3.4 %block_tokens.1 = bf16[576,512]{1,0:T(8,128)(2,1)S(1)} custom-call(bf16[864,512]{1,0:T(8,128)(2,1)S(1)} %bitcast.8, bf16[640,512]{1,0:T(8,128)(2,1)S(1)} %copy-done.3, bf16[640,1536]{1,0:T(8,128)(2,1)S(1)} %copy-done.1, bf16[512,1536]{1,0:T(8,128)(2,1)S(1)} %copy-done.2, f32[1,512]{1,0:T(1,128)S(1)} %bitcast.10, bf16[160,144]{1,0:T(8,128)(2,1)S(1)} %copy-done.4, ...), custom_call_target="tpu_custom_call" | custom-call | flops 1200000000 | bytes 6000000 | tf_op jit(solution)/shard_map/block_tokens/pallas_call | solution.py:387
  69.0 2.8 %collective-permute-start.4 = (bf16[3,24,512]{2,1,0:T(8,128)(2,1)S(1)}, bf16[3,24,512]{2,1,0:T(8,128)(2,1)S(1)}, u32[]{:S(2)}, u32[]{:S(2)}) collective-permute-start(bf16[3,24,512]{2,1,0:T(8,128)(2,1)S(1)} %bitcast.14), channel_id=1, source_target_pairs={{0,32},{1,33},{2,34},{3,35},{4,36},{5,37},{6,38},{7,39},{8,40},{9,... | collective-permute-start | bytes 221192 | tf_op jit(solution)/shard_map/ppermute | solution.py:409
  71.9 5.6 %collective-permute-done.4 = bf16[3,24,512]{2,1,0:T(8,128)(2,1)S(1)} collective-permute-done((bf16[3,24,512]{2,1,0:T(8,128)(2,1)S(1)}, bf16[3,24,512]{2,1,0:T(8,128)(2,1)S(1)}, u32[]{:S(2)}, u32[]{:S(2)}) %collective-permute-start.4) | collective-permute-done | bytes 73760 | tf_op jit(solution)/shard_map/ppermute | solution.py:409
  77.6 14.0 %collective-permute-done.5 = bf16[24,6,512]{2,1,0:T(8,128)(2,1)S(1)} collective-permute-done((bf16[24,6,512]{2,1,0:T(8,128)(2,1)S(1)}, bf16[24,6,512]{2,1,0:T(8,128)(2,1)S(1)}, u32[]{:S(2)}, u32[]{:S(2)}) %collective-permute-start.5) | collective-permute-done | bytes 147488 | tf_op jit(solution)/shard_map/ppermute | solution.py:409
  91.6 1.0 fusion.2
  92.6 1.4 %reduce_sum.30 = bf16[16,2048]{1,0:T(8,128)(2,1)S(1)} reduce(bf16[16,16,2048]{2,1,0:T(8,128)(2,1)} %all-to-all-done, bf16[]{:T(256)} %constant.14.clone.1), dimensions={0}, to_apply=%region_0.0 | reduce | flops 491520 | bytes 1114114 | tf_op jit(solution)/shard_map/reduce_sum | solution.py:434
  94.0 16.3 %all_to_all.10 = bf16[8,16,2048]{2,1,0:T(8,128)(2,1)S(1)} all-to-all(bf16[8,16,2048]{2,1,0:T(8,128)(2,1)S(1)} %broadcast_in_dim.19), channel_id=1, replica_groups=mesh['lat'=8,'tile'=16,'core'=2] {'lat'}, dimensions={0} | all-to-all | bytes 1048576 | tf_op jit(solution)/shard_map/all_to_all | solution.py:436
  110.9 0.7 convert_reduce_fusion
  (32 shorter events, 1.8 us)
Async XLA Ops:
  0.6 6.7 %copy-start.7 = (bf16[24,24,512]{2,1,0:T(8,128)(2,1)S(1)}, bf16[24,24,512]{2,1,0:T(8,128)(2,1)}, u32[]{:S(2)}) copy-start(bf16[24,24,512]{2,1,0:T(8,128)(2,1)} %param.17) | copy-start | bytes 1769476
  0.6 6.8 %copy-start.8 = (bf16[24,24,512]{2,1,0:T(8,128)(2,1)S(1)}, bf16[24,24,512]{2,1,0:T(8,128)(2,1)}, u32[]{:S(2)}) copy-start(bf16[24,24,512]{2,1,0:T(8,128)(2,1)} %param.18) | copy-start | bytes 1769476
  2.7 9.9 %collective-permute-start = (bf16[48,6,512]{2,1,0:T(8,128)(2,1)S(1)}, bf16[48,6,512]{2,1,0:T(8,128)(2,1)S(1)}, u32[]{:S(2)}, u32[]{:S(2)}) collective-permute-start(bf16[48,6,512]{2,1,0:T(8,128)(2,1)S(1)} %pad_maximum_fusion.3), channel_id=1, source_target_pairs={{0,31},{1,0},{2,1},{3,2},{4,3},{5,4},{6,5},{7,6},{8,7},{9,8},{10,9... | collective-permute-start | bytes 884744 | tf_op jit(solution)/shard_map/ppermute | solution.py:409
  12.7 9.8 %collective-permute-start.2 = (bf16[13,24,512]{2,1,0:T(8,128)(2,1)S(1)}, bf16[13,24,512]{2,1,0:T(8,128)(2,1)S(1)}, u32[]{:S(2)}, u32[]{:S(2)}) collective-permute-start(bf16[13,24,512]{2,1,0:T(8,128)(2,1)S(1)} %fusion.4), channel_id=1, source_target_pairs={{0,224},{1,225},{2,226},{3,227},{4,228},{5,229},{6,230},{7,231},{8... | collective-permute-start | bytes 958472 | tf_op jit(solution)/shard_map/ppermute | solution.py:409
  18.0 8.2 %collective-permute-start.1 = (bf16[3,24,512]{2,1,0:T(8,128)(2,1)S(1)}, bf16[3,24,512]{2,1,0:T(8,128)(2,1)S(1)}, u32[]{:S(2)}, u32[]{:S(2)}) collective-permute-start(bf16[3,24,512]{2,1,0:T(8,128)(2,1)S(1)} %pad_maximum_fusion.6), channel_id=1, source_target_pairs={{0,32},{1,33},{2,34},{3,35},{4,36},{5,37},{6,38},{7,39},{8,40},{9,... | collective-permute-start | bytes 221192 | tf_op jit(solution)/shard_map/ppermute | solution.py:409
  51.0 3.0 %collective-permute-start.3 = (bf16[16,16,2048]{2,1,0:T(8,128)(2,1)}, bf16[16,16,2048]{2,1,0:T(8,128)(2,1)S(1)}, u32[]{:S(2)}, u32[]{:S(2)}) collective-permute-start(bf16[16,16,2048]{2,1,0:T(8,128)(2,1)} %get-tuple-element.12), channel_id=1, source_target_pairs={{0,1},{1,0},{2,3},{3,2},{4,5},{5,4},{6,7},{7,6},{8,9},{9,8},{10,11... | collective-permute-start | bytes 3145736 | tf_op jit(solution)/shard_map/ppermute | solution.py:423
  53.9 8.4 %copy-start.1 = (bf16[640,1536]{1,0:T(8,128)(2,1)S(1)}, bf16[640,1536]{1,0:T(8,128)(2,1)}, u32[]{:S(2)}) copy-start(bf16[640,1536]{1,0:T(8,128)(2,1)} %get-tuple-element.16.dqkv_ref) | copy-start | bytes 5898244
  56.7 5.7 %copy-start = (bf16[36,24,512]{2,1,0:T(8,128)(2,1)S(1)}, bf16[36,24,512]{2,1,0:T(8,128)(2,1)}, u32[]{:S(2)}) copy-start(bf16[36,24,512]{2,1,0:T(8,128)(2,1)} %pad_maximum_fusion) | copy-start | bytes 2654212
  56.7 5.7 %copy-start.3 = (bf16[640,512]{1,0:T(8,128)(2,1)S(1)}, bf16[640,512]{1,0:T(8,128)(2,1)}, u32[]{:S(2)}) copy-start(bf16[640,512]{1,0:T(8,128)(2,1)} %get-tuple-element.15.gn_ref) | copy-start | bytes 1966084
  56.7 5.7 %copy-start.6 = (f32[512]{0:T(512)S(1)}, f32[512]{0:T(512)}, u32[]{:S(2)}) copy-start(f32[512]{0:T(512)} %param.19) | copy-start | bytes 6148
  56.7 35.9 %all-to-all-start = ((bf16[16,16,2048]{2,1,0:T(8,128)(2,1)}), bf16[16,16,2048]{2,1,0:T(8,128)(2,1)}, u32[]{:S(2)}, u32[]{:S(2)}) async-start(bf16[16,16,2048]{2,1,0:T(8,128)(2,1)} %add.3), calls=%async_computation | async-start | bytes 2097152 | tf_op jit(solution)/shard_map/all_to_all | solution.py:425
  62.4 1.4 %copy-start.2 = (bf16[512,1536]{1,0:T(8,128)(2,1)S(1)}, bf16[512,1536]{1,0:T(8,128)(2,1)}, u32[]{:S(2)}) copy-start(bf16[512,1536]{1,0:T(8,128)(2,1)} %wqkv_ref.1) | copy-start | bytes 4718596
  63.8 0.9 copy-start.4
  64.7 0.9 copy-start.5
  69.0 8.4 %collective-permute-start.4 = (bf16[3,24,512]{2,1,0:T(8,128)(2,1)S(1)}, bf16[3,24,512]{2,1,0:T(8,128)(2,1)S(1)}, u32[]{:S(2)}, u32[]{:S(2)}) collective-permute-start(bf16[3,24,512]{2,1,0:T(8,128)(2,1)S(1)} %bitcast.14), channel_id=1, source_target_pairs={{0,32},{1,33},{2,34},{3,35},{4,36},{5,37},{6,38},{7,39},{8,40},{9,... | collective-permute-start | bytes 221192 | tf_op jit(solution)/shard_map/ppermute | solution.py:409
  77.5 14.1 %collective-permute-start.5 = (bf16[24,6,512]{2,1,0:T(8,128)(2,1)S(1)}, bf16[24,6,512]{2,1,0:T(8,128)(2,1)S(1)}, u32[]{:S(2)}, u32[]{:S(2)}) collective-permute-start(bf16[24,6,512]{2,1,0:T(8,128)(2,1)S(1)} %pad_maximum_fusion.5), channel_id=1, source_target_pairs={{0,1},{1,2},{2,3},{3,4},{4,5},{5,6},{6,7},{7,8},{8,9},{9,10},{10,1... | collective-permute-start | bytes 442376 | tf_op jit(solution)/shard_map/ppermute | solution.py:409

commit v2 on v1

v2 whole, which is shorter than its diff:
```python
import functools

import jax
import jax.numpy as jnp
import numpy as np
from jax import lax
from jax.experimental import pallas as pl
from jax.experimental.pallas import tpu as pltpu
from jax.sharding import Mesh, PartitionSpec as P

HEADS = 8
HEAD = 64
WLAT = 6
WLON = 12
SLAT = 3
SLON = 6
D = 512
ROWS = 24
COLS = 24
WR = WLAT * COLS
WIN = WLAT * WLON
WP = 80
WRP = 2 * WP
NWR = 6
EARLY = 3
CROWS = 28
PAIRS = 13
QROWS = 160

EPSILON = 1e-05
GRANT = 63 * 1024 * 1024
MASKED = -1000000000.0
OUTSIDE = -3.0e38
BF = jnp.bfloat16
F32 = jnp.float32


def window_row(i, col):
    return (col // WLON) * WP + i * WLON + col % WLON


def to_windows():
    out = np.zeros((WRP, WR), np.float32)
    for t in range(WR):
        out[window_row(t // COLS, t % COLS), t] = 1
    return out.astype(jnp.bfloat16)


def cot_offsets(pairs, padded):
    out = np.zeros((4 * padded, pairs * 2 * COLS), np.float32)
    for a in range(pairs):
        for rp in range(2):
            for col in range(COLS):
                q = (col % 2) * 2 + rp
                out[q * padded + a * 12 + col // 2, (2 * a + rp) * COLS + col] = 1
    return out.astype(jnp.bfloat16)


FINE_PARTS = ((0, 0), (0, 1), (0, 2), (1, 2), (1, 3), (2, 3), (2, 4), (3, 4), (3, 5))


def fine_offsets():
    out = np.zeros((len(FINE_PARTS), 4 * 48, WRP), np.float32)
    for n, (g, k) in enumerate(FINE_PARTS):
        padded = 48 if g < 3 else 16
        for a in range(4 * g, min(4 * g + 4, PAIRS)):
            for rp in range(2):
                f = 5 + 2 * a + rp
                if f // WLAT != k:
                    continue
                for col in range(COLS):
                    q = (col % 2) * 2 + rp
                    out[n, q * padded + (a - 4 * g) * 12 + col // 2, window_row(f % WLAT, col)] = 1
    return out.astype(jnp.bfloat16)


def from_offsets():
    out = np.zeros((4, WRP, 256), np.float32)
    for k in range(1, 5):
        for t in range(WR):
            f = WLAT * k + t // COLS
            col = t % COLS
            a, rp = divmod(f - 5, 2)
            q = (col % 2) * 2 + rp
            out[k - 1, window_row(t // COLS, col), q * 64 + 12 * a + col // 2 - 32 * (k - 1)] = 1
    return out.astype(jnp.bfloat16)


def dot(a, b):
    return jnp.dot(a, b, preferred_element_type=F32)


def dot_nt(a, b):
    return lax.dot_general(a, b, (((1,), (1,)), ((), ())), preferred_element_type=F32)


def dot_tn(a, b):
    return lax.dot_general(a, b, (((0,), (0,)), ((), ())), preferred_element_type=F32)


def norm_parts(values):
    average = jnp.mean(values, axis=-1, keepdims=True)
    centred = values - average
    spread = jnp.mean(centred * centred, axis=-1, keepdims=True)
    scale = lax.rsqrt(spread + EPSILON)
    return centred * scale, scale


def norm_back(hat, scale, dy):
    mean_dy = jnp.mean(dy, axis=-1, keepdims=True)
    mean_dyh = jnp.mean(dy * hat, axis=-1, keepdims=True)
    return scale * (dy - mean_dy - hat * mean_dyh)


def stacked(two, low):
    gap = jnp.zeros((128 - WP, 2 * HEAD), BF)
    return jnp.concatenate([two * low, gap, two * (1 - low), gap], axis=0)


def over_queries(keys_by_queries, rows, first_lane):
    both = [dot_tn(keys_by_queries[:, 128 * i : 128 * i + WP], rows) for i in range(2)]
    return jnp.where(first_lane, both[0], both[1])


def padded_keys(values):
    return jnp.concatenate([values, jnp.zeros((WP - WIN, 256), F32)], axis=0).astype(BF)


UNITS = [(w, hp) for w in range(2) for hp in range(HEADS // 2)]


def lane_halves():
    first_lane = lax.broadcasted_iota(jnp.int32, (1, 2 * HEAD), 1) < HEAD
    return first_lane, first_lane.astype(F32).astype(BF)


def rows_of(start, size):
    return pl.ds(pl.multiple_of(start, 16), size)


def heads(qkv, start, w, hp, low):
    win = rows_of(start + WP * w, WP)
    q2 = qkv[win, 128 * hp : 128 * hp + 128]
    k2 = qkv[win, D + 128 * hp : D + 128 * hp + 128]
    v2 = qkv[win, 2 * D + 128 * hp : 2 * D + 128 * hp + 128]
    return stacked(q2 * 0.125, low), k2, v2, win


def attention(first, mask, x_ref, px, gain, wqkv, wproj, xw, normed, qkv, probs, attn, fine):
    first_lane, low = lane_halves()
    base = WRP * first
    span = slice(base, base + 3 * WRP)
    for k in range(3):
        rows = slice(base + WRP * k, base + WRP * k + WRP)
        x = dot(px[...], x_ref[WR * k : WR * k + WR, :])
        xw[WRP * k : WRP * k + WRP, :] = x.astype(BF)
        hat, _ = norm_parts(x)
        normed[rows, :] = (hat * gain[...]).astype(BF)
    for j in range(6):
        columns = slice(256 * j, 256 * j + 256)
        qkv[span, columns] = dot(normed[span, :], wqkv[:, columns]).astype(BF)

    def window_row(k, carry):
        masked = None if mask is None else mask(k)
        parts = [heads(qkv, k * WRP, w, hp, low) for w, hp in UNITS]
        s = [dot_nt(k2, qs)[:WIN] for qs, k2, _, _ in parts]
        if masked is not None:
            s = [jnp.where(masked, MASKED, v) for v in s]
        top = [jnp.max(v, axis=0, keepdims=True) for v in s]
        e = [jnp.exp(v - t) for v, t in zip(s, top)]
        total = [jnp.sum(v, axis=0, keepdims=True) for v in e]
        p = [v * (1.0 / t) for v, t in zip(e, total)]
        for (w, hp), v in zip(UNITS, p):
            probs[k, 4 * w + hp] = v
        o = [over_queries(padded_keys(v), v2, first_lane) for v, (_, _, v2, _) in zip(p, parts)]
        for (w, hp), v, (_, _, _, win) in zip(UNITS, o, parts):
            attn[win, 128 * hp : 128 * hp + 128] = v.astype(BF)
        return carry

    lax.fori_loop(first, first + 3, window_row, 0)
    for j in range(2):
        columns = slice(256 * j, 256 * j + 256)
        fine[span, columns] = (
            xw[:, columns].astype(F32) + dot(attn[span, :], wproj[:, columns])
        ).astype(BF)


def early_kernel(x_ref, px_ref, ng_ref, wqkv, wproj, normed, qkv, probs, attn, fine, xw):
    attention(0, None, x_ref, px_ref, ng_ref, wqkv, wproj, xw, normed, qkv, probs, attn, fine)


def kernel(
    lat_size, x_ref, c_ref, ng_ref, mg_ref, eg_ref, px_ref, pf_ref, pc_ref, pc3_ref, pi_ref,
    wqkv_hbm, wproj_hbm, wm_hbm, we_hbm, normed_hbm, qkv_hbm, probs_hbm, attn_hbm, fine_hbm,
    mine_hbm, other_hbm, gn_hbm, dqkv_hbm,
    wqkv, wproj, wm, we, xw, normed, qkv, probs, attn, fine, fq, cq, mg, dw, gq, gn, d_attn, dqkv, mine, other, sems,
):
    lat = lax.axis_index("lat")
    core = lax.axis_index("core")
    done = slice(0, EARLY * WRP)
    sources = (
        (wqkv_hbm, wqkv), (wproj_hbm, wproj), (fine_hbm, fine.at[done]), (wm_hbm, wm), (we_hbm, we),
        (probs_hbm, probs.at[0:EARLY]), (qkv_hbm, qkv.at[done]),
        (attn_hbm, attn.at[done]), (normed_hbm, normed.at[done]),
    )
    loads = [pltpu.make_async_copy(src, dst, sems.at[i]) for i, (src, dst) in enumerate(sources)]
    for load in loads:
        load.start()

    key = lax.broadcasted_iota(jnp.int32, (WIN, 256), 0)
    query = lax.broadcasted_iota(jnp.int32, (WIN, 256), 1) % 128
    apart = (key >= WIN // 2) != (query >= WIN // 2)
    first_lane, low = lane_halves()

    def masked_at(k):
        edge = ((k == NWR - 1) & (lat == 0)) | ((k == EARLY) & (lat == lat_size - 1))
        return apart & edge

    loads[0].wait()
    loads[1].wait()
    attention(EARLY, masked_at, x_ref, px_ref, ng_ref, wqkv, wproj, xw, normed, qkv, probs, attn, fine)
    loads[2].wait()

    for g in range(4):
        n = 48 if g < 3 else 16
        f = sum(
            dot(pf_ref[m, : 4 * n, :], fine[WRP * k : WRP * k + WRP, :])
            for m, (gg, k) in enumerate((g_, (k_ - 1) % NWR) for g_, k_ in FINE_PARTS)
            if gg == g
        ).astype(BF)
        if g < 3:
            c = dot(pc_ref[...], c_ref[48 + 192 * g : 48 + 192 * g + 192, :]).astype(BF)
        else:
            c = dot(pc3_ref[...], c_ref[624:672, :]).astype(BF)
        for q in range(4):
            fq[q, 48 * g : 48 * g + n, :] = f[n * q : n * q + n]
            cq[q, 48 * g : 48 * g + n, :] = c[n * q : n * q + n]

    def merge_stats(rows):
        total = jnp.zeros((32, 1), F32)
        for q in range(4):
            total = total + jnp.sum(fq[q, rows, :].astype(F32), axis=-1, keepdims=True)
        average = total * (1.0 / (4 * D))
        total = jnp.zeros((32, 1), F32)
        for q in range(4):
            centred = fq[q, rows, :].astype(F32) - average
            total = total + jnp.sum(centred * centred, axis=-1, keepdims=True)
        return average, lax.rsqrt(total * (1.0 / (4 * D)) + EPSILON)

    for r in range(QROWS // 32):
        rows = slice(32 * r, 32 * r + 32)
        average, scale = merge_stats(rows)
        for q in range(4):
            hat = (fq[q, rows, :].astype(F32) - average) * scale
            mg[rows, D * q : D * q + D] = (hat * mg_ref[:, D * q : D * q + D]).astype(BF)

    loads[3].wait()
    loads[4].wait()
    coarse = dot(mg[...], wm[...]).astype(BF)
    for q in range(4):
        qq = (0, 2, 1, 3)[q]
        wide = dot(coarse, we[:, D * qq : D * qq + D])
        hat, scale = norm_parts(wide)
        dy = cq[q].astype(F32) * eg_ref[...]
        dw[:, D * qq : D * qq + D] = norm_back(hat, scale, dy).astype(BF)
    d_coarse = dot_nt(dw[...], we[...]).astype(BF)
    mg[...] = dot_nt(d_coarse, wm[...]).astype(BF)

    for r in range(QROWS // 32):
        rows = slice(32 * r, 32 * r + 32)
        average, scale = merge_stats(rows)
        sum_dy = jnp.zeros((32, 1), F32)
        sum_dyh = jnp.zeros((32, 1), F32)
        for q in range(4):
            hat = (fq[q, rows, :].astype(F32) - average) * scale
            dy = mg[rows, D * q : D * q + D].astype(F32) * mg_ref[:, D * q : D * q + D]
            sum_dy = sum_dy + jnp.sum(dy, axis=-1, keepdims=True)
            sum_dyh = sum_dyh + jnp.sum(dy * hat, axis=-1, keepdims=True)
        mean_dy = sum_dy * (1.0 / (4 * D))
        mean_dyh = sum_dyh * (1.0 / (4 * D))
        for q in range(4):
            hat = (fq[q, rows, :].astype(F32) - average) * scale
            dy = mg[rows, D * q : D * q + D].astype(F32) * mg_ref[:, D * q : D * q + D]
            back = (scale * (dy - mean_dy - hat * mean_dyh)).astype(BF)
            gq[q, rows, :] = (cq[q, rows, :].astype(F32) + back.astype(F32)).astype(BF)

    for k in range(4):
        parts = jnp.concatenate([gq[q, 32 * k : 32 * k + 64, :] for q in range(4)], axis=0)
        gn[WRP * k : WRP * k + WRP, :] = dot(pi_ref[k], parts).astype(BF)

    stores = []

    def store(src, dst):
        copy = pltpu.make_async_copy(src, dst, sems.at[9 + len(stores)])
        copy.start()
        stores.append(copy)

    def put(j, block):
        columns = slice(D * j, D * j + D)
        pairs = block.astype(BF).reshape(mine.shape[0], 2, mine.shape[1], D)
        even, odd = pairs[:, 0], pairs[:, 1]
        mine[:, :, columns] = jnp.where(core == 0, even, odd)
        other[:, :, columns] = jnp.where(core == 0, odd, even)
        store(other.at[:, :, columns], other_hbm.at[:, :, columns])
        store(mine.at[:, :, columns], mine_hbm.at[:, :, columns])

    for load in loads[5:]:
        load.wait()
    inner = slice(0, 4 * WRP)
    store(gn, gn_hbm)
    put(3, dot_tn(attn[inner, :], gn[...]))

    for j in range(2):
        columns = slice(256 * j, 256 * j + 256)
        d_attn[:, columns] = dot_nt(gn[...], wproj[columns, :]).astype(BF)

    def backward(k, carry):
        start = pl.multiple_of(k * WRP, 16)
        masked = masked_at(k)
        parts = [heads(qkv, start, w, hp, low) for w, hp in UNITS]
        do = [
            stacked(d_attn[win, 128 * hp : 128 * hp + 128], low)
            for (_, hp), (_, _, _, win) in zip(UNITS, parts)
        ]
        dp = [dot_nt(v2, d)[:WIN] for d, (_, _, v2, _) in zip(do, parts)]
        p = [probs[k, 4 * w + hp] for w, hp in UNITS]
        dv = [dot(padded_keys(v), d) for v, d in zip(p, do)]
        dp = [v.astype(BF).astype(F32) for v in dp]
        inner = [jnp.sum(a * b, axis=0, keepdims=True) for a, b in zip(dp, p)]
        ds = [b * (a - c) for a, b, c in zip(dp, p, inner)]
        ds = [padded_keys(jnp.where(masked, 0.0, v)) for v in ds]
        dk = [dot(v, qs) for v, (qs, _, _, _) in zip(ds, parts)]
        dq = [over_queries(v, k2, first_lane) * 0.125 for v, (_, k2, _, _) in zip(ds, parts)]
        for i, ((_, hp), (_, _, _, win)) in enumerate(zip(UNITS, parts)):
            lanes = slice(128 * hp, 128 * hp + 128)
            dqkv[win, lanes] = dq[i].astype(BF)
            dqkv[win, D + lanes.start : D + lanes.stop] = dk[i].astype(BF)
            dqkv[win, 2 * D + lanes.start : 2 * D + lanes.stop] = dv[i].astype(BF)
        return carry

    lax.fori_loop(0, 4, backward, 0)
    store(dqkv, dqkv_hbm)
    for j in range(3):
        put(j, dot_tn(normed[inner, :], dqkv[:, D * j : D * j + D]))
    for copy in stores:
        copy.wait()


def finish_kernel(early_ref, late_ref, gn_ref, dqkv_ref, wqkv_ref, ng_ref, px_ref, pxt_ref, dwork_ref, d_normed):
    for j in range(2):
        columns = slice(256 * j, 256 * j + 256)
        d_normed[:, columns] = dot_nt(dqkv_ref[...], wqkv_ref[columns, :]).astype(BF)

    for k in range(4):
        rows = slice(WRP * k, WRP * k + WRP)
        x = early_ref[WR * k : WR * k + WR, :] if k < EARLY else late_ref[:WR, :]
        hat, scale = norm_parts(dot(px_ref[...], x))
        back = norm_back(hat, scale, d_normed[rows, :].astype(F32) * ng_ref[...])
        d_work = (gn_ref[rows, :].astype(F32) + back).astype(BF)
        dwork_ref[WR * k : WR * k + WR, :] = dot(pxt_ref[...], d_work).astype(BF)


VMEM = pl.BlockSpec(memory_space=pltpu.VMEM)
HBM = pl.BlockSpec(memory_space=pl.ANY)


def start_early(x, norm_gain, w_qkv, w_proj):
    rows = EARLY * WRP
    shapes = [((rows, D), BF), ((rows, 3 * D), BF), ((EARLY, HEADS, WIN, 256), F32), ((rows, D), BF), ((rows, D), BF)]
    return pl.pallas_call(
        early_kernel,
        out_shape=tuple(jax.ShapeDtypeStruct(*one) for one in shapes),
        in_specs=[VMEM] * 5,
        out_specs=(VMEM,) * 5,
        scratch_shapes=[pltpu.VMEM((rows, D), BF)],
        compiler_params=pltpu.CompilerParams(vmem_limit_bytes=GRANT),
        cost_estimate=pl.CostEstimate(flops=1_400_000_000, bytes_accessed=8_000_000, transcendentals=0),
        name="block_early",
    )(x, jnp.asarray(to_windows()), norm_gain[None], w_qkv, w_proj)


def compute(tiles, lats, early, x, c, norm_gain, w_qkv, w_proj, merge_gain, w_merge, w_expand, expand_gain):
    bf = lambda *shape: pltpu.VMEM(shape, BF)
    share = (tiles, D // (2 * tiles), 4 * D)
    return pl.pallas_call(
        functools.partial(kernel, lats),
        out_shape=tuple(
            jax.ShapeDtypeStruct(shape, BF) for shape in (share, share, (4 * WRP, D), (4 * WRP, 3 * D))
        ),
        in_specs=[VMEM] * 10 + [HBM] * 9,
        out_specs=(HBM,) * 4,
        scratch_shapes=[
            bf(D, 3 * D), bf(D, D), bf(4 * D, 2 * D), bf(2 * D, 4 * D),
            bf((NWR - EARLY) * WRP, D), bf(NWR * WRP, D), bf(NWR * WRP, 3 * D), pltpu.VMEM((NWR, HEADS, WIN, 256), F32),
            bf(NWR * WRP, D), bf(NWR * WRP, D),
            bf(4, QROWS, D), bf(4, QROWS, D), bf(QROWS, 4 * D), bf(QROWS, 4 * D), bf(4, QROWS, D),
            bf(4 * WRP, D), bf(4 * WRP, D), bf(4 * WRP, 3 * D), bf(*share), bf(*share),
            pltpu.SemaphoreType.DMA((19,)),
        ],
        compiler_params=pltpu.CompilerParams(vmem_limit_bytes=GRANT),
        cost_estimate=pl.CostEstimate(flops=7_000_000_000, bytes_accessed=18_000_000, transcendentals=0),
        name="block",
    )(
        x, c, norm_gain[None], merge_gain[None], expand_gain[None],
        jnp.asarray(to_windows()), jnp.asarray(fine_offsets()),
        jnp.asarray(cot_offsets(4, 48)), jnp.asarray(cot_offsets(1, 16)), jnp.asarray(from_offsets()),
        w_qkv, w_proj, w_merge, w_expand, *early,
    )


def finish_tokens(x_early, x, gn, dqkv, w_qkv, norm_gain):
    return pl.pallas_call(
        finish_kernel,
        out_shape=jax.ShapeDtypeStruct((4 * WR, D), BF),
        in_specs=[VMEM] * 8,
        out_specs=VMEM,
        scratch_shapes=[pltpu.VMEM((4 * WRP, D), BF)],
        compiler_params=pltpu.CompilerParams(vmem_limit_bytes=GRANT),
        cost_estimate=pl.CostEstimate(flops=1_200_000_000, bytes_accessed=6_000_000, transcendentals=0),
        name="block_tokens",
    )(x_early, x, gn, dqkv, w_qkv, norm_gain[None], jnp.asarray(to_windows()), jnp.asarray(to_windows().T))


def add_kernel(a_ref, b_ref, out_ref):
    out_ref[...] = a_ref[...] + b_ref[...]


def pair_sum(a, b):
    steps = 4 if a.shape[0] % 4 == 0 else 1
    block = pl.BlockSpec((a.shape[0] // steps,) + a.shape[1:], lambda i: (i, 0, 0))
    return pl.pallas_call(
        add_kernel,
        grid=(steps,),
        out_shape=jax.ShapeDtypeStruct(a.shape, BF),
        in_specs=[block, block],
        out_specs=block,
        compiler_params=pltpu.CompilerParams(vmem_limit_bytes=GRANT),
        name="pair_sum",
    )(a, b)


def body(tokens, cotangent, norm_gain, w_qkv, w_proj, merge_gain, w_merge, w_expand, expand_gain):
    lats, tiles, cores = lax.axis_size("lat"), lax.axis_size("tile"), lax.axis_size("core")
    lons = tiles * cores
    names = ("lat", "tile", "core")

    def moved(value, dlat, dlon):
        pairs = []
        for a in range(lats):
            for b in range(lons):
                pairs.append((a * lons + b, ((a + dlat) % lats) * lons + (b + dlon) % lons))
        return lax.ppermute(value, names, pairs)

    beside = moved(jnp.concatenate([tokens[:, :SLON], cotangent[:, :SLON]], axis=0), 0, -1)
    below = moved(jnp.concatenate([tokens[:9], cotangent[:4]], axis=0), -1, 0)
    above = moved(tokens[ROWS - 3 :], 1, 0)
    low_corner = moved(jnp.concatenate([tokens[:9, :SLON], cotangent[:4, :SLON]], axis=0), -1, -1)
    high_corner = moved(tokens[ROWS - 3 :, :SLON], 1, -1)

    first, last = SLAT, ROWS - SLAT
    x_early = jnp.concatenate([tokens[first:last, SLON:], beside[first:last]], axis=1)
    x_early = x_early.reshape(EARLY * WR, D)
    early = start_early(x_early, norm_gain, w_qkv, w_proj)
    early, below, above, low_corner, high_corner = lax.optimization_barrier(
        (early, below, above, low_corner, high_corner)
    )

    left = jnp.concatenate([tokens[last:, SLON:], below[:9, SLON:], above[:, SLON:], tokens[:first, SLON:]], axis=0)
    right = jnp.concatenate([beside[last:ROWS], low_corner[:9], high_corner, beside[:first]], axis=0)
    x = jnp.concatenate([left, right], axis=1).reshape((NWR - EARLY) * WR, D)
    left = jnp.concatenate([cotangent[:, SLON:], below[9:, SLON:]], axis=0)
    right = jnp.concatenate([beside[ROWS:], low_corner[9:]], axis=0)
    c = jnp.concatenate([left, right], axis=1).reshape(CROWS * COLS, D)

    mine, other, gn, dqkv = compute(
        tiles, lats, early, x, c, norm_gain, w_qkv, w_proj, merge_gain, w_merge, w_expand, expand_gain
    )

    theirs = lax.ppermute(other, "core", [(i, cores - 1 - i) for i in range(cores)])
    pair, dqkv = lax.optimization_barrier((pair_sum(mine, theirs), dqkv))
    spread = lax.all_to_all(pair, "tile", 0, 0, tiled=True)

    d_work = finish_tokens(x_early, x, gn, dqkv, w_qkv, norm_gain).reshape(ROWS, COLS, D)
    last_row, last_col = ROWS - SLAT, COLS - SLON
    rows = moved(d_work[last_row:, :last_col], 1, 0)
    corner = moved(d_work[last_row:, last_col:], 1, 1)
    edge = d_work[:last_row, last_col:]
    spread, rows, corner, edge = lax.optimization_barrier((spread, rows, corner, edge))
    columns = moved(edge, 0, 1)
    top = jnp.concatenate([corner, rows], axis=1)
    rest = jnp.concatenate([columns, d_work[:last_row, :last_col]], axis=1)
    d_tokens = jnp.concatenate([top, rest], axis=0)

    share = jnp.sum(spread.astype(F32), axis=0).astype(BF)
    copies = jnp.broadcast_to(share[None], (lats,) + share.shape)
    gathered = lax.all_to_all(copies, "lat", 0, 0, tiled=True)
    grad_qkv = jnp.sum(gathered[:, :, : 3 * D].astype(F32), axis=0)
    grad_proj = jnp.sum(gathered[:, :, 3 * D :].astype(F32), axis=0)
    return (d_tokens, grad_qkv, grad_proj)


def solution(mesh):
    lats, lons = mesh.shape["lat"], mesh.shape["lon"]
    fine_mesh = Mesh(mesh.devices.reshape(lats, lons // 2, 2), ("lat", "tile", "core"))
    lon = ("tile", "core")
    in_specs = (P("lat", lon, None), P("lat", lon, None), P(), P(), P(), P(), P(), P(), P())
    out_specs = (P("lat", lon, None), P(lon, None), P(lon, None))
    return jax.shard_map(body, mesh=fine_mesh, in_specs=in_specs, out_specs=out_specs, check_vma=False)
```

time: 112 us -> 122 us (1.089); the launches traced: 112 us -> 120 us
  blocking collectives: 16.3 us -> 0 us
  Pallas kernels: 27.2 us -> 37.2 us
  starting transfers between devices: 18.7 us -> 28 us
  local copies, waits for them, and re-layouts: 5.63 us -> 14.2 us
  waiting for transfers between devices: 34.3 us -> 31.2 us
    all_to_all x1 -> x0, blocking collectives: 16.3 us -> none  [body(): gathered = lax.all_to_all(copies, 'lat', 0, 0, tiled=True)]
    slice x7 -> x23, local copies, waits for them, and re-layouts: 0.41 us -> 13.3 us  [the longest x1 1.52 us: body(): above = moved(tokens[ROWS - 3:], 1, 0)]
    pallas_call x0 -> x2, Pallas kernels: none -> 10.4 us  [the longest x1 6.81 us: start_early(): pl.pallas_call(early_kernel, out_shape=tuple((jax.ShapeDtypeStruct(*one)...]
    ppermute x5 -> x8, waiting for transfers between devices: 31.4 us -> 23.9 us  [moved(): return lax.ppermute(value, names, pairs)]
    all_to_all x0 -> x1, starting transfers between devices: none -> 4.55 us  [body(): gathered = lax.all_to_all(copies, 'lat', 0, 0, tiled=True)]
    ppermute x5 -> x8, starting transfers between devices: 13 us -> 17.3 us  [moved(): return lax.ppermute(value, names, pairs)]
    all_to_all x0 -> x1, waiting for transfers between devices: none -> 4.06 us  [body(): gathered = lax.all_to_all(copies, 'lat', 0, 0, tiled=True)]
    pallas_call x1, Pallas kernels: 23.8 us -> 20.3 us  [compute(): pl.pallas_call(functools.partial(kernel, lats), out_shape=tuple((jax.Shap...]
  transfers between devices with their start and end apart: 7 -> 11, of which waited for: 6 -> 6; matrix products, arithmetic and copies ran while one was open for 2% -> 9% of each run, Pallas kernels for 3% -> 11%
where the time goes in v2:
time: 122 us; the launch traced here: 120 us
  Pallas kernels  37.2 us (30%)
  waiting for transfers between devices  31.2 us (26%)
  starting transfers between devices  28 us (23%)
  local copies, waits for them, and re-layouts  14.2 us (12%)
  other arithmetic  8.69 us (7%)
    ppermute x8, waiting for transfers between devices, moved(): return lax.ppermute(value, names, pairs)  23.9 us
    pallas_call x1, Pallas kernels, compute(): pl.pallas_call(functools.partial(kernel, lats), out_shape=tuple((jax.Shap...  20.3 us
    ppermute x8, starting transfers between devices, moved(): return lax.ppermute(value, names, pairs)  17.3 us
    pallas_call x1, Pallas kernels, start_early(): pl.pallas_call(early_kernel, out_shape=tuple((jax.ShapeDtypeStruct(*one)...  6.81 us
    pallas_call x1, Pallas kernels, finish_tokens(): pl.pallas_call(finish_kernel, out_shape=jax.ShapeDtypeStruct((4 * WR, D),...  6.46 us
    all_to_all x1, starting transfers between devices, body(): spread = lax.all_to_all(pair, 'tile', 0, 0, tiled=True)  4.89 us
    all_to_all x1, starting transfers between devices, body(): gathered = lax.all_to_all(copies, 'lat', 0, 0, tiled=True)  4.55 us
    all_to_all x1, waiting for transfers between devices, body(): gathered = lax.all_to_all(copies, 'lat', 0, 0, tiled=True)  4.06 us
  transfers between devices with their start and end apart: 11, of which 6 were waited for; matrix products, arithmetic and copies ran while one was open for 9% of the time, Pallas kernels for 11%

profile of v2, /device:TPU:0, one launch (start us, length us, event | category | flops | bytes accessed | tf_op | source)
XLA Modules:
  0.0 120.1 jit_solution(7056017315008110112)
XLA Ops:
  0.7 1.4 %slice.91 = bf16[3,6,512]{2,1,0:T(8,128)(2,1)} slice(bf16[24,24,512]{2,1,0:T(8,128)(2,1)} %param.17), slice={[21:24], [0:6], [0:512]} | slice | bytes 36864 | tf_op jit(solution)/shard_map/slice | solution.py:458
  2.0 5.8 %collective-permute-start.4 = (bf16[3,6,512]{2,1,0:T(8,128)(2,1)}, bf16[3,6,512]{2,1,0:T(8,128)(2,1)}, u32[]{:S(2)}, u32[]{:S(2)}) collective-permute-start(bf16[3,6,512]{2,1,0:T(8,128)(2,1)} %slice.91), channel_id=1, source_target_pairs={{0,63},{1,32},{2,33},{3,34},{4,35},{5,36},{6,37},{7,38},{8,39},{9,... | collective-permute-start | bytes 55304 | tf_op jit(solution)/shard_map/ppermute | solution.py:452
  7.8 1.5 %slice.88 = bf16[3,24,512]{2,1,0:T(8,128)(2,1)} slice(bf16[24,24,512]{2,1,0:T(8,128)(2,1)} %param.17), slice={[21:24], [0:24], [0:512]} | slice | bytes 147456 | tf_op jit(solution)/shard_map/slice | solution.py:456
  9.3 1.8 %collective-permute-start.2 = (bf16[3,24,512]{2,1,0:T(8,128)(2,1)}, bf16[3,24,512]{2,1,0:T(8,128)(2,1)}, u32[]{:S(2)}, u32[]{:S(2)}) collective-permute-start(bf16[3,24,512]{2,1,0:T(8,128)(2,1)} %slice.88), channel_id=1, source_target_pairs={{0,32},{1,33},{2,34},{3,35},{4,36},{5,37},{6,38},{7,39},{8,40},{9,... | collective-permute-start | bytes 221192 | tf_op jit(solution)/shard_map/ppermute | solution.py:452
  13.5 3.8 %collective-permute-start.3 = (bf16[13,6,512]{2,1,0:T(8,128)(2,1)}, bf16[13,6,512]{2,1,0:T(8,128)(2,1)}, u32[]{:S(2)}, u32[]{:S(2)}) collective-permute-start(bf16[13,6,512]{2,1,0:T(8,128)(2,1)} %pad_maximum_fusion.3), channel_id=1, source_target_pairs={{0,255},{1,224},{2,225},{3,226},{4,227},{5,228},{6,229},{7,230},{8... | collective-permute-start | bytes 239624 | tf_op jit(solution)/shard_map/ppermute | solution.py:452
  17.4 1.1 collective-permute-start
  19.2 2.0 %collective-permute-start.1 = (bf16[13,24,512]{2,1,0:T(8,128)(2,1)}, bf16[13,24,512]{2,1,0:T(8,128)(2,1)}, u32[]{:S(2)}, u32[]{:S(2)}) collective-permute-start(bf16[13,24,512]{2,1,0:T(8,128)(2,1)} %pad_maximum_fusion.2), channel_id=1, source_target_pairs={{0,224},{1,225},{2,226},{3,227},{4,228},{5,229},{6,230},{7,231},{8... | collective-permute-start | bytes 958472 | tf_op jit(solution)/shard_map/ppermute | solution.py:452
  22.3 1.7 %collective-permute-done = bf16[48,6,512]{2,1,0:T(8,128)(2,1)S(1)} collective-permute-done((bf16[48,6,512]{2,1,0:T(8,128)(2,1)S(1)}, bf16[48,6,512]{2,1,0:T(8,128)(2,1)S(1)}, u32[]{:S(2)}, u32[]{:S(2)}) %collective-permute-start) | collective-permute-done | bytes 294944 | tf_op jit(solution)/shard_map/ppermute | solution.py:452
  25.4 6.8 %block_early.1 = (bf16[480,512]{1,0:T(8,128)(2,1)}, bf16[480,1536]{1,0:T(8,128)(2,1)}, f32[3,8,72,256]{3,2,1,0:T(8,128)}, bf16[480,512]{1,0:T(8,128)(2,1)}, bf16[480,512]{1,0:T(8,128)(2,1)}) custom-call(bf16[432,512]{1,0:T(8,128)(2,1)} %bitcast.11, bf16[160,144]{1,0:T(8,128)(2,1)} %constant.16.clone.px_ref, f32[1,512]{1,0:T(1,128)} %bitcast.16, ...), custom_call_target="tpu_custom_call" | custom-call | flops 1400000000 | bytes 8000000 | tf_op jit(solution)/shard_map/block_early/pallas_call | solution.py:370
  34.9 1.0 slice.92
  37.9 1.6 %maximum_maximum_fusion.2 = bf16[18,24,512]{2,1,0:T(8,128)(2,1)} fusion(bf16[3,6,512]{2,1,0:T(8,128)(2,1)S(1)} %copy-done.6, bf16[3,6,512]{2,1,0:T(8,128)(2,1)} %collective-permute-done.4, bf16[9,6,512]{2,1,0:T(8,128)(2,1)S(1)} %slice.96, bf16[3,6,512]{2,1,0:T(8,128)(2,1)S(1)} %copy-done.5, bf16[3,18,512]{2,1,0:T(8,128)(2,1)S(1)} %copy-done.4, ...), kind=kLoop, calls=%fused_computation.4 | loop fusion | flops 3538944 | bytes 884736 | tf_op jit(solution)/shard_map/concatenate | solution.py:470
  39.5 20.3 %block.1 = (bf16[16,16,2048]{2,1,0:T(8,128)(2,1)}, bf16[16,16,2048]{2,1,0:T(8,128)(2,1)}, bf16[640,512]{1,0:T(8,128)(2,1)}, bf16[640,1536]{1,0:T(8,128)(2,1)}) custom-call(bf16[432,512]{1,0:T(8,128)(2,1)} %bitcast.13, bf16[672,512]{1,0:T(8,128)(2,1)} %bitcast.15, f32[1,512]{1,0:T(1,128)} %bitcast.17, f32[1,2048]{1,0:T(1,128)} %bitcast.19, ...), custom_call_target="tpu_custom_call" | custom-call | flops 7000000000 | bytes 18000000 | tf_op jit(solution)/shard_map/block/pallas_call | solution.py:385
  59.8 1.3 %collective-permute-start.5 = (bf16[16,16,2048]{2,1,0:T(8,128)(2,1)}, bf16[16,16,2048]{2,1,0:T(8,128)(2,1)}, u32[]{:S(2)}, u32[]{:S(2)}) collective-permute-start(bf16[16,16,2048]{2,1,0:T(8,128)(2,1)} %get-tuple-element.42), channel_id=1, source_target_pairs={{0,1},{1,0},{2,3},{3,2},{4,5},{5,4},{6,7},{7,6},{8,9},{9,8},{10,11... | collective-permute-start | bytes 3145736 | tf_op jit(solution)/shard_map/ppermute | solution.py:479
  61.1 2.6 %collective-permute-done.5.b_ref = bf16[16,16,2048]{2,1,0:T(8,128)(2,1)} collective-permute-done((bf16[16,16,2048]{2,1,0:T(8,128)(2,1)}, bf16[16,16,2048]{2,1,0:T(8,128)(2,1)}, u32[]{:S(2)}, u32[]{:S(2)}) %collective-permute-start.5) | collective-permute-done | bytes 1048608 | tf_op jit(solution)/shard_map/ppermute | solution.py:479
  63.7 3.6 %pair_sum.1 = bf16[16,16,2048]{2,1,0:T(8,128)(2,1)} custom-call(bf16[16,16,2048]{2,1,0:T(8,128)(2,1)} %get-tuple-element.41.a_ref, bf16[16,16,2048]{2,1,0:T(8,128)(2,1)} %collective-permute-done.5.b_ref), custom_call_target="tpu_custom_call" | custom-call | tf_op jit(solution)/shard_map/pair_sum/pallas_call | solution.py:431
  67.3 4.9 %all-to-all-start = ((bf16[16,16,2048]{2,1,0:T(8,128)(2,1)}), bf16[16,16,2048]{2,1,0:T(8,128)(2,1)}, u32[]{:S(2)}, u32[]{:S(2)}) async-start(bf16[16,16,2048]{2,1,0:T(8,128)(2,1)} %pair_sum.1), calls=%async_computation | async-start | bytes 2097152 | tf_op jit(solution)/shard_map/all_to_all | solution.py:481
  72.2 6.5 %block_tokens.1 = bf16[576,512]{1,0:T(8,128)(2,1)} custom-call(bf16[432,512]{1,0:T(8,128)(2,1)} %bitcast.12, bf16[432,512]{1,0:T(8,128)(2,1)} %bitcast.14, bf16[640,512]{1,0:T(8,128)(2,1)} %get-tuple-element.45.gn_ref, bf16[640,1536]{1,0:T(8,128)(2,1)} %get-tuple-element.46.dqkv_ref, bf16[512,1536]{1,0:T(8,128)(2,1)} %wqkv_ref.1, f32[1,512]{1,0:T(1,128)} %bitcast.18, ...), custom_call_target="tpu_custom_call" | custom-call | flops 1200000000 | bytes 6000000 | tf_op jit(solution)/shard_map/block_tokens/pallas_call | solution.py:412
  81.2 1.9 %collective-permute-start.7 = (bf16[3,6,512]{2,1,0:T(8,128)(2,1)S(1)}, bf16[3,6,512]{2,1,0:T(8,128)(2,1)S(1)}, u32[]{:S(2)}, u32[]{:S(2)}) collective-permute-start(bf16[3,6,512]{2,1,0:T(8,128)(2,1)S(1)} %slice.113), channel_id=1, source_target_pairs={{0,33},{1,34},{2,35},{3,36},{4,37},{5,38},{6,39},{7,40},{8,41},{9,... | collective-permute-start | bytes 55304 | tf_op jit(solution)/shard_map/ppermute | solution.py:452
  84.0 15.3 %collective-permute-done.7 = bf16[3,6,512]{2,1,0:T(8,128)(2,1)S(1)} collective-permute-done((bf16[3,6,512]{2,1,0:T(8,128)(2,1)S(1)}, bf16[3,6,512]{2,1,0:T(8,128)(2,1)S(1)}, u32[]{:S(2)}, u32[]{:S(2)}) %collective-permute-start.7) | collective-permute-done | bytes 18464 | tf_op jit(solution)/shard_map/ppermute | solution.py:452
  100.0 1.4 %reduce_sum.30 = bf16[16,2048]{1,0:T(8,128)(2,1)S(1)} reduce(bf16[16,16,2048]{2,1,0:T(8,128)(2,1)} %all-to-all-done, bf16[]{:T(256)} %constant.14.clone.1), dimensions={0}, to_apply=%region_0.0 | reduce | flops 491520 | bytes 1114114 | tf_op jit(solution)/shard_map/reduce_sum | solution.py:494
  102.2 4.6 %all-to-all-start.1 = ((bf16[8,16,2048]{2,1,0:T(8,128)(2,1)}), bf16[8,16,2048]{2,1,0:T(8,128)(2,1)S(1)}, u32[]{:S(2)}, u32[]{:S(2)}) async-start(bf16[8,16,2048]{2,1,0:T(8,128)(2,1)} %broadcast_in_dim.20), calls=%async_computation.1 | async-start | bytes 1048576 | tf_op jit(solution)/shard_map/all_to_all | solution.py:496
  106.8 6.9 %collective-permute-done.8 = bf16[21,6,512]{2,1,0:T(8,128)(2,1)S(1)} collective-permute-done((bf16[21,6,512]{2,1,0:T(8,128)(2,1)S(1)}, bf16[21,6,512]{2,1,0:T(8,128)(2,1)S(1)}, u32[]{:S(2)}, u32[]{:S(2)}) %collective-permute-start.8) | collective-permute-done | bytes 129056 | tf_op jit(solution)/shard_map/ppermute | solution.py:452
  113.7 1.0 maximum_maximum_fusion.1
  114.7 4.1 %all-to-all-done.1 = bf16[8,16,2048]{2,1,0:T(8,128)(2,1)S(1)} async-done(((bf16[8,16,2048]{2,1,0:T(8,128)(2,1)}), bf16[8,16,2048]{2,1,0:T(8,128)(2,1)S(1)}, u32[]{:S(2)}, u32[]{:S(2)}) %all-to-all-start.1) | async-done | bytes 524320 | tf_op jit(solution)/shard_map/all_to_all | solution.py:496
  (54 shorter events, 16.6 us)
Async XLA Ops:
  0.6 16.7 %slice-start = ((bf16[24,24,512]{2,1,0:T(8,128)(2,1)}), bf16[24,6,512]{2,1,0:T(8,128)(2,1)S(1)}, s32[]{:S(2)}) async-start(bf16[24,24,512]{2,1,0:T(8,128)(2,1)} %param.17), calls=%async_computation.2 | async-start | bytes 393216 | tf_op jit(solution)/shard_map/slice | solution.py:454
  0.6 16.6 %slice-start.2 = ((bf16[24,24,512]{2,1,0:T(8,128)(2,1)}), bf16[24,6,512]{2,1,0:T(8,128)(2,1)S(1)}, s32[]{:S(2)}) async-start(bf16[24,24,512]{2,1,0:T(8,128)(2,1)} %param.18), calls=%async_computation.4 | async-start | bytes 393216 | tf_op jit(solution)/shard_map/slice | solution.py:454
  2.0 16.4 %slice-start.1 = ((bf16[24,24,512]{2,1,0:T(8,128)(2,1)}), bf16[9,24,512]{2,1,0:T(8,128)(2,1)S(1)}, s32[]{:S(2)}) async-start(bf16[24,24,512]{2,1,0:T(8,128)(2,1)} %param.17), calls=%async_computation.3 | async-start | bytes 442368 | tf_op jit(solution)/shard_map/slice | solution.py:455
  2.0 16.4 %slice-start.3 = ((bf16[24,24,512]{2,1,0:T(8,128)(2,1)}), bf16[4,24,512]{2,1,0:T(8,128)(2,1)S(1)}, s32[]{:S(2)}) async-start(bf16[24,24,512]{2,1,0:T(8,128)(2,1)} %param.18), calls=%async_computation.5 | async-start | bytes 196608 | tf_op jit(solution)/shard_map/slice | solution.py:455
  2.0 30.3 %collective-permute-start.4 = (bf16[3,6,512]{2,1,0:T(8,128)(2,1)}, bf16[3,6,512]{2,1,0:T(8,128)(2,1)}, u32[]{:S(2)}, u32[]{:S(2)}) collective-permute-start(bf16[3,6,512]{2,1,0:T(8,128)(2,1)} %slice.91), channel_id=1, source_target_pairs={{0,63},{1,32},{2,33},{3,34},{4,35},{5,36},{6,37},{7,38},{8,39},{9,... | collective-permute-start | bytes 55304 | tf_op jit(solution)/shard_map/ppermute | solution.py:452
  9.3 23.0 %collective-permute-start.2 = (bf16[3,24,512]{2,1,0:T(8,128)(2,1)}, bf16[3,24,512]{2,1,0:T(8,128)(2,1)}, u32[]{:S(2)}, u32[]{:S(2)}) collective-permute-start(bf16[3,24,512]{2,1,0:T(8,128)(2,1)} %slice.88), channel_id=1, source_target_pairs={{0,32},{1,33},{2,34},{3,35},{4,36},{5,37},{6,38},{7,39},{8,40},{9,... | collective-permute-start | bytes 221192 | tf_op jit(solution)/shard_map/ppermute | solution.py:452
  13.4 7.8 %copy-start.1 = (bf16[24,24,512]{2,1,0:T(8,128)(2,1)S(1)}, bf16[24,24,512]{2,1,0:T(8,128)(2,1)}, u32[]{:S(2)}) copy-start(bf16[24,24,512]{2,1,0:T(8,128)(2,1)} %param.17) | copy-start | bytes 1769476
  13.5 18.9 %collective-permute-start.3 = (bf16[13,6,512]{2,1,0:T(8,128)(2,1)}, bf16[13,6,512]{2,1,0:T(8,128)(2,1)}, u32[]{:S(2)}, u32[]{:S(2)}) collective-permute-start(bf16[13,6,512]{2,1,0:T(8,128)(2,1)} %pad_maximum_fusion.3), channel_id=1, source_target_pairs={{0,255},{1,224},{2,225},{3,226},{4,227},{5,228},{6,229},{7,230},{8... | collective-permute-start | bytes 239624 | tf_op jit(solution)/shard_map/ppermute | solution.py:452
  17.3 4.1 %copy-start.2 = (bf16[24,24,512]{2,1,0:T(8,128)(2,1)S(1)}, bf16[24,24,512]{2,1,0:T(8,128)(2,1)}, u32[]{:S(2)}) copy-start(bf16[24,24,512]{2,1,0:T(8,128)(2,1)} %param.18) | copy-start | bytes 1769476
  17.4 6.6 %collective-permute-start = (bf16[48,6,512]{2,1,0:T(8,128)(2,1)S(1)}, bf16[48,6,512]{2,1,0:T(8,128)(2,1)S(1)}, u32[]{:S(2)}, u32[]{:S(2)}) collective-permute-start(bf16[48,6,512]{2,1,0:T(8,128)(2,1)S(1)} %pad_maximum_fusion.1), channel_id=1, source_target_pairs={{0,31},{1,0},{2,1},{3,2},{4,3},{5,4},{6,5},{7,6},{8,7},{9,8},{10,9... | collective-permute-start | bytes 884744 | tf_op jit(solution)/shard_map/ppermute | solution.py:452
  19.2 13.1 %collective-permute-start.1 = (bf16[13,24,512]{2,1,0:T(8,128)(2,1)}, bf16[13,24,512]{2,1,0:T(8,128)(2,1)}, u32[]{:S(2)}, u32[]{:S(2)}) collective-permute-start(bf16[13,24,512]{2,1,0:T(8,128)(2,1)} %pad_maximum_fusion.2), channel_id=1, source_target_pairs={{0,224},{1,225},{2,226},{3,227},{4,228},{5,229},{6,230},{7,231},{8... | collective-permute-start | bytes 958472 | tf_op jit(solution)/shard_map/ppermute | solution.py:452
  32.3 5.6 %copy-start.3 = (bf16[3,18,512]{2,1,0:T(8,128)(2,1)S(1)}, bf16[3,18,512]{2,1,0:T(8,128)(2,1)}, u32[]{:S(2)}) copy-start(bf16[3,18,512]{2,1,0:T(8,128)(2,1)} %get-tuple-element.51) | copy-start | bytes 165892
  32.3 5.6 %copy-start.4 = (bf16[3,18,512]{2,1,0:T(8,128)(2,1)S(1)}, bf16[3,18,512]{2,1,0:T(8,128)(2,1)}, u32[]{:S(2)}) copy-start(bf16[3,18,512]{2,1,0:T(8,128)(2,1)} %get-tuple-element.52) | copy-start | bytes 165892
  32.3 5.5 %copy-start.5 = (bf16[3,6,512]{2,1,0:T(8,128)(2,1)S(1)}, bf16[3,6,512]{2,1,0:T(8,128)(2,1)}, u32[]{:S(2)}) copy-start(bf16[3,6,512]{2,1,0:T(8,128)(2,1)} %get-tuple-element.53) | copy-start | bytes 55300
  32.3 5.5 %copy-start.6 = (bf16[3,6,512]{2,1,0:T(8,128)(2,1)S(1)}, bf16[3,6,512]{2,1,0:T(8,128)(2,1)}, u32[]{:S(2)}) copy-start(bf16[3,6,512]{2,1,0:T(8,128)(2,1)} %get-tuple-element.54) | copy-start | bytes 55300
  59.8 3.9 %collective-permute-start.5 = (bf16[16,16,2048]{2,1,0:T(8,128)(2,1)}, bf16[16,16,2048]{2,1,0:T(8,128)(2,1)}, u32[]{:S(2)}, u32[]{:S(2)}) collective-permute-start(bf16[16,16,2048]{2,1,0:T(8,128)(2,1)} %get-tuple-element.42), channel_id=1, source_target_pairs={{0,1},{1,0},{2,3},{3,2},{4,5},{5,4},{6,7},{7,6},{8,9},{9,8},{10,11... | collective-permute-start | bytes 3145736 | tf_op jit(solution)/shard_map/ppermute | solution.py:479
  67.3 32.7 %all-to-all-start = ((bf16[16,16,2048]{2,1,0:T(8,128)(2,1)}), bf16[16,16,2048]{2,1,0:T(8,128)(2,1)}, u32[]{:S(2)}, u32[]{:S(2)}) async-start(bf16[16,16,2048]{2,1,0:T(8,128)(2,1)} %pair_sum.1), calls=%async_computation | async-start | bytes 2097152 | tf_op jit(solution)/shard_map/all_to_all | solution.py:481
  79.5 19.8 %collective-permute-start.6 = (bf16[3,18,512]{2,1,0:T(8,128)(2,1)S(1)}, bf16[3,18,512]{2,1,0:T(8,128)(2,1)S(1)}, u32[]{:S(2)}, u32[]{:S(2)}) collective-permute-start(bf16[3,18,512]{2,1,0:T(8,128)(2,1)S(1)} %slice.112), channel_id=1, source_target_pairs={{0,32},{1,33},{2,34},{3,35},{4,36},{5,37},{6,38},{7,39},{8,40},{9,... | collective-permute-start | bytes 165896 | tf_op jit(solution)/shard_map/ppermute | solution.py:452
  81.2 18.1 %collective-permute-start.7 = (bf16[3,6,512]{2,1,0:T(8,128)(2,1)S(1)}, bf16[3,6,512]{2,1,0:T(8,128)(2,1)S(1)}, u32[]{:S(2)}, u32[]{:S(2)}) collective-permute-start(bf16[3,6,512]{2,1,0:T(8,128)(2,1)S(1)} %slice.113), channel_id=1, source_target_pairs={{0,33},{1,34},{2,35},{3,36},{4,37},{5,38},{6,39},{7,40},{8,41},{9,... | collective-permute-start | bytes 55304 | tf_op jit(solution)/shard_map/ppermute | solution.py:452
  84.0 22.7 %copy-start = (bf16[576,512]{1,0:T(8,128)(2,1)S(1)}, bf16[576,512]{1,0:T(8,128)(2,1)}, u32[]{:S(2)}) copy-start(bf16[576,512]{1,0:T(8,128)(2,1)} %block_tokens.1) | copy-start | bytes 1769476
  102.2 16.6 %all-to-all-start.1 = ((bf16[8,16,2048]{2,1,0:T(8,128)(2,1)}), bf16[8,16,2048]{2,1,0:T(8,128)(2,1)S(1)}, u32[]{:S(2)}, u32[]{:S(2)}) async-start(bf16[8,16,2048]{2,1,0:T(8,128)(2,1)} %broadcast_in_dim.20), calls=%async_computation.1 | async-start | bytes 1048576 | tf_op jit(solution)/shard_map/all_to_all | solution.py:496
  106.8 6.9 %collective-permute-start.8 = (bf16[21,6,512]{2,1,0:T(8,128)(2,1)S(1)}, bf16[21,6,512]{2,1,0:T(8,128)(2,1)S(1)}, u32[]{:S(2)}, u32[]{:S(2)}) collective-permute-start(bf16[21,6,512]{2,1,0:T(8,128)(2,1)S(1)} %slice.114), channel_id=1, source_target_pairs={{0,1},{1,2},{2,3},{3,4},{4,5},{5,6},{6,7},{7,8},{8,9},{9,10},{10,1... | collective-permute-start | bytes 387080 | tf_op jit(solution)/shard_map/ppermute | solution.py:452

commit v3 on v2

--- a/solution.py
+++ b/solution.py
@@ -29,6 +29,7 @@
 
 EPSILON = 1e-05
 GRANT = 63 * 1024 * 1024
+SMALL_GRANT = 24 * 1024 * 1024
 MASKED = -1000000000.0
 OUTSIDE = -3.0e38
 BF = jnp.bfloat16
@@ -373,7 +374,7 @@
         in_specs=[VMEM] * 5,
         out_specs=(VMEM,) * 5,
         scratch_shapes=[pltpu.VMEM((rows, D), BF)],
-        compiler_params=pltpu.CompilerParams(vmem_limit_bytes=GRANT),
+        compiler_params=pltpu.CompilerParams(vmem_limit_bytes=SMALL_GRANT),
         cost_estimate=pl.CostEstimate(flops=1_400_000_000, bytes_accessed=8_000_000, transcendentals=0),
         name="block_early",
     )(x, jnp.asarray(to_windows()), norm_gain[None], w_qkv, w_proj)
@@ -415,28 +416,10 @@
         in_specs=[VMEM] * 8,
         out_specs=VMEM,
         scratch_shapes=[pltpu.VMEM((4 * WRP, D), BF)],
-        compiler_params=pltpu.CompilerParams(vmem_limit_bytes=GRANT),
+        compiler_params=pltpu.CompilerParams(vmem_limit_bytes=SMALL_GRANT),
         cost_estimate=pl.CostEstimate(flops=1_200_000_000, bytes_accessed=6_000_000, transcendentals=0),
         name="block_tokens",
     )(x_early, x, gn, dqkv, w_qkv, norm_gain[None], jnp.asarray(to_windows()), jnp.asarray(to_windows().T))
-
-
-def add_kernel(a_ref, b_ref, out_ref):
-    out_ref[...] = a_ref[...] + b_ref[...]
-
-
-def pair_sum(a, b):
-    steps = 4 if a.shape[0] % 4 == 0 else 1
-    block = pl.BlockSpec((a.shape[0] // steps,) + a.shape[1:], lambda i: (i, 0, 0))
-    return pl.pallas_call(
-        add_kernel,
-        grid=(steps,),
-        out_shape=jax.ShapeDtypeStruct(a.shape, BF),
-        in_specs=[block, block],
-        out_specs=block,
-        compiler_params=pltpu.CompilerParams(vmem_limit_bytes=GRANT),
-        name="pair_sum",
-    )(a, b)
 
 
 def body(tokens, cotangent, norm_gain, w_qkv, w_proj, merge_gain, w_merge, w_expand, expand_gain):
@@ -452,32 +435,26 @@
         return lax.ppermute(value, names, pairs)
 
     beside = moved(jnp.concatenate([tokens[:, :SLON], cotangent[:, :SLON]], axis=0), 0, -1)
-    below = moved(jnp.concatenate([tokens[:9], cotangent[:4]], axis=0), -1, 0)
-    above = moved(tokens[ROWS - 3 :], 1, 0)
-    low_corner = moved(jnp.concatenate([tokens[:9, :SLON], cotangent[:4, :SLON]], axis=0), -1, -1)
-    high_corner = moved(tokens[ROWS - 3 :, :SLON], 1, -1)
-
+    work = jnp.concatenate([tokens[:, SLON:], beside[:ROWS]], axis=1)
+    cwork = jnp.concatenate([cotangent[:, SLON:], beside[ROWS:]], axis=1)
     first, last = SLAT, ROWS - SLAT
-    x_early = jnp.concatenate([tokens[first:last, SLON:], beside[first:last]], axis=1)
-    x_early = x_early.reshape(EARLY * WR, D)
+    below = moved(jnp.concatenate([work[:9], cwork[:4]], axis=0), -1, 0)
+    above = moved(work[last:], 1, 0)
+
+    x_early = work[first:last].reshape(EARLY * WR, D)
     early = start_early(x_early, norm_gain, w_qkv, w_proj)
-    early, below, above, low_corner, high_corner = lax.optimization_barrier(
-        (early, below, above, low_corner, high_corner)
-    )
-
-    left = jnp.concatenate([tokens[last:, SLON:], below[:9, SLON:], above[:, SLON:], tokens[:first, SLON:]], axis=0)
-    right = jnp.concatenate([beside[last:ROWS], low_corner[:9], high_corner, beside[:first]], axis=0)
-    x = jnp.concatenate([left, right], axis=1).reshape((NWR - EARLY) * WR, D)
-    left = jnp.concatenate([cotangent[:, SLON:], below[9:, SLON:]], axis=0)
-    right = jnp.concatenate([beside[ROWS:], low_corner[9:]], axis=0)
-    c = jnp.concatenate([left, right], axis=1).reshape(CROWS * COLS, D)
+    early, below, above = lax.optimization_barrier((early, below, above))
+
+    x = jnp.concatenate([work[last:], below[:9], above, work[:first]], axis=0)
+    x = x.reshape((NWR - EARLY) * WR, D)
+    c = jnp.concatenate([cwork, below[9:]], axis=0).reshape(CROWS * COLS, D)
 
     mine, other, gn, dqkv = compute(
         tiles, lats, early, x, c, norm_gain, w_qkv, w_proj, merge_gain, w_merge, w_expand, expand_gain
     )
 
     theirs = lax.ppermute(other, "core", [(i, cores - 1 - i) for i in range(cores)])
-    pair, dqkv = lax.optimization_barrier((pair_sum(mine, theirs), dqkv))
+    pair, dqkv = lax.optimization_barrier((mine + theirs, dqkv))
     spread = lax.all_to_all(pair, "tile", 0, 0, tiled=True)
 
     d_work = finish_tokens(x_early, x, gn, dqkv, w_qkv, norm_gain).reshape(ROWS, COLS, D)

time: 122 us -> 109 us (0.89); the launches traced: 120 us -> 108 us
  Pallas kernels: 37.2 us -> 27.4 us
  waiting for transfers between devices: 31.2 us -> 40.2 us
  local copies, waits for them, and re-layouts: 14.2 us -> 8.3 us
  starting transfers between devices: 28 us -> 23.2 us
    slice x19 -> x5, local copies, waits for them, and re-layouts: 10.7 us -> 0.37 us  [the longest x2 0.19 us: body(): cwork = jnp.concatenate([cotangent[:, SLON:], beside[ROWS:]], axis=1)]
    ppermute x8 -> x6, waiting for transfers between devices: 23.9 us -> 33.3 us  [moved(): return lax.ppermute(value, names, pairs)]
    unnamed x14 -> x36, local copies, waits for them, and re-layouts: 0.03 us -> 5.01 us
    ppermute x8 -> x6, starting transfers between devices: 17.3 us -> 13 us  [moved(): return lax.ppermute(value, names, pairs)]
    pallas_call x1 -> x0, Pallas kernels: 3.57 us -> none  [pair_sum(): pl.pallas_call(add_kernel, grid=(steps,), out_shape=jax.ShapeDtypeStruct(...]
    pallas_call x1, Pallas kernels: 6.46 us -> 3.14 us  [finish_tokens(): pl.pallas_call(finish_kernel, out_shape=jax.ShapeDtypeStruct((4 * WR, D),...]
    pallas_call x1, Pallas kernels: 6.81 us -> 3.86 us  [start_early(): pl.pallas_call(early_kernel, out_shape=tuple((jax.ShapeDtypeStruct(*one)...]
    concatenate x5, other arithmetic: 4.88 us -> 1.93 us  [the longest x1 0.97 us: body(): c = jnp.concatenate([cwork, below[9:]], axis=0).reshape(CROWS * COLS, D)]
  transfers between devices with their start and end apart: 11 -> 9, of which waited for: 6 -> 6; matrix products, arithmetic and copies ran while one was open for 9% -> 1% of each run, Pallas kernels for 11% -> 6%
where the time goes in v3:
time: 109 us; the launch traced here: 108 us
  waiting for transfers between devices  40.2 us (37%)
  Pallas kernels  27.4 us (25%)
  starting transfers between devices  23.2 us (21%)
  other arithmetic  8.41 us (8%)
  local copies, waits for them, and re-layouts  8.3 us (8%)
    ppermute x6, waiting for transfers between devices, moved(): return lax.ppermute(value, names, pairs)  33.3 us
    pallas_call x1, Pallas kernels, compute(): pl.pallas_call(functools.partial(kernel, lats), out_shape=tuple((jax.Shap...  20.3 us
    ppermute x6, starting transfers between devices, moved(): return lax.ppermute(value, names, pairs)  13 us
    all_to_all x1, starting transfers between devices, body(): spread = lax.all_to_all(pair, 'tile', 0, 0, tiled=True)  5.65 us
    unnamed x36, local copies, waits for them, and re-layouts  5.01 us
    all_to_all x1, starting transfers between devices, body(): gathered = lax.all_to_all(copies, 'lat', 0, 0, tiled=True)  4.26 us
    all_to_all x1, waiting for transfers between devices, body(): gathered = lax.all_to_all(copies, 'lat', 0, 0, tiled=True)  4.06 us
    pallas_call x1, Pallas kernels, start_early(): pl.pallas_call(early_kernel, out_shape=tuple((jax.ShapeDtypeStruct(*one)...  3.86 us
  transfers between devices with their start and end apart: 9, of which 6 were waited for; matrix products, arithmetic and copies ran while one was open for 1% of the time, Pallas kernels for 6%

profile of v3, /device:TPU:0, one launch (start us, length us, event | category | flops | bytes accessed | tf_op | source)
XLA Modules:
  0.0 108.4 jit_solution(14979122271413055338)
XLA Ops:
  0.7 1.0 slice.59
  1.7 0.9 slice.60
  2.7 4.6 %collective-permute-start = (bf16[48,6,512]{2,1,0:T(8,128)(2,1)S(1)}, bf16[48,6,512]{2,1,0:T(8,128)(2,1)S(1)}, u32[]{:S(2)}, u32[]{:S(2)}) collective-permute-start(bf16[48,6,512]{2,1,0:T(8,128)(2,1)S(1)} %pad_maximum_fusion.2), channel_id=1, source_target_pairs={{0,31},{1,0},{2,1},{3,2},{4,3},{5,4},{6,5},{7,6},{8,7},{9,8},{10,9... | collective-permute-start | bytes 884744 | tf_op jit(solution)/shard_map/ppermute | solution.py:435
  7.6 5.0 %collective-permute-done = bf16[48,6,512]{2,1,0:T(8,128)(2,1)S(1)} collective-permute-done((bf16[48,6,512]{2,1,0:T(8,128)(2,1)S(1)}, bf16[48,6,512]{2,1,0:T(8,128)(2,1)S(1)}, u32[]{:S(2)}, u32[]{:S(2)}) %collective-permute-start) | collective-permute-done | bytes 294944 | tf_op jit(solution)/shard_map/ppermute | solution.py:435
  12.7 5.3 %collective-permute-start.1 = (bf16[13,24,512]{2,1,0:T(8,128)(2,1)S(1)}, bf16[13,24,512]{2,1,0:T(8,128)(2,1)S(1)}, u32[]{:S(2)}, u32[]{:S(2)}) collective-permute-start(bf16[13,24,512]{2,1,0:T(8,128)(2,1)S(1)} %fusion.2), channel_id=1, source_target_pairs={{0,224},{1,225},{2,226},{3,227},{4,228},{5,229},{6,230},{7,231},{8... | collective-permute-start | bytes 958472 | tf_op jit(solution)/shard_map/ppermute | solution.py:435
  18.4 3.9 %block_early.1 = (bf16[480,512]{1,0:T(8,128)(2,1)S(1)}, bf16[480,1536]{1,0:T(8,128)(2,1)S(1)}, f32[3,8,72,256]{3,2,1,0:T(8,128)S(1)}, bf16[480,512]{1,0:T(8,128)(2,1)S(1)}, bf16[480,512]{1,0:T(8,128)(2,1)S(1)}) custom-call(bf16[432,512]{1,0:T(8,128)(2,1)S(1)} %bitcast.11, bf16[160,144]{1,0:T(8,128)(2,1)S(1)} %copy-done.5, f32[1,512]{1,0:T(1,128)S(1)} %bitcast.16, ...), custom_call_target="tpu_custom_call" | custom-call | flops 1400000000 | bytes 8000000 | tf_op jit(solution)/shard_map/block_early/pallas_call | solution.py:371
  23.9 2.4 %collective-permute-done.2 = bf16[3,24,512]{2,1,0:T(8,128)(2,1)S(1)} collective-permute-done((bf16[3,24,512]{2,1,0:T(8,128)(2,1)S(1)}, bf16[3,24,512]{2,1,0:T(8,128)(2,1)S(1)}, u32[]{:S(2)}, u32[]{:S(2)}) %collective-permute-start.2) | collective-permute-done | bytes 73760 | tf_op jit(solution)/shard_map/ppermute | solution.py:435
  26.3 1.0 pad_maximum_fusion
  28.1 20.3 %block.1 = (bf16[16,16,2048]{2,1,0:T(8,128)(2,1)}, bf16[16,16,2048]{2,1,0:T(8,128)(2,1)}, bf16[640,512]{1,0:T(8,128)(2,1)}, bf16[640,1536]{1,0:T(8,128)(2,1)}) custom-call(bf16[432,512]{1,0:T(8,128)(2,1)} %bitcast.13, bf16[672,512]{1,0:T(8,128)(2,1)} %bitcast.18, f32[1,512]{1,0:T(1,128)} %bitcast.15, f32[1,2048]{1,0:T(1,128)} %bitcast.19, ...), custom_call_target="tpu_custom_call" | custom-call | flops 7000000000 | bytes 18000000 | tf_op jit(solution)/shard_map/block/pallas_call | solution.py:386
  48.8 2.9 %collective-permute-done.3 = bf16[16,16,2048]{2,1,0:T(8,128)(2,1)S(1)} collective-permute-done((bf16[16,16,2048]{2,1,0:T(8,128)(2,1)}, bf16[16,16,2048]{2,1,0:T(8,128)(2,1)S(1)}, u32[]{:S(2)}, u32[]{:S(2)}) %collective-permute-start.3) | collective-permute-done | bytes 1048608 | tf_op jit(solution)/shard_map/ppermute | solution.py:456
  51.6 2.6 %add.3 = bf16[16,16,2048]{2,1,0:T(8,128)(2,1)} add(bf16[16,16,2048]{2,1,0:T(8,128)(2,1)} %get-tuple-element.37, bf16[16,16,2048]{2,1,0:T(8,128)(2,1)S(1)} %collective-permute-done.3) | non-fusion elementwise | flops 524288 | bytes 3145728 | tf_op jit(solution)/shard_map/add | solution.py:457
  54.3 5.6 %all-to-all-start = ((bf16[16,16,2048]{2,1,0:T(8,128)(2,1)}), bf16[16,16,2048]{2,1,0:T(8,128)(2,1)}, u32[]{:S(2)}, u32[]{:S(2)}) async-start(bf16[16,16,2048]{2,1,0:T(8,128)(2,1)} %add.3), calls=%async_computation | async-start | bytes 2097152 | tf_op jit(solution)/shard_map/all_to_all | solution.py:458
  60.0 1.4 %copy-done.3 = bf16[512,1536]{1,0:T(8,128)(2,1)S(1)} copy-done((bf16[512,1536]{1,0:T(8,128)(2,1)S(1)}, bf16[512,1536]{1,0:T(8,128)(2,1)}, u32[]{:S(2)}) %copy-start.3) | copy-done | bytes 1572888
  61.4 1.1 %copy-done.4 = bf16[640,512]{1,0:T(8,128)(2,1)S(1)} copy-done((bf16[640,512]{1,0:T(8,128)(2,1)S(1)}, bf16[640,512]{1,0:T(8,128)(2,1)}, u32[]{:S(2)}) %copy-start.4) | copy-done | bytes 655384
  62.5 0.9 copy-done.7
  63.3 3.1 %block_tokens.1 = bf16[576,512]{1,0:T(8,128)(2,1)S(1)} custom-call(bf16[432,512]{1,0:T(8,128)(2,1)S(1)} %bitcast.12, bf16[432,512]{1,0:T(8,128)(2,1)S(1)} %bitcast.14, bf16[640,512]{1,0:T(8,128)(2,1)S(1)} %copy-done.4, bf16[640,1536]{1,0:T(8,128)(2,1)S(1)} %copy-done, bf16[512,1536]{1,0:T(8,128)(2,1)S(1)} %copy-done.3, f32[1,512]{1,0:T(1,128)S(1)} %bitcast.17, ...), custom_call_target="tpu_custom_call" | custom-call | flops 1200000000 | bytes 6000000 | tf_op jit(solution)/shard_map/block_tokens/pallas_call | solution.py:413
  66.5 2.8 %collective-permute-start.4 = (bf16[3,18,512]{2,1,0:T(8,128)(2,1)S(1)}, bf16[3,18,512]{2,1,0:T(8,128)(2,1)S(1)}, u32[]{:S(2)}, u32[]{:S(2)}) collective-permute-start(bf16[3,18,512]{2,1,0:T(8,128)(2,1)S(1)} %slice.83), channel_id=1, source_target_pairs={{0,32},{1,33},{2,34},{3,35},{4,36},{5,37},{6,38},{7,39},{8,40},{9,... | collective-permute-start | bytes 165896 | tf_op jit(solution)/shard_map/ppermute | solution.py:435
  69.5 19.1 %collective-permute-done.5 = bf16[3,6,512]{2,1,0:T(8,128)(2,1)S(1)} collective-permute-done((bf16[3,6,512]{2,1,0:T(8,128)(2,1)S(1)}, bf16[3,6,512]{2,1,0:T(8,128)(2,1)S(1)}, u32[]{:S(2)}, u32[]{:S(2)}) %collective-permute-start.5) | collective-permute-done | bytes 18464 | tf_op jit(solution)/shard_map/ppermute | solution.py:435
  88.5 1.4 %reduce_sum.30 = bf16[16,2048]{1,0:T(8,128)(2,1)S(1)} reduce(bf16[16,16,2048]{2,1,0:T(8,128)(2,1)} %all-to-all-done, bf16[]{:T(256)} %constant.14.clone.1), dimensions={0}, to_apply=%region_0.0 | reduce | flops 491520 | bytes 1114114 | tf_op jit(solution)/shard_map/reduce_sum | solution.py:471
  89.9 0.9 broadcast_in_dim.20
  90.8 4.3 %all-to-all-start.1 = ((bf16[8,16,2048]{2,1,0:T(8,128)(2,1)}), bf16[8,16,2048]{2,1,0:T(8,128)(2,1)S(1)}, u32[]{:S(2)}, u32[]{:S(2)}) async-start(bf16[8,16,2048]{2,1,0:T(8,128)(2,1)} %broadcast_in_dim.20), calls=%async_computation.1 | async-start | bytes 1048576 | tf_op jit(solution)/shard_map/all_to_all | solution.py:473
  95.1 6.9 %collective-permute-done.6 = bf16[21,6,512]{2,1,0:T(8,128)(2,1)S(1)} collective-permute-done((bf16[21,6,512]{2,1,0:T(8,128)(2,1)S(1)}, bf16[21,6,512]{2,1,0:T(8,128)(2,1)S(1)}, u32[]{:S(2)}, u32[]{:S(2)}) %collective-permute-start.6) | collective-permute-done | bytes 129056 | tf_op jit(solution)/shard_map/ppermute | solution.py:435
  102.0 1.0 maximum_maximum_fusion
  103.0 4.1 %all-to-all-done.1 = bf16[8,16,2048]{2,1,0:T(8,128)(2,1)S(1)} async-done(((bf16[8,16,2048]{2,1,0:T(8,128)(2,1)}), bf16[8,16,2048]{2,1,0:T(8,128)(2,1)S(1)}, u32[]{:S(2)}, u32[]{:S(2)}) %all-to-all-start.1) | async-done | bytes 524320 | tf_op jit(solution)/shard_map/all_to_all | solution.py:473
  (57 shorter events, 5.2 us)
Async XLA Ops:
  0.6 6.7 %copy-start.16 = (bf16[24,24,512]{2,1,0:T(8,128)(2,1)S(1)}, bf16[24,24,512]{2,1,0:T(8,128)(2,1)}, u32[]{:S(2)}) copy-start(bf16[24,24,512]{2,1,0:T(8,128)(2,1)} %param.17) | copy-start | bytes 1769476
  0.6 6.8 %copy-start.17 = (bf16[24,24,512]{2,1,0:T(8,128)(2,1)S(1)}, bf16[24,24,512]{2,1,0:T(8,128)(2,1)}, u32[]{:S(2)}) copy-start(bf16[24,24,512]{2,1,0:T(8,128)(2,1)} %param.18) | copy-start | bytes 1769476
  2.7 9.9 %collective-permute-start = (bf16[48,6,512]{2,1,0:T(8,128)(2,1)S(1)}, bf16[48,6,512]{2,1,0:T(8,128)(2,1)S(1)}, u32[]{:S(2)}, u32[]{:S(2)}) collective-permute-start(bf16[48,6,512]{2,1,0:T(8,128)(2,1)S(1)} %pad_maximum_fusion.2), channel_id=1, source_target_pairs={{0,31},{1,0},{2,1},{3,2},{4,3},{5,4},{6,5},{7,6},{8,7},{9,8},{10,9... | collective-permute-start | bytes 884744 | tf_op jit(solution)/shard_map/ppermute | solution.py:435
  12.7 5.7 %copy-start.10 = (bf16[512,512]{1,0:T(8,128)(2,1)S(1)}, bf16[512,512]{1,0:T(8,128)(2,1)}, u32[]{:S(2)}) copy-start(bf16[512,512]{1,0:T(8,128)(2,1)} %wproj_hbm.1) | copy-start | bytes 1572868
  12.7 5.7 %copy-start.2 = (bf16[512,1536]{1,0:T(8,128)(2,1)S(1)}, bf16[512,1536]{1,0:T(8,128)(2,1)}, u32[]{:S(2)}) copy-start(bf16[512,1536]{1,0:T(8,128)(2,1)} %wqkv_ref.1) | copy-start | bytes 4718596
  12.7 5.7 %copy-start.5 = (bf16[160,144]{1,0:T(8,128)(2,1)S(1)}, bf16[160,144]{1,0:T(8,128)(2,1)}, u32[]{:S(2)}) copy-start(bf16[160,144]{1,0:T(8,128)(2,1)} %constant.16.clone.px_ref) | copy-start | bytes 138244
  12.7 5.7 %copy-start.8 = (f32[512]{0:T(512)S(1)}, f32[512]{0:T(512)}, u32[]{:S(2)}) copy-start(f32[512]{0:T(512)} %param.19) | copy-start | bytes 6148
  12.7 13.5 %collective-permute-start.1 = (bf16[13,24,512]{2,1,0:T(8,128)(2,1)S(1)}, bf16[13,24,512]{2,1,0:T(8,128)(2,1)S(1)}, u32[]{:S(2)}, u32[]{:S(2)}) collective-permute-start(bf16[13,24,512]{2,1,0:T(8,128)(2,1)S(1)} %fusion.2), channel_id=1, source_target_pairs={{0,224},{1,225},{2,226},{3,227},{4,228},{5,229},{6,230},{7,231},{8... | collective-permute-start | bytes 958472 | tf_op jit(solution)/shard_map/ppermute | solution.py:435
  18.0 8.2 %collective-permute-start.2 = (bf16[3,24,512]{2,1,0:T(8,128)(2,1)S(1)}, bf16[3,24,512]{2,1,0:T(8,128)(2,1)S(1)}, u32[]{:S(2)}, u32[]{:S(2)}) collective-permute-start(bf16[3,24,512]{2,1,0:T(8,128)(2,1)S(1)} %pad_maximum_fusion.4), channel_id=1, source_target_pairs={{0,32},{1,33},{2,34},{3,35},{4,36},{5,37},{6,38},{7,39},{8,40},{9,... | collective-permute-start | bytes 221192 | tf_op jit(solution)/shard_map/ppermute | solution.py:435
  23.9 4.2 %copy-start.11 = (f32[3,8,72,256]{3,2,1,0:T(8,128)}, f32[3,8,72,256]{3,2,1,0:T(8,128)S(1)}, u32[]{:S(2)}) copy-start(f32[3,8,72,256]{3,2,1,0:T(8,128)S(1)} %get-tuple-element.34.probs_hbm) | copy-start | bytes 5308420
  23.9 4.2 %copy-start.12 = (bf16[480,1536]{1,0:T(8,128)(2,1)}, bf16[480,1536]{1,0:T(8,128)(2,1)S(1)}, u32[]{:S(2)}) copy-start(bf16[480,1536]{1,0:T(8,128)(2,1)S(1)} %get-tuple-element.33.qkv_hbm) | copy-start | bytes 4423684
  23.9 4.2 %copy-start.13 = (bf16[480,512]{1,0:T(8,128)(2,1)}, bf16[480,512]{1,0:T(8,128)(2,1)S(1)}, u32[]{:S(2)}) copy-start(bf16[480,512]{1,0:T(8,128)(2,1)S(1)} %get-tuple-element.32.normed_hbm) | copy-start | bytes 1474564
  48.4 3.2 %collective-permute-start.3 = (bf16[16,16,2048]{2,1,0:T(8,128)(2,1)}, bf16[16,16,2048]{2,1,0:T(8,128)(2,1)S(1)}, u32[]{:S(2)}, u32[]{:S(2)}) collective-permute-start(bf16[16,16,2048]{2,1,0:T(8,128)(2,1)} %get-tuple-element.38), channel_id=1, source_target_pairs={{0,1},{1,0},{2,3},{3,2},{4,5},{5,4},{6,7},{7,6},{8,9},{9,8},{10,11... | collective-permute-start | bytes 3145736 | tf_op jit(solution)/shard_map/ppermute | solution.py:456
  51.6 8.3 %copy-start.1 = (bf16[18,24,512]{2,1,0:T(8,128)(2,1)S(1)}, bf16[18,24,512]{2,1,0:T(8,128)(2,1)}, u32[]{:S(2)}) copy-start(bf16[18,24,512]{2,1,0:T(8,128)(2,1)} %fusion.1) | copy-start | bytes 1327108
  54.3 5.7 %copy-start = (bf16[640,1536]{1,0:T(8,128)(2,1)S(1)}, bf16[640,1536]{1,0:T(8,128)(2,1)}, u32[]{:S(2)}) copy-start(bf16[640,1536]{1,0:T(8,128)(2,1)} %get-tuple-element.42.dqkv_ref) | copy-start | bytes 5898244
  54.3 5.7 %copy-start.6 = (bf16[160,144]{1,0:T(8,128)(2,1)S(1)}, bf16[160,144]{1,0:T(8,128)(2,1)}, u32[]{:S(2)}) copy-start(bf16[160,144]{1,0:T(8,128)(2,1)} %constant.16.clone.px_ref) | copy-start | bytes 138244
  54.3 5.7 %copy-start.9 = (f32[512]{0:T(512)S(1)}, f32[512]{0:T(512)}, u32[]{:S(2)}) copy-start(f32[512]{0:T(512)} %param.19) | copy-start | bytes 6148
  54.3 34.3 %all-to-all-start = ((bf16[16,16,2048]{2,1,0:T(8,128)(2,1)}), bf16[16,16,2048]{2,1,0:T(8,128)(2,1)}, u32[]{:S(2)}, u32[]{:S(2)}) async-start(bf16[16,16,2048]{2,1,0:T(8,128)(2,1)} %add.3), calls=%async_computation | async-start | bytes 2097152 | tf_op jit(solution)/shard_map/all_to_all | solution.py:458
  60.0 1.4 %copy-start.3 = (bf16[512,1536]{1,0:T(8,128)(2,1)S(1)}, bf16[512,1536]{1,0:T(8,128)(2,1)}, u32[]{:S(2)}) copy-start(bf16[512,1536]{1,0:T(8,128)(2,1)} %wqkv_ref.1) | copy-start | bytes 4718596
  61.4 1.1 %copy-start.4 = (bf16[640,512]{1,0:T(8,128)(2,1)S(1)}, bf16[640,512]{1,0:T(8,128)(2,1)}, u32[]{:S(2)}) copy-start(bf16[640,512]{1,0:T(8,128)(2,1)} %get-tuple-element.41.gn_ref) | copy-start | bytes 1966084
  66.5 22.0 %collective-permute-start.4 = (bf16[3,18,512]{2,1,0:T(8,128)(2,1)S(1)}, bf16[3,18,512]{2,1,0:T(8,128)(2,1)S(1)}, u32[]{:S(2)}, u32[]{:S(2)}) collective-permute-start(bf16[3,18,512]{2,1,0:T(8,128)(2,1)S(1)} %slice.83), channel_id=1, source_target_pairs={{0,32},{1,33},{2,34},{3,35},{4,36},{5,37},{6,38},{7,39},{8,40},{9,... | collective-permute-start | bytes 165896 | tf_op jit(solution)/shard_map/ppermute | solution.py:435
  69.3 19.2 %collective-permute-start.5 = (bf16[3,6,512]{2,1,0:T(8,128)(2,1)S(1)}, bf16[3,6,512]{2,1,0:T(8,128)(2,1)S(1)}, u32[]{:S(2)}, u32[]{:S(2)}) collective-permute-start(bf16[3,6,512]{2,1,0:T(8,128)(2,1)S(1)} %slice.84), channel_id=1, source_target_pairs={{0,33},{1,34},{2,35},{3,36},{4,37},{5,38},{6,39},{7,40},{8,41},{9,... | collective-permute-start | bytes 55304 | tf_op jit(solution)/shard_map/ppermute | solution.py:435
  90.8 16.3 %all-to-all-start.1 = ((bf16[8,16,2048]{2,1,0:T(8,128)(2,1)}), bf16[8,16,2048]{2,1,0:T(8,128)(2,1)S(1)}, u32[]{:S(2)}, u32[]{:S(2)}) async-start(bf16[8,16,2048]{2,1,0:T(8,128)(2,1)} %broadcast_in_dim.20), calls=%async_computation.1 | async-start | bytes 1048576 | tf_op jit(solution)/shard_map/all_to_all | solution.py:473
  95.0 6.9 %collective-permute-start.6 = (bf16[21,6,512]{2,1,0:T(8,128)(2,1)S(1)}, bf16[21,6,512]{2,1,0:T(8,128)(2,1)S(1)}, u32[]{:S(2)}, u32[]{:S(2)}) collective-permute-start(bf16[21,6,512]{2,1,0:T(8,128)(2,1)S(1)} %slice.85), channel_id=1, source_target_pairs={{0,1},{1,2},{2,3},{3,4},{4,5},{5,6},{6,7},{7,8},{8,9},{9,10},{10,1... | collective-permute-start | bytes 387080 | tf_op jit(solution)/shard_map/ppermute | solution.py:435
  (3 other events, 2.5 us)

commit v4 on v3

--- a/solution.py
+++ b/solution.py
@@ -28,7 +28,7 @@
 QROWS = 160
 
 EPSILON = 1e-05
-GRANT = 63 * 1024 * 1024
+GRANT = 40 * 1024 * 1024
 SMALL_GRANT = 24 * 1024 * 1024
 MASKED = -1000000000.0
 OUTSIDE = -3.0e38

time: 109 us -> 106 us (0.972)
  other arithmetic: 8.41 us -> 5.5 us
  waiting for transfers between devices: 40.2 us -> 41.5 us
    ppermute x6, waiting for transfers between devices: 33.3 us -> 34.8 us  [moved(): return lax.ppermute(value, names, pairs)]
    add x1, other arithmetic: 2.64 us -> 1.37 us  [body(): pair, dqkv = lax.optimization_barrier((mine + theirs, dqkv))]
    unnamed x36 -> x32, local copies, waits for them, and re-layouts: 5.01 us -> 4.5 us
  transfers between devices with their start and end apart: 9 -> 9, of which waited for: 6 -> 6; matrix products, arithmetic and copies ran while one was open for 1% -> 1% of each run, Pallas kernels for 6% -> 7%
where the time goes in v4:
time: 106 us; the launch traced here: 105 us
  waiting for transfers between devices  41.5 us (39%)
  Pallas kernels  26.5 us (25%)
  starting transfers between devices  23.1 us (22%)
  local copies, waits for them, and re-layouts  7.79 us (7%)
  other arithmetic  5.5 us (5%)
    ppermute x6, waiting for transfers between devices, moved(): return lax.ppermute(value, names, pairs)  34.8 us
    pallas_call x1, Pallas kernels, compute(): pl.pallas_call(functools.partial(kernel, lats), out_shape=tuple((jax.Shap...  19.4 us
    ppermute x6, starting transfers between devices, moved(): return lax.ppermute(value, names, pairs)  12.8 us
    all_to_all x1, starting transfers between devices, body(): spread = lax.all_to_all(pair, 'tile', 0, 0, tiled=True)  5.92 us
    unnamed x32, local copies, waits for them, and re-layouts  4.5 us
    all_to_all x1, starting transfers between devices, body(): gathered = lax.all_to_all(copies, 'lat', 0, 0, tiled=True)  4.26 us
    all_to_all x1, waiting for transfers between devices, body(): gathered = lax.all_to_all(copies, 'lat', 0, 0, tiled=True)  4.06 us
    pallas_call x1, Pallas kernels, start_early(): pl.pallas_call(early_kernel, out_shape=tuple((jax.ShapeDtypeStruct(*one)...  4.01 us
  transfers between devices with their start and end apart: 9, of which 6 were waited for; matrix products, arithmetic and copies ran while one was open for 1% of the time, Pallas kernels for 7%

profile of v4, /device:TPU:0, one launch (start us, length us, event | category | flops | bytes accessed | tf_op | source)
XLA Modules:
  0.0 105.3 jit_solution(3735872393966244806)
XLA Ops:
  0.7 1.0 slice.59
  1.7 0.9 slice.60
  2.7 4.6 %collective-permute-start = (bf16[48,6,512]{2,1,0:T(8,128)(2,1)S(1)}, bf16[48,6,512]{2,1,0:T(8,128)(2,1)S(1)}, u32[]{:S(2)}, u32[]{:S(2)}) collective-permute-start(bf16[48,6,512]{2,1,0:T(8,128)(2,1)S(1)} %pad_maximum_fusion.2), channel_id=1, source_target_pairs={{0,31},{1,0},{2,1},{3,2},{4,3},{5,4},{6,5},{7,6},{8,7},{9,8},{10,9... | collective-permute-start | bytes 884744 | tf_op jit(solution)/shard_map/ppermute | solution.py:435
  7.6 5.0 %collective-permute-done = bf16[48,6,512]{2,1,0:T(8,128)(2,1)S(1)} collective-permute-done((bf16[48,6,512]{2,1,0:T(8,128)(2,1)S(1)}, bf16[48,6,512]{2,1,0:T(8,128)(2,1)S(1)}, u32[]{:S(2)}, u32[]{:S(2)}) %collective-permute-start) | collective-permute-done | bytes 294944 | tf_op jit(solution)/shard_map/ppermute | solution.py:435
  12.7 5.3 %collective-permute-start.1 = (bf16[13,24,512]{2,1,0:T(8,128)(2,1)S(1)}, bf16[13,24,512]{2,1,0:T(8,128)(2,1)S(1)}, u32[]{:S(2)}, u32[]{:S(2)}) collective-permute-start(bf16[13,24,512]{2,1,0:T(8,128)(2,1)S(1)} %fusion.2), channel_id=1, source_target_pairs={{0,224},{1,225},{2,226},{3,227},{4,228},{5,229},{6,230},{7,231},{8... | collective-permute-start | bytes 958472 | tf_op jit(solution)/shard_map/ppermute | solution.py:435
  18.2 4.0 %block_early.1 = (bf16[480,512]{1,0:T(8,128)(2,1)S(1)}, bf16[480,1536]{1,0:T(8,128)(2,1)S(1)}, f32[3,8,72,256]{3,2,1,0:T(8,128)S(1)}, bf16[480,512]{1,0:T(8,128)(2,1)S(1)}, bf16[480,512]{1,0:T(8,128)(2,1)S(1)}) custom-call(bf16[432,512]{1,0:T(8,128)(2,1)S(1)} %bitcast.11, bf16[160,144]{1,0:T(8,128)(2,1)S(1)} %copy-done.4, f32[1,512]{1,0:T(1,128)S(1)} %bitcast.16, ...), custom_call_target="tpu_custom_call" | custom-call | flops 1400000000 | bytes 8000000 | tf_op jit(solution)/shard_map/block_early/pallas_call | solution.py:371
  22.3 3.8 %collective-permute-done.2 = bf16[3,24,512]{2,1,0:T(8,128)(2,1)S(1)} collective-permute-done((bf16[3,24,512]{2,1,0:T(8,128)(2,1)S(1)}, bf16[3,24,512]{2,1,0:T(8,128)(2,1)S(1)}, u32[]{:S(2)}, u32[]{:S(2)}) %collective-permute-start.2) | collective-permute-done | bytes 73760 | tf_op jit(solution)/shard_map/ppermute | solution.py:435
  27.4 19.4 %block.1 = (bf16[16,16,2048]{2,1,0:T(8,128)(2,1)S(1)}, bf16[16,16,2048]{2,1,0:T(8,128)(2,1)S(1)}, bf16[640,512]{1,0:T(8,128)(2,1)S(1)}, bf16[640,1536]{1,0:T(8,128)(2,1)S(1)}) custom-call(bf16[432,512]{1,0:T(8,128)(2,1)S(1)} %bitcast.13, bf16[672,512]{1,0:T(8,128)(2,1)S(1)} %bitcast.15, f32[1,512]{1,0:T(1,128)S(1)} %bitcast.17, f32[1,2048]{1,0:T(1,128)S(1)} %bitcast.19, ...), custom_call_target="tpu_custom_call" | custom-call | flops 7000000000 | bytes 18000000 | tf_op jit(solution)/shard_map/block/pallas_call | solution.py:386
  46.9 2.6 %collective-permute-done.3 = bf16[16,16,2048]{2,1,0:T(8,128)(2,1)S(1)} collective-permute-done((bf16[16,16,2048]{2,1,0:T(8,128)(2,1)S(1)}, bf16[16,16,2048]{2,1,0:T(8,128)(2,1)S(1)}, u32[]{:S(2)}, u32[]{:S(2)}) %collective-permute-start.3) | collective-permute-done | bytes 1048608 | tf_op jit(solution)/shard_map/ppermute | solution.py:456
  49.6 1.4 %add.3 = bf16[16,16,2048]{2,1,0:T(8,128)(2,1)} add(bf16[16,16,2048]{2,1,0:T(8,128)(2,1)S(1)} %get-tuple-element.37, bf16[16,16,2048]{2,1,0:T(8,128)(2,1)S(1)} %collective-permute-done.3) | non-fusion elementwise | flops 524288 | bytes 3145728 | tf_op jit(solution)/shard_map/add | solution.py:457
  50.9 5.9 %all-to-all-start = ((bf16[16,16,2048]{2,1,0:T(8,128)(2,1)}), bf16[16,16,2048]{2,1,0:T(8,128)(2,1)}, u32[]{:S(2)}, u32[]{:S(2)}) async-start(bf16[16,16,2048]{2,1,0:T(8,128)(2,1)} %add.3), calls=%async_computation | async-start | bytes 2097152 | tf_op jit(solution)/shard_map/all_to_all | solution.py:458
  56.9 1.4 %copy-done.1 = bf16[512,1536]{1,0:T(8,128)(2,1)S(1)} copy-done((bf16[512,1536]{1,0:T(8,128)(2,1)S(1)}, bf16[512,1536]{1,0:T(8,128)(2,1)}, u32[]{:S(2)}) %copy-start.1) | copy-done | bytes 1572888
  58.3 1.1 %copy-done.3 = bf16[640,512]{1,0:T(8,128)(2,1)S(1)} copy-done((bf16[640,512]{1,0:T(8,128)(2,1)S(1)}, bf16[640,512]{1,0:T(8,128)(2,1)}, u32[]{:S(2)}) %copy-start.3) | copy-done | bytes 655384
  59.4 0.9 copy-done.5
  60.2 3.1 %block_tokens.1 = bf16[576,512]{1,0:T(8,128)(2,1)S(1)} custom-call(bf16[432,512]{1,0:T(8,128)(2,1)S(1)} %bitcast.12, bf16[432,512]{1,0:T(8,128)(2,1)S(1)} %bitcast.14, bf16[640,512]{1,0:T(8,128)(2,1)S(1)} %copy-done.3, bf16[640,1536]{1,0:T(8,128)(2,1)S(1)} %get-tuple-element.42.dqkv_ref, bf16[512,1536]{1,0:T(8,128)(2,1)S(1)} %copy-done.1, ...), custom_call_target="tpu_custom_call" | custom-call | flops 1200000000 | bytes 6000000 | tf_op jit(solution)/shard_map/block_tokens/pallas_call | solution.py:413
  63.4 2.8 %collective-permute-start.4 = (bf16[3,18,512]{2,1,0:T(8,128)(2,1)S(1)}, bf16[3,18,512]{2,1,0:T(8,128)(2,1)S(1)}, u32[]{:S(2)}, u32[]{:S(2)}) collective-permute-start(bf16[3,18,512]{2,1,0:T(8,128)(2,1)S(1)} %slice.83), channel_id=1, source_target_pairs={{0,32},{1,33},{2,34},{3,35},{4,36},{5,37},{6,38},{7,39},{8,40},{9,... | collective-permute-start | bytes 165896 | tf_op jit(solution)/shard_map/ppermute | solution.py:435
  66.4 19.1 %collective-permute-done.5 = bf16[3,6,512]{2,1,0:T(8,128)(2,1)S(1)} collective-permute-done((bf16[3,6,512]{2,1,0:T(8,128)(2,1)S(1)}, bf16[3,6,512]{2,1,0:T(8,128)(2,1)S(1)}, u32[]{:S(2)}, u32[]{:S(2)}) %collective-permute-start.5) | collective-permute-done | bytes 18464 | tf_op jit(solution)/shard_map/ppermute | solution.py:435
  85.5 1.4 %reduce_sum.30 = bf16[16,2048]{1,0:T(8,128)(2,1)S(1)} reduce(bf16[16,16,2048]{2,1,0:T(8,128)(2,1)} %all-to-all-done, bf16[]{:T(256)} %constant.14.clone.1), dimensions={0}, to_apply=%region_0.0 | reduce | flops 491520 | bytes 1114114 | tf_op jit(solution)/shard_map/reduce_sum | solution.py:471
  86.9 0.9 broadcast_in_dim.20
  87.7 4.3 %all-to-all-start.1 = ((bf16[8,16,2048]{2,1,0:T(8,128)(2,1)}), bf16[8,16,2048]{2,1,0:T(8,128)(2,1)S(1)}, u32[]{:S(2)}, u32[]{:S(2)}) async-start(bf16[8,16,2048]{2,1,0:T(8,128)(2,1)} %broadcast_in_dim.20), calls=%async_computation.1 | async-start | bytes 1048576 | tf_op jit(solution)/shard_map/all_to_all | solution.py:473
  92.0 6.9 %collective-permute-done.6 = bf16[21,6,512]{2,1,0:T(8,128)(2,1)S(1)} collective-permute-done((bf16[21,6,512]{2,1,0:T(8,128)(2,1)S(1)}, bf16[21,6,512]{2,1,0:T(8,128)(2,1)S(1)}, u32[]{:S(2)}, u32[]{:S(2)}) %collective-permute-start.6) | collective-permute-done | bytes 129056 | tf_op jit(solution)/shard_map/ppermute | solution.py:435
  98.9 1.0 maximum_maximum_fusion
  100.0 4.1 %all-to-all-done.1 = bf16[8,16,2048]{2,1,0:T(8,128)(2,1)S(1)} async-done(((bf16[8,16,2048]{2,1,0:T(8,128)(2,1)}), bf16[8,16,2048]{2,1,0:T(8,128)(2,1)S(1)}, u32[]{:S(2)}, u32[]{:S(2)}) %all-to-all-start.1) | async-done | bytes 524320 | tf_op jit(solution)/shard_map/all_to_all | solution.py:473
  104.7 0.7 convert_reduce_fusion
  (53 shorter events, 2.9 us)
Async XLA Ops:
  0.6 6.7 %copy-start.14 = (bf16[24,24,512]{2,1,0:T(8,128)(2,1)S(1)}, bf16[24,24,512]{2,1,0:T(8,128)(2,1)}, u32[]{:S(2)}) copy-start(bf16[24,24,512]{2,1,0:T(8,128)(2,1)} %param.17) | copy-start | bytes 1769476
  0.6 6.8 %copy-start.15 = (bf16[24,24,512]{2,1,0:T(8,128)(2,1)S(1)}, bf16[24,24,512]{2,1,0:T(8,128)(2,1)}, u32[]{:S(2)}) copy-start(bf16[24,24,512]{2,1,0:T(8,128)(2,1)} %param.18) | copy-start | bytes 1769476
  2.7 9.9 %collective-permute-start = (bf16[48,6,512]{2,1,0:T(8,128)(2,1)S(1)}, bf16[48,6,512]{2,1,0:T(8,128)(2,1)S(1)}, u32[]{:S(2)}, u32[]{:S(2)}) collective-permute-start(bf16[48,6,512]{2,1,0:T(8,128)(2,1)S(1)} %pad_maximum_fusion.2), channel_id=1, source_target_pairs={{0,31},{1,0},{2,1},{3,2},{4,3},{5,4},{6,5},{7,6},{8,7},{9,8},{10,9... | collective-permute-start | bytes 884744 | tf_op jit(solution)/shard_map/ppermute | solution.py:435
  12.7 5.5 %copy-start.7 = (bf16[512,512]{1,0:T(8,128)(2,1)S(1)}, bf16[512,512]{1,0:T(8,128)(2,1)}, u32[]{:S(2)}) copy-start(bf16[512,512]{1,0:T(8,128)(2,1)} %wproj_hbm.1) | copy-start | bytes 1572868
  12.7 5.5 %copy-start = (bf16[512,1536]{1,0:T(8,128)(2,1)S(1)}, bf16[512,1536]{1,0:T(8,128)(2,1)}, u32[]{:S(2)}) copy-start(bf16[512,1536]{1,0:T(8,128)(2,1)} %wqkv_ref.1) | copy-start | bytes 4718596
  12.7 5.5 %copy-start.4 = (bf16[160,144]{1,0:T(8,128)(2,1)S(1)}, bf16[160,144]{1,0:T(8,128)(2,1)}, u32[]{:S(2)}) copy-start(bf16[160,144]{1,0:T(8,128)(2,1)} %constant.16.clone.px_ref) | copy-start | bytes 138244
  12.7 5.5 %copy-start.6 = (f32[512]{0:T(512)S(1)}, f32[512]{0:T(512)}, u32[]{:S(2)}) copy-start(f32[512]{0:T(512)} %param.19) | copy-start | bytes 6148
  12.7 13.3 %collective-permute-start.1 = (bf16[13,24,512]{2,1,0:T(8,128)(2,1)S(1)}, bf16[13,24,512]{2,1,0:T(8,128)(2,1)S(1)}, u32[]{:S(2)}, u32[]{:S(2)}) collective-permute-start(bf16[13,24,512]{2,1,0:T(8,128)(2,1)S(1)} %fusion.2), channel_id=1, source_target_pairs={{0,224},{1,225},{2,226},{3,227},{4,228},{5,229},{6,230},{7,231},{8... | collective-permute-start | bytes 958472 | tf_op jit(solution)/shard_map/ppermute | solution.py:435
  18.0 8.0 %collective-permute-start.2 = (bf16[3,24,512]{2,1,0:T(8,128)(2,1)S(1)}, bf16[3,24,512]{2,1,0:T(8,128)(2,1)S(1)}, u32[]{:S(2)}, u32[]{:S(2)}) collective-permute-start(bf16[3,24,512]{2,1,0:T(8,128)(2,1)S(1)} %pad_maximum_fusion.4), channel_id=1, source_target_pairs={{0,32},{1,33},{2,34},{3,35},{4,36},{5,37},{6,38},{7,39},{8,40},{9,... | collective-permute-start | bytes 221192 | tf_op jit(solution)/shard_map/ppermute | solution.py:435
  26.1 0.7 copy-start.8
  26.1 1.2 %copy-start.10 = (bf16[9,192,160]{2,1,0:T(8,128)(2,1)S(1)}, bf16[9,192,160]{2,1,0:T(8,128)(2,1)}, u32[]{:S(2)}) copy-start(bf16[9,192,160]{2,1,0:T(8,128)(2,1)} %constant.17.clone.pf_ref) | copy-start | bytes 1658884
  26.1 1.2 %copy-start.11 = (bf16[4,160,256]{2,1,0:T(8,128)(2,1)S(1)}, bf16[4,160,256]{2,1,0:T(8,128)(2,1)}, u32[]{:S(2)}) copy-start(bf16[4,160,256]{2,1,0:T(8,128)(2,1)} %constant.20.clone.pi_ref) | copy-start | bytes 983044
  26.2 1.2 %copy-start.12 = (bf16[192,192]{1,0:T(8,128)(2,1)S(1)}, bf16[192,192]{1,0:T(8,128)(2,1)}, u32[]{:S(2)}) copy-start(bf16[192,192]{1,0:T(8,128)(2,1)} %constant.18.clone.pc_ref) | copy-start | bytes 221188
  26.2 1.2 %copy-start.13 = (bf16[64,48]{1,0:T(8,128)(2,1)S(1)}, bf16[64,48]{1,0:T(8,128)(2,1)}, u32[]{:S(2)}) copy-start(bf16[64,48]{1,0:T(8,128)(2,1)} %constant.19.clone.pc3_ref) | copy-start | bytes 18436
  46.8 4.1 %copy-start.2 = (bf16[640,512]{1,0:T(8,128)(2,1)}, bf16[640,512]{1,0:T(8,128)(2,1)S(1)}, u32[]{:S(2)}) copy-start(bf16[640,512]{1,0:T(8,128)(2,1)S(1)} %get-tuple-element.41.gn_ref) | copy-start | bytes 1966084
  46.8 2.7 %collective-permute-start.3 = (bf16[16,16,2048]{2,1,0:T(8,128)(2,1)S(1)}, bf16[16,16,2048]{2,1,0:T(8,128)(2,1)S(1)}, u32[]{:S(2)}, u32[]{:S(2)}) collective-permute-start(bf16[16,16,2048]{2,1,0:T(8,128)(2,1)S(1)} %get-tuple-element.38), channel_id=1, source_target_pairs={{0,1},{1,0},{2,3},{3,2},{4,5},{5,4},{6,7},{7,6},{8,9},{9,8},{10,11... | collective-permute-start | bytes 3145736 | tf_op jit(solution)/shard_map/ppermute | solution.py:456
  50.9 34.6 %all-to-all-start = ((bf16[16,16,2048]{2,1,0:T(8,128)(2,1)}), bf16[16,16,2048]{2,1,0:T(8,128)(2,1)}, u32[]{:S(2)}, u32[]{:S(2)}) async-start(bf16[16,16,2048]{2,1,0:T(8,128)(2,1)} %add.3), calls=%async_computation | async-start | bytes 2097152 | tf_op jit(solution)/shard_map/all_to_all | solution.py:458
  56.9 1.4 %copy-start.1 = (bf16[512,1536]{1,0:T(8,128)(2,1)S(1)}, bf16[512,1536]{1,0:T(8,128)(2,1)}, u32[]{:S(2)}) copy-start(bf16[512,1536]{1,0:T(8,128)(2,1)} %wqkv_ref.1) | copy-start | bytes 4718596
  58.3 1.1 %copy-start.3 = (bf16[640,512]{1,0:T(8,128)(2,1)S(1)}, bf16[640,512]{1,0:T(8,128)(2,1)}, u32[]{:S(2)}) copy-start(bf16[640,512]{1,0:T(8,128)(2,1)} %copy-done.2) | copy-start | bytes 1966084
  59.4 0.9 copy-start.5
  63.4 22.1 %collective-permute-start.4 = (bf16[3,18,512]{2,1,0:T(8,128)(2,1)S(1)}, bf16[3,18,512]{2,1,0:T(8,128)(2,1)S(1)}, u32[]{:S(2)}, u32[]{:S(2)}) collective-permute-start(bf16[3,18,512]{2,1,0:T(8,128)(2,1)S(1)} %slice.83), channel_id=1, source_target_pairs={{0,32},{1,33},{2,34},{3,35},{4,36},{5,37},{6,38},{7,39},{8,40},{9,... | collective-permute-start | bytes 165896 | tf_op jit(solution)/shard_map/ppermute | solution.py:435
  66.2 19.2 %collective-permute-start.5 = (bf16[3,6,512]{2,1,0:T(8,128)(2,1)S(1)}, bf16[3,6,512]{2,1,0:T(8,128)(2,1)S(1)}, u32[]{:S(2)}, u32[]{:S(2)}) collective-permute-start(bf16[3,6,512]{2,1,0:T(8,128)(2,1)S(1)} %slice.84), channel_id=1, source_target_pairs={{0,33},{1,34},{2,35},{3,36},{4,37},{5,38},{6,39},{7,40},{8,41},{9,... | collective-permute-start | bytes 55304 | tf_op jit(solution)/shard_map/ppermute | solution.py:435
  87.7 16.3 %all-to-all-start.1 = ((bf16[8,16,2048]{2,1,0:T(8,128)(2,1)}), bf16[8,16,2048]{2,1,0:T(8,128)(2,1)S(1)}, u32[]{:S(2)}, u32[]{:S(2)}) async-start(bf16[8,16,2048]{2,1,0:T(8,128)(2,1)} %broadcast_in_dim.20), calls=%async_computation.1 | async-start | bytes 1048576 | tf_op jit(solution)/shard_map/all_to_all | solution.py:473
  92.0 6.9 %collective-permute-start.6 = (bf16[21,6,512]{2,1,0:T(8,128)(2,1)S(1)}, bf16[21,6,512]{2,1,0:T(8,128)(2,1)S(1)}, u32[]{:S(2)}, u32[]{:S(2)}) collective-permute-start(bf16[21,6,512]{2,1,0:T(8,128)(2,1)S(1)} %slice.85), channel_id=1, source_target_pairs={{0,1},{1,2},{2,3},{3,4},{4,5},{5,6},{6,7},{7,8},{8,9},{9,10},{10,1... | collective-permute-start | bytes 387080 | tf_op jit(solution)/shard_map/ppermute | solution.py:435
  (1 other events, 0.7 us)

commit v5 on v4

--- a/solution.py
+++ b/solution.py
@@ -422,6 +422,27 @@
     )(x_early, x, gn, dqkv, w_qkv, norm_gain[None], jnp.asarray(to_windows()), jnp.asarray(to_windows().T))
 
 
+def copies_kernel(in_ref, out_ref):
+    for j in range(in_ref.shape[2] // D):
+        columns = slice(D * j, D * j + D)
+        total = in_ref[0, :, columns].astype(F32)
+        for i in range(1, in_ref.shape[0]):
+            total = total + in_ref[i, :, columns].astype(F32)
+        for i in range(out_ref.shape[0]):
+            out_ref[i, :, columns] = total.astype(BF)
+
+
+def share_copies(spread, copies):
+    return pl.pallas_call(
+        copies_kernel,
+        out_shape=jax.ShapeDtypeStruct((copies,) + spread.shape[1:], BF),
+        in_specs=[VMEM],
+        out_specs=VMEM,
+        compiler_params=pltpu.CompilerParams(vmem_limit_bytes=SMALL_GRANT),
+        name="share_copies",
+    )(spread)
+
+
 def body(tokens, cotangent, norm_gain, w_qkv, w_proj, merge_gain, w_merge, w_expand, expand_gain):
     lats, tiles, cores = lax.axis_size("lat"), lax.axis_size("tile"), lax.axis_size("core")
     lons = tiles * cores
@@ -459,18 +480,15 @@
 
     d_work = finish_tokens(x_early, x, gn, dqkv, w_qkv, norm_gain).reshape(ROWS, COLS, D)
     last_row, last_col = ROWS - SLAT, COLS - SLON
+    spread, d_work = lax.optimization_barrier((spread, d_work))
     rows = moved(d_work[last_row:, :last_col], 1, 0)
     corner = moved(d_work[last_row:, last_col:], 1, 1)
-    edge = d_work[:last_row, last_col:]
-    spread, rows, corner, edge = lax.optimization_barrier((spread, rows, corner, edge))
-    columns = moved(edge, 0, 1)
+    columns = moved(d_work[:last_row, last_col:], 0, 1)
     top = jnp.concatenate([corner, rows], axis=1)
     rest = jnp.concatenate([columns, d_work[:last_row, :last_col]], axis=1)
     d_tokens = jnp.concatenate([top, rest], axis=0)
 
-    share = jnp.sum(spread.astype(F32), axis=0).astype(BF)
-    copies = jnp.broadcast_to(share[None], (lats,) + share.shape)
-    gathered = lax.all_to_all(copies, "lat", 0, 0, tiled=True)
+    gathered = lax.all_to_all(share_copies(spread, lats), "lat", 0, 0, tiled=True)
     grad_qkv = jnp.sum(gathered[:, :, : 3 * D].astype(F32), axis=0)
     grad_proj = jnp.sum(gathered[:, :, 3 * D :].astype(F32), axis=0)
     return (d_tokens, grad_qkv, grad_proj)

time: 106 us -> 110 us (1.038)
  the two profiles are of different devices: /device:TPU:0 before, /device:TPU:1 now
where the time goes in v5:
time: 110 us
  waiting for transfers between devices  37.9 us (34%)
  starting transfers between devices  32.8 us (30%)
  Pallas kernels  27.5 us (25%)
  local copies, waits for them, and re-layouts  6.51 us (6%)
  other arithmetic  4.12 us (4%)
    pallas_call x1, Pallas kernels, compute(): pl.pallas_call(functools.partial(kernel, lats), out_shape=tuple((jax.Shap...  19.4 us
    all_to_all x1, waiting for transfers between devices, body(): spread = lax.all_to_all(pair, 'tile', 0, 0, tiled=True)  19.4 us
    ppermute x6, starting transfers between devices, moved(): return lax.ppermute(value, names, pairs)  17.2 us
    ppermute x6, waiting for transfers between devices, moved(): return lax.ppermute(value, names, pairs)  16.2 us
    all_to_all x1, starting transfers between devices, body(): spread = lax.all_to_all(pair, 'tile', 0, 0, tiled=True)  5.74 us
    ppermute x1, starting transfers between devices, body(): lax.ppermute(other, 'core', [(i, cores - 1 - i) for i in range(cores)])  5.01 us
    all_to_all x1, starting transfers between devices, body(): lax.all_to_all(share_copies(spread, lats), 'lat', 0, 0, tiled=True)  4.85 us
    unnamed x32, local copies, waits for them, and re-layouts  4.07 us
  transfers between devices with their start and end apart: 9, of which 5 were waited for; matrix products, arithmetic and copies ran while one was open for 1% of the time, Pallas kernels for 7%

profile of v5, /device:TPU:1, one launch (start us, length us, event | category | flops | bytes accessed | tf_op | source)
XLA Modules:
  0.0 109.7 jit_solution(17323887311361500294)
XLA Ops:
  0.7 1.0 slice.59
  1.7 0.9 slice.60
  2.7 3.3 %collective-permute-start = (bf16[48,6,512]{2,1,0:T(8,128)(2,1)S(1)}, bf16[48,6,512]{2,1,0:T(8,128)(2,1)S(1)}, u32[]{:S(2)}, u32[]{:S(2)}) collective-permute-start(bf16[48,6,512]{2,1,0:T(8,128)(2,1)S(1)} %pad_maximum_fusion.2), channel_id=1, source_target_pairs={{0,31},{1,0},{2,1},{3,2},{4,3},{5,4},{6,5},{7,6},{8,7},{9,8},{10,9... | collective-permute-start | bytes 884744 | tf_op jit(solution)/shard_map/ppermute | solution.py:456
  6.4 4.9 %collective-permute-done = bf16[48,6,512]{2,1,0:T(8,128)(2,1)S(1)} collective-permute-done((bf16[48,6,512]{2,1,0:T(8,128)(2,1)S(1)}, bf16[48,6,512]{2,1,0:T(8,128)(2,1)S(1)}, u32[]{:S(2)}, u32[]{:S(2)}) %collective-permute-start) | collective-permute-done | bytes 294944 | tf_op jit(solution)/shard_map/ppermute | solution.py:456
  11.5 5.3 %collective-permute-start.1 = (bf16[13,24,512]{2,1,0:T(8,128)(2,1)S(1)}, bf16[13,24,512]{2,1,0:T(8,128)(2,1)S(1)}, u32[]{:S(2)}, u32[]{:S(2)}) collective-permute-start(bf16[13,24,512]{2,1,0:T(8,128)(2,1)S(1)} %fusion.2), channel_id=1, source_target_pairs={{0,224},{1,225},{2,226},{3,227},{4,228},{5,229},{6,230},{7,231},{8... | collective-permute-start | bytes 958472 | tf_op jit(solution)/shard_map/ppermute | solution.py:456
  17.0 4.0 %block_early.1 = (bf16[480,512]{1,0:T(8,128)(2,1)S(1)}, bf16[480,1536]{1,0:T(8,128)(2,1)S(1)}, f32[3,8,72,256]{3,2,1,0:T(8,128)S(1)}, bf16[480,512]{1,0:T(8,128)(2,1)S(1)}, bf16[480,512]{1,0:T(8,128)(2,1)S(1)}) custom-call(bf16[432,512]{1,0:T(8,128)(2,1)S(1)} %bitcast.11, bf16[160,144]{1,0:T(8,128)(2,1)S(1)} %copy-done.4, f32[1,512]{1,0:T(1,128)S(1)} %bitcast.16, ...), custom_call_target="tpu_custom_call" | custom-call | flops 1400000000 | bytes 8000000 | tf_op jit(solution)/shard_map/block_early/pallas_call | solution.py:371
  21.0 3.4 %collective-permute-done.2 = bf16[3,24,512]{2,1,0:T(8,128)(2,1)S(1)} collective-permute-done((bf16[3,24,512]{2,1,0:T(8,128)(2,1)S(1)}, bf16[3,24,512]{2,1,0:T(8,128)(2,1)S(1)}, u32[]{:S(2)}, u32[]{:S(2)}) %collective-permute-start.2) | collective-permute-done | bytes 73760 | tf_op jit(solution)/shard_map/ppermute | solution.py:456
  25.7 19.4 %block.1 = (bf16[16,16,2048]{2,1,0:T(8,128)(2,1)S(1)}, bf16[16,16,2048]{2,1,0:T(8,128)(2,1)S(1)}, bf16[640,512]{1,0:T(8,128)(2,1)S(1)}, bf16[640,1536]{1,0:T(8,128)(2,1)S(1)}) custom-call(bf16[432,512]{1,0:T(8,128)(2,1)S(1)} %bitcast.13, bf16[672,512]{1,0:T(8,128)(2,1)S(1)} %bitcast.15, f32[1,512]{1,0:T(1,128)S(1)} %bitcast.17, f32[1,2048]{1,0:T(1,128)S(1)} %bitcast.19, ...), custom_call_target="tpu_custom_call" | custom-call | flops 7000000000 | bytes 18000000 | tf_op jit(solution)/shard_map/block/pallas_call | solution.py:386
  45.1 5.0 %collective-permute-start.3 = (bf16[16,16,2048]{2,1,0:T(8,128)(2,1)S(1)}, bf16[16,16,2048]{2,1,0:T(8,128)(2,1)S(1)}, u32[]{:S(2)}, u32[]{:S(2)}) collective-permute-start(bf16[16,16,2048]{2,1,0:T(8,128)(2,1)S(1)} %get-tuple-element.36), channel_id=1, source_target_pairs={{0,1},{1,0},{2,3},{3,2},{4,5},{5,4},{6,7},{7,6},{8,9},{9,8},{10,11... | collective-permute-start | bytes 3145736 | tf_op jit(solution)/shard_map/ppermute | solution.py:477
  50.1 2.3 %collective-permute-done.3 = bf16[16,16,2048]{2,1,0:T(8,128)(2,1)S(1)} collective-permute-done((bf16[16,16,2048]{2,1,0:T(8,128)(2,1)S(1)}, bf16[16,16,2048]{2,1,0:T(8,128)(2,1)S(1)}, u32[]{:S(2)}, u32[]{:S(2)}) %collective-permute-start.3) | collective-permute-done | bytes 1048608 | tf_op jit(solution)/shard_map/ppermute | solution.py:477
  52.4 1.4 %add.3 = bf16[16,16,2048]{2,1,0:T(8,128)(2,1)} add(bf16[16,16,2048]{2,1,0:T(8,128)(2,1)S(1)} %get-tuple-element.35, bf16[16,16,2048]{2,1,0:T(8,128)(2,1)S(1)} %collective-permute-done.3) | non-fusion elementwise | flops 524288 | bytes 3145728 | tf_op jit(solution)/shard_map/add | solution.py:478
  53.8 5.7 %all-to-all-start = ((bf16[16,16,2048]{2,1,0:T(8,128)(2,1)}), bf16[16,16,2048]{2,1,0:T(8,128)(2,1)S(1)}, u32[]{:S(2)}, u32[]{:S(2)}) async-start(bf16[16,16,2048]{2,1,0:T(8,128)(2,1)} %add.3), calls=%async_computation | async-start | bytes 2097152 | tf_op jit(solution)/shard_map/all_to_all | solution.py:479
  59.6 1.5 %copy-done.1 = bf16[640,1536]{1,0:T(8,128)(2,1)S(1)} copy-done((bf16[640,1536]{1,0:T(8,128)(2,1)S(1)}, bf16[640,1536]{1,0:T(8,128)(2,1)}, u32[]{:S(2)}) %copy-start.1) | copy-done | bytes 1966104
  61.1 1.4 %copy-done.3 = bf16[512,1536]{1,0:T(8,128)(2,1)S(1)} copy-done((bf16[512,1536]{1,0:T(8,128)(2,1)S(1)}, bf16[512,1536]{1,0:T(8,128)(2,1)}, u32[]{:S(2)}) %copy-start.3) | copy-done | bytes 1572888
  62.5 3.1 %block_tokens.1 = bf16[576,512]{1,0:T(8,128)(2,1)S(1)} custom-call(bf16[432,512]{1,0:T(8,128)(2,1)S(1)} %bitcast.12, bf16[432,512]{1,0:T(8,128)(2,1)S(1)} %bitcast.14, bf16[640,512]{1,0:T(8,128)(2,1)S(1)} %get-tuple-element.39.gn_ref, bf16[640,1536]{1,0:T(8,128)(2,1)S(1)} %copy-done.1, bf16[512,1536]{1,0:T(8,128)(2,1)S(1)} %copy-done.3, ...), custom_call_target="tpu_custom_call" | custom-call | flops 1200000000 | bytes 6000000 | tf_op jit(solution)/shard_map/block_tokens/pallas_call | solution.py:413
  65.6 19.4 %all-to-all-done.in_ref = bf16[16,16,2048]{2,1,0:T(8,128)(2,1)S(1)} async-done(((bf16[16,16,2048]{2,1,0:T(8,128)(2,1)}), bf16[16,16,2048]{2,1,0:T(8,128)(2,1)S(1)}, u32[]{:S(2)}, u32[]{:S(2)}) %all-to-all-start) | async-done | bytes 1048608 | tf_op jit(solution)/shard_map/all_to_all | solution.py:479
  85.0 0.9 share_copies.1
  86.0 4.8 %all-to-all-start.1 = ((bf16[8,16,2048]{2,1,0:T(8,128)(2,1)}), bf16[8,16,2048]{2,1,0:T(8,128)(2,1)S(1)}, u32[]{:S(2)}, u32[]{:S(2)}) async-start(bf16[8,16,2048]{2,1,0:T(8,128)(2,1)} %share_copies.1), calls=%async_computation.1 | async-start | bytes 1048576 | tf_op jit(solution)/shard_map/all_to_all | solution.py:491
  90.9 3.9 %collective-permute-start.6 = (bf16[21,6,512]{2,1,0:T(8,128)(2,1)S(1)}, bf16[21,6,512]{2,1,0:T(8,128)(2,1)S(1)}, u32[]{:S(2)}, u32[]{:S(2)}) collective-permute-start(bf16[21,6,512]{2,1,0:T(8,128)(2,1)S(1)} %slice.73), channel_id=1, source_target_pairs={{0,1},{1,2},{2,3},{3,4},{4,5},{5,6},{6,7},{7,8},{8,9},{9,10},{10,1... | collective-permute-start | bytes 387080 | tf_op jit(solution)/shard_map/ppermute | solution.py:456
  94.8 3.2 %collective-permute-start.5 = (bf16[3,18,512]{2,1,0:T(8,128)(2,1)S(1)}, bf16[3,18,512]{2,1,0:T(8,128)(2,1)S(1)}, u32[]{:S(2)}, u32[]{:S(2)}) collective-permute-start(bf16[3,18,512]{2,1,0:T(8,128)(2,1)S(1)} %slice.72), channel_id=1, source_target_pairs={{0,32},{1,33},{2,34},{3,35},{4,36},{5,37},{6,38},{7,39},{8,40},{9,... | collective-permute-start | bytes 165896 | tf_op jit(solution)/shard_map/ppermute | solution.py:456
  98.0 1.4 %collective-permute-start.4 = (bf16[3,6,512]{2,1,0:T(8,128)(2,1)S(1)}, bf16[3,6,512]{2,1,0:T(8,128)(2,1)S(1)}, u32[]{:S(2)}, u32[]{:S(2)}) collective-permute-start(bf16[3,6,512]{2,1,0:T(8,128)(2,1)S(1)} %slice.71), channel_id=1, source_target_pairs={{0,33},{1,34},{2,35},{3,36},{4,37},{5,38},{6,39},{7,40},{8,41},{9,... | collective-permute-start | bytes 55304 | tf_op jit(solution)/shard_map/ppermute | solution.py:456
  99.4 7.9 %collective-permute-done.4 = bf16[3,6,512]{2,1,0:T(8,128)(2,1)S(1)} collective-permute-done((bf16[3,6,512]{2,1,0:T(8,128)(2,1)S(1)}, bf16[3,6,512]{2,1,0:T(8,128)(2,1)S(1)}, u32[]{:S(2)}, u32[]{:S(2)}) %collective-permute-start.4) | collective-permute-done | bytes 18464 | tf_op jit(solution)/shard_map/ppermute | solution.py:456
  107.3 1.0 maximum_maximum_fusion
  109.0 0.7 convert_reduce_fusion
  (52 shorter events, 2.7 us)
Async XLA Ops:
  0.6 5.4 %copy-start.14 = (bf16[24,24,512]{2,1,0:T(8,128)(2,1)S(1)}, bf16[24,24,512]{2,1,0:T(8,128)(2,1)}, u32[]{:S(2)}) copy-start(bf16[24,24,512]{2,1,0:T(8,128)(2,1)} %param.17) | copy-start | bytes 1769476
  0.6 5.6 %copy-start.15 = (bf16[24,24,512]{2,1,0:T(8,128)(2,1)S(1)}, bf16[24,24,512]{2,1,0:T(8,128)(2,1)}, u32[]{:S(2)}) copy-start(bf16[24,24,512]{2,1,0:T(8,128)(2,1)} %param.18) | copy-start | bytes 1769476
  2.7 8.6 %collective-permute-start = (bf16[48,6,512]{2,1,0:T(8,128)(2,1)S(1)}, bf16[48,6,512]{2,1,0:T(8,128)(2,1)S(1)}, u32[]{:S(2)}, u32[]{:S(2)}) collective-permute-start(bf16[48,6,512]{2,1,0:T(8,128)(2,1)S(1)} %pad_maximum_fusion.2), channel_id=1, source_target_pairs={{0,31},{1,0},{2,1},{3,2},{4,3},{5,4},{6,5},{7,6},{8,7},{9,8},{10,9... | collective-permute-start | bytes 884744 | tf_op jit(solution)/shard_map/ppermute | solution.py:456
  11.4 5.6 %copy-start.7 = (bf16[512,512]{1,0:T(8,128)(2,1)S(1)}, bf16[512,512]{1,0:T(8,128)(2,1)}, u32[]{:S(2)}) copy-start(bf16[512,512]{1,0:T(8,128)(2,1)} %wproj_hbm.1) | copy-start | bytes 1572868
  11.4 5.5 %copy-start.2 = (bf16[512,1536]{1,0:T(8,128)(2,1)S(1)}, bf16[512,1536]{1,0:T(8,128)(2,1)}, u32[]{:S(2)}) copy-start(bf16[512,1536]{1,0:T(8,128)(2,1)} %wqkv_ref.1) | copy-start | bytes 4718596
  11.4 5.5 %copy-start.4 = (bf16[160,144]{1,0:T(8,128)(2,1)S(1)}, bf16[160,144]{1,0:T(8,128)(2,1)}, u32[]{:S(2)}) copy-start(bf16[160,144]{1,0:T(8,128)(2,1)} %constant.14.clone.px_ref) | copy-start | bytes 138244
  11.4 5.5 %copy-start.6 = (f32[512]{0:T(512)S(1)}, f32[512]{0:T(512)}, u32[]{:S(2)}) copy-start(f32[512]{0:T(512)} %param.19) | copy-start | bytes 6148
  11.5 12.9 %collective-permute-start.1 = (bf16[13,24,512]{2,1,0:T(8,128)(2,1)S(1)}, bf16[13,24,512]{2,1,0:T(8,128)(2,1)S(1)}, u32[]{:S(2)}, u32[]{:S(2)}) collective-permute-start(bf16[13,24,512]{2,1,0:T(8,128)(2,1)S(1)} %fusion.2), channel_id=1, source_target_pairs={{0,224},{1,225},{2,226},{3,227},{4,228},{5,229},{6,230},{7,231},{8... | collective-permute-start | bytes 958472 | tf_op jit(solution)/shard_map/ppermute | solution.py:456
  16.7 7.6 %collective-permute-start.2 = (bf16[3,24,512]{2,1,0:T(8,128)(2,1)S(1)}, bf16[3,24,512]{2,1,0:T(8,128)(2,1)S(1)}, u32[]{:S(2)}, u32[]{:S(2)}) collective-permute-start(bf16[3,24,512]{2,1,0:T(8,128)(2,1)S(1)} %pad_maximum_fusion.4), channel_id=1, source_target_pairs={{0,32},{1,33},{2,34},{3,35},{4,36},{5,37},{6,38},{7,39},{8,40},{9,... | collective-permute-start | bytes 221192 | tf_op jit(solution)/shard_map/ppermute | solution.py:456
  24.4 0.7 copy-start.8
  24.5 1.2 %copy-start.10 = (bf16[9,192,160]{2,1,0:T(8,128)(2,1)S(1)}, bf16[9,192,160]{2,1,0:T(8,128)(2,1)}, u32[]{:S(2)}) copy-start(bf16[9,192,160]{2,1,0:T(8,128)(2,1)} %constant.15.clone.pf_ref) | copy-start | bytes 1658884
  24.5 1.2 %copy-start.11 = (bf16[4,160,256]{2,1,0:T(8,128)(2,1)S(1)}, bf16[4,160,256]{2,1,0:T(8,128)(2,1)}, u32[]{:S(2)}) copy-start(bf16[4,160,256]{2,1,0:T(8,128)(2,1)} %constant.18.clone.pi_ref) | copy-start | bytes 983044
  24.5 1.2 %copy-start.12 = (bf16[192,192]{1,0:T(8,128)(2,1)S(1)}, bf16[192,192]{1,0:T(8,128)(2,1)}, u32[]{:S(2)}) copy-start(bf16[192,192]{1,0:T(8,128)(2,1)} %constant.16.clone.pc_ref) | copy-start | bytes 221188
  24.5 1.2 %copy-start.13 = (bf16[64,48]{1,0:T(8,128)(2,1)S(1)}, bf16[64,48]{1,0:T(8,128)(2,1)}, u32[]{:S(2)}) copy-start(bf16[64,48]{1,0:T(8,128)(2,1)} %constant.17.clone.pc3_ref) | copy-start | bytes 18436
  45.1 8.7 %copy-start = (bf16[640,1536]{1,0:T(8,128)(2,1)}, bf16[640,1536]{1,0:T(8,128)(2,1)S(1)}, u32[]{:S(2)}) copy-start(bf16[640,1536]{1,0:T(8,128)(2,1)S(1)} %get-tuple-element.40.dqkv_ref) | copy-start | bytes 5898244
  45.1 7.3 %collective-permute-start.3 = (bf16[16,16,2048]{2,1,0:T(8,128)(2,1)S(1)}, bf16[16,16,2048]{2,1,0:T(8,128)(2,1)S(1)}, u32[]{:S(2)}, u32[]{:S(2)}) collective-permute-start(bf16[16,16,2048]{2,1,0:T(8,128)(2,1)S(1)} %get-tuple-element.36), channel_id=1, source_target_pairs={{0,1},{1,0},{2,3},{3,2},{4,5},{5,4},{6,7},{7,6},{8,9},{9,8},{10,11... | collective-permute-start | bytes 3145736 | tf_op jit(solution)/shard_map/ppermute | solution.py:477
  53.8 5.7 %copy-start.5 = (bf16[144,160]{1,0:T(8,128)(2,1)S(1)}, bf16[144,160]{1,0:T(8,128)(2,1)}, u32[]{:S(2)}) copy-start(bf16[144,160]{1,0:T(8,128)(2,1)} %constant.19.clone.pxt_ref) | copy-start | bytes 138244
  53.8 31.2 %all-to-all-start = ((bf16[16,16,2048]{2,1,0:T(8,128)(2,1)}), bf16[16,16,2048]{2,1,0:T(8,128)(2,1)S(1)}, u32[]{:S(2)}, u32[]{:S(2)}) async-start(bf16[16,16,2048]{2,1,0:T(8,128)(2,1)} %add.3), calls=%async_computation | async-start | bytes 2097152 | tf_op jit(solution)/shard_map/all_to_all | solution.py:479
  59.5 1.5 %copy-start.1 = (bf16[640,1536]{1,0:T(8,128)(2,1)S(1)}, bf16[640,1536]{1,0:T(8,128)(2,1)}, u32[]{:S(2)}) copy-start(bf16[640,1536]{1,0:T(8,128)(2,1)} %copy-done) | copy-start | bytes 5898244
  61.1 1.4 %copy-start.3 = (bf16[512,1536]{1,0:T(8,128)(2,1)S(1)}, bf16[512,1536]{1,0:T(8,128)(2,1)}, u32[]{:S(2)}) copy-start(bf16[512,1536]{1,0:T(8,128)(2,1)} %wqkv_ref.1) | copy-start | bytes 4718596
  86.0 22.4 %all-to-all-start.1 = ((bf16[8,16,2048]{2,1,0:T(8,128)(2,1)}), bf16[8,16,2048]{2,1,0:T(8,128)(2,1)S(1)}, u32[]{:S(2)}, u32[]{:S(2)}) async-start(bf16[8,16,2048]{2,1,0:T(8,128)(2,1)} %share_copies.1), calls=%async_computation.1 | async-start | bytes 1048576 | tf_op jit(solution)/shard_map/all_to_all | solution.py:491
  90.9 16.4 %collective-permute-start.6 = (bf16[21,6,512]{2,1,0:T(8,128)(2,1)S(1)}, bf16[21,6,512]{2,1,0:T(8,128)(2,1)S(1)}, u32[]{:S(2)}, u32[]{:S(2)}) collective-permute-start(bf16[21,6,512]{2,1,0:T(8,128)(2,1)S(1)} %slice.73), channel_id=1, source_target_pairs={{0,1},{1,2},{2,3},{3,4},{4,5},{5,6},{6,7},{7,8},{8,9},{9,10},{10,1... | collective-permute-start | bytes 387080 | tf_op jit(solution)/shard_map/ppermute | solution.py:456
  94.8 12.5 %collective-permute-start.5 = (bf16[3,18,512]{2,1,0:T(8,128)(2,1)S(1)}, bf16[3,18,512]{2,1,0:T(8,128)(2,1)S(1)}, u32[]{:S(2)}, u32[]{:S(2)}) collective-permute-start(bf16[3,18,512]{2,1,0:T(8,128)(2,1)S(1)} %slice.72), channel_id=1, source_target_pairs={{0,32},{1,33},{2,34},{3,35},{4,36},{5,37},{6,38},{7,39},{8,40},{9,... | collective-permute-start | bytes 165896 | tf_op jit(solution)/shard_map/ppermute | solution.py:456
  98.0 9.3 %collective-permute-start.4 = (bf16[3,6,512]{2,1,0:T(8,128)(2,1)S(1)}, bf16[3,6,512]{2,1,0:T(8,128)(2,1)S(1)}, u32[]{:S(2)}, u32[]{:S(2)}) collective-permute-start(bf16[3,6,512]{2,1,0:T(8,128)(2,1)S(1)} %slice.71), channel_id=1, source_target_pairs={{0,33},{1,34},{2,35},{3,36},{4,37},{5,38},{6,39},{7,40},{8,41},{9,... | collective-permute-start | bytes 55304 | tf_op jit(solution)/shard_map/ppermute | solution.py:456
  (1 other events, 0.7 us)

commit v6 on v5

--- a/solution.py
+++ b/solution.py
@@ -40,10 +40,11 @@
     return (col // WLON) * WP + i * WLON + col % WLON
 
 
-def to_windows():
+def to_windows(upward=False):
     out = np.zeros((WRP, WR), np.float32)
     for t in range(WR):
-        out[window_row(t // COLS, t % COLS), t] = 1
+        i = t // COLS
+        out[window_row(WLAT - 1 - i if upward else i, t % COLS), t] = 1
     return out.astype(jnp.bfloat16)
 
 
@@ -69,9 +70,10 @@
                 f = 5 + 2 * a + rp
                 if f // WLAT != k:
                     continue
+                i = f % WLAT if k > 0 else WLAT - 1 - f
                 for col in range(COLS):
                     q = (col % 2) * 2 + rp
-                    out[n, q * padded + (a - 4 * g) * 12 + col // 2, window_row(f % WLAT, col)] = 1
+                    out[n, q * padded + (a - 4 * g) * 12 + col // 2, window_row(i, col)] = 1
     return out.astype(jnp.bfloat16)
 
 
@@ -147,13 +149,33 @@
     return stacked(q2 * 0.125, low), k2, v2, win
 
 
-def attention(first, mask, x_ref, px, gain, wqkv, wproj, xw, normed, qkv, probs, attn, fine):
+def first_row_attention(qkv, attn, start, masked):
+    win, top = slice(start, start + WP), slice(start, start + 16)
+    head = lax.broadcasted_iota(jnp.int32, (1, D), 1) // HEAD
+    mine = [head == h for h in range(HEADS)]
+    q = qkv[top, :D] * 0.125
+    qs = jnp.concatenate([q * m.astype(F32).astype(BF) for m in mine], axis=0)
+    s = dot_nt(qkv[win, D : 2 * D], qs)[:WIN]
+    if masked is not None:
+        s = jnp.where(masked, MASKED, s)
+    e = jnp.exp(s - jnp.max(s, axis=0, keepdims=True))
+    p = e * (1.0 / jnp.sum(e, axis=0, keepdims=True))
+    p = jnp.concatenate([p, jnp.zeros((WP - WIN, p.shape[1]), F32)], axis=0).astype(BF)
+    o = dot_tn(p, qkv[win, 2 * D :])
+    total = jnp.zeros((16, D), F32)
+    for h, m in enumerate(mine):
+        total = jnp.where(m, o[16 * h : 16 * h + 16], total)
+    attn[top, :] = total.astype(BF)
+    attn[start + 16 : start + WP, :] = jnp.zeros((WP - 16, D), BF)
+
+
+def attention(first, whole, mask, edge, x_ref, px, gain, wqkv, wproj, xw, normed, qkv, probs, attn, fine):
     first_lane, low = lane_halves()
     base = WRP * first
     span = slice(base, base + 3 * WRP)
     for k in range(3):
         rows = slice(base + WRP * k, base + WRP * k + WRP)
-        x = dot(px[...], x_ref[WR * k : WR * k + WR, :])
+        x = dot(px[k][...], x_ref[WR * k : WR * k + WR, :])
         xw[WRP * k : WRP * k + WRP, :] = x.astype(BF)
         hat, _ = norm_parts(x)
         normed[rows, :] = (hat * gain[...]).astype(BF)
@@ -178,7 +200,10 @@
             attn[win, 128 * hp : 128 * hp + 128] = v.astype(BF)
         return carry
 
-    lax.fori_loop(first, first + 3, window_row, 0)
+    lax.fori_loop(first, first + whole, window_row, 0)
+    for k in range(first + whole, first + 3):
+        for w in range(2):
+            first_row_attention(qkv, attn, WRP * k + WP * w, edge if k == NWR - 1 else None)
     for j in range(2):
         columns = slice(256 * j, 256 * j + 256)
         fine[span, columns] = (
@@ -187,11 +212,11 @@
 
 
 def early_kernel(x_ref, px_ref, ng_ref, wqkv, wproj, normed, qkv, probs, attn, fine, xw):
-    attention(0, None, x_ref, px_ref, ng_ref, wqkv, wproj, xw, normed, qkv, probs, attn, fine)
+    attention(0, 3, None, None, x_ref, (px_ref,) * 3, ng_ref, wqkv, wproj, xw, normed, qkv, probs, attn, fine)
 
 
 def kernel(
-    lat_size, x_ref, c_ref, ng_ref, mg_ref, eg_ref, px_ref, pf_ref, pc_ref, pc3_ref, pi_ref,
+    lat_size, x_ref, c_ref, ng_ref, mg_ref, eg_ref, px_ref, pxu_ref, pf_ref, pc_ref, pc3_ref, pi_ref,
     wqkv_hbm, wproj_hbm, wm_hbm, we_hbm, normed_hbm, qkv_hbm, probs_hbm, attn_hbm, fine_hbm,
     mine_hbm, other_hbm, gn_hbm, dqkv_hbm,
     wqkv, wproj, wm, we, xw, normed, qkv, probs, attn, fine, fq, cq, mg, dw, gq, gn, d_attn, dqkv, mine, other, sems,
@@ -214,12 +239,14 @@
     first_lane, low = lane_halves()
 
     def masked_at(k):
-        edge = ((k == NWR - 1) & (lat == 0)) | ((k == EARLY) & (lat == lat_size - 1))
+        edge = (k == EARLY) & (lat == lat_size - 1)
         return apart & edge
+
+    upper = (key[:, : 16 * HEADS] >= WIN // 2) & (lat == 0)
 
     loads[0].wait()
     loads[1].wait()
-    attention(EARLY, masked_at, x_ref, px_ref, ng_ref, wqkv, wproj, xw, normed, qkv, probs, attn, fine)
+    attention(EARLY, 1, masked_at, upper, x_ref, (px_ref, px_ref, pxu_ref), ng_ref, wqkv, wproj, xw, normed, qkv, probs, attn, fine)
     loads[2].wait()
 
     for g in range(4):
@@ -388,11 +415,11 @@
         out_shape=tuple(
             jax.ShapeDtypeStruct(shape, BF) for shape in (share, share, (4 * WRP, D), (4 * WRP, 3 * D))
         ),
-        in_specs=[VMEM] * 10 + [HBM] * 9,
+        in_specs=[VMEM] * 11 + [HBM] * 9,
         out_specs=(HBM,) * 4,
         scratch_shapes=[
             bf(D, 3 * D), bf(D, D), bf(4 * D, 2 * D), bf(2 * D, 4 * D),
-            bf((NWR - EARLY) * WRP, D), bf(NWR * WRP, D), bf(NWR * WRP, 3 * D), pltpu.VMEM((NWR, HEADS, WIN, 256), F32),
+            bf((NWR - EARLY) * WRP, D), bf(NWR * WRP, D), bf(NWR * WRP, 3 * D), pltpu.VMEM((EARLY + 1, HEADS, WIN, 256), F32),
             bf(NWR * WRP, D), bf(NWR * WRP, D),
             bf(4, QROWS, D), bf(4, QROWS, D), bf(QROWS, 4 * D), bf(QROWS, 4 * D), bf(4, QROWS, D),
             bf(4 * WRP, D), bf(4 * WRP, D), bf(4 * WRP, 3 * D), bf(*share), bf(*share),
@@ -403,7 +430,7 @@
         name="block",
     )(
         x, c, norm_gain[None], merge_gain[None], expand_gain[None],
-        jnp.asarray(to_windows()), jnp.asarray(fine_offsets()),
+        jnp.asarray(to_windows()), jnp.asarray(to_windows(True)), jnp.asarray(fine_offsets()),
         jnp.asarray(cot_offsets(4, 48)), jnp.asarray(cot_offsets(1, 16)), jnp.asarray(from_offsets()),
         w_qkv, w_proj, w_merge, w_expand, *early,
     )
@@ -480,10 +507,11 @@
 
     d_work = finish_tokens(x_early, x, gn, dqkv, w_qkv, norm_gain).reshape(ROWS, COLS, D)
     last_row, last_col = ROWS - SLAT, COLS - SLON
-    spread, d_work = lax.optimization_barrier((spread, d_work))
     rows = moved(d_work[last_row:, :last_col], 1, 0)
     corner = moved(d_work[last_row:, last_col:], 1, 1)
-    columns = moved(d_work[:last_row, last_col:], 0, 1)
+    edge = d_work[:last_row, last_col:]
+    spread, rows, corner, edge = lax.optimization_barrier((spread, rows, corner, edge))
+    columns = moved(edge, 0, 1)
     top = jnp.concatenate([corner, rows], axis=1)
     rest = jnp.concatenate([columns, d_work[:last_row, :last_col]], axis=1)
     d_tokens = jnp.concatenate([top, rest], axis=0)

time: 110 us -> 104 us (0.945)
  the two profiles are of different devices: /device:TPU:1 before, /device:TPU:0 now
where the time goes in v6:
time: 104 us
  waiting for transfers between devices  41.9 us (40%)
  Pallas kernels  27 us (26%)
  starting transfers between devices  23 us (22%)
  local copies, waits for them, and re-layouts  6.53 us (6%)
  other arithmetic  4.11 us (4%)
    ppermute x6, waiting for transfers between devices, moved(): return lax.ppermute(value, names, pairs)  35.2 us
    pallas_call x1, Pallas kernels, compute(): pl.pallas_call(functools.partial(kernel, lats), out_shape=tuple((jax.Shap...  18.9 us
    ppermute x6, starting transfers between devices, moved(): return lax.ppermute(value, names, pairs)  12.8 us
    all_to_all x1, starting transfers between devices, body(): spread = lax.all_to_all(pair, 'tile', 0, 0, tiled=True)  5.79 us
    all_to_all x1, starting transfers between devices, body(): lax.all_to_all(share_copies(spread, lats), 'lat', 0, 0, tiled=True)  4.15 us
    unnamed x34, local copies, waits for them, and re-layouts  4.09 us
    all_to_all x1, waiting for transfers between devices, body(): lax.all_to_all(share_copies(spread, lats), 'lat', 0, 0, tiled=True)  4.06 us
    pallas_call x1, Pallas kernels, start_early(): pl.pallas_call(early_kernel, out_shape=tuple((jax.ShapeDtypeStruct(*one)...  4.01 us
  transfers between devices with their start and end apart: 9, of which 6 were waited for; matrix products, arithmetic and copies ran while one was open for 1% of the time, Pallas kernels for 7%

profile of v6, /device:TPU:0, one launch (start us, length us, event | category | flops | bytes accessed | tf_op | source)
XLA Modules:
  0.0 103.6 jit_solution(15360363845605186213)
XLA Ops:
  0.7 1.0 slice.59
  1.7 0.9 slice.60
  2.7 4.6 %collective-permute-start = (bf16[48,6,512]{2,1,0:T(8,128)(2,1)S(1)}, bf16[48,6,512]{2,1,0:T(8,128)(2,1)S(1)}, u32[]{:S(2)}, u32[]{:S(2)}) collective-permute-start(bf16[48,6,512]{2,1,0:T(8,128)(2,1)S(1)} %pad_maximum_fusion.2), channel_id=1, source_target_pairs={{0,31},{1,0},{2,1},{3,2},{4,3},{5,4},{6,5},{7,6},{8,7},{9,8},{10,9... | collective-permute-start | bytes 884744 | tf_op jit(solution)/shard_map/ppermute | solution.py:483
  7.6 5.0 %collective-permute-done = bf16[48,6,512]{2,1,0:T(8,128)(2,1)S(1)} collective-permute-done((bf16[48,6,512]{2,1,0:T(8,128)(2,1)S(1)}, bf16[48,6,512]{2,1,0:T(8,128)(2,1)S(1)}, u32[]{:S(2)}, u32[]{:S(2)}) %collective-permute-start) | collective-permute-done | bytes 294944 | tf_op jit(solution)/shard_map/ppermute | solution.py:483
  12.7 5.3 %collective-permute-start.1 = (bf16[13,24,512]{2,1,0:T(8,128)(2,1)S(1)}, bf16[13,24,512]{2,1,0:T(8,128)(2,1)S(1)}, u32[]{:S(2)}, u32[]{:S(2)}) collective-permute-start(bf16[13,24,512]{2,1,0:T(8,128)(2,1)S(1)} %fusion.2), channel_id=1, source_target_pairs={{0,224},{1,225},{2,226},{3,227},{4,228},{5,229},{6,230},{7,231},{8... | collective-permute-start | bytes 958472 | tf_op jit(solution)/shard_map/ppermute | solution.py:483
  18.2 4.0 %block_early.1 = (bf16[480,512]{1,0:T(8,128)(2,1)S(1)}, bf16[480,1536]{1,0:T(8,128)(2,1)S(1)}, f32[3,8,72,256]{3,2,1,0:T(8,128)S(1)}, bf16[480,512]{1,0:T(8,128)(2,1)S(1)}, bf16[480,512]{1,0:T(8,128)(2,1)S(1)}) custom-call(bf16[432,512]{1,0:T(8,128)(2,1)S(1)} %bitcast.11, bf16[160,144]{1,0:T(8,128)(2,1)S(1)} %copy-done.4, f32[1,512]{1,0:T(1,128)S(1)} %bitcast.16, ...), custom_call_target="tpu_custom_call" | custom-call | flops 1400000000 | bytes 8000000 | tf_op jit(solution)/shard_map/block_early/pallas_call | solution.py:398
  22.3 3.8 %collective-permute-done.2 = bf16[3,24,512]{2,1,0:T(8,128)(2,1)S(1)} collective-permute-done((bf16[3,24,512]{2,1,0:T(8,128)(2,1)S(1)}, bf16[3,24,512]{2,1,0:T(8,128)(2,1)S(1)}, u32[]{:S(2)}, u32[]{:S(2)}) %collective-permute-start.2) | collective-permute-done | bytes 73760 | tf_op jit(solution)/shard_map/ppermute | solution.py:483
  26.8 0.5 copy-done.10
  27.4 18.9 %block.1 = (bf16[16,16,2048]{2,1,0:T(8,128)(2,1)S(1)}, bf16[16,16,2048]{2,1,0:T(8,128)(2,1)S(1)}, bf16[640,512]{1,0:T(8,128)(2,1)S(1)}, bf16[640,1536]{1,0:T(8,128)(2,1)S(1)}) custom-call(bf16[432,512]{1,0:T(8,128)(2,1)S(1)} %bitcast.13, bf16[672,512]{1,0:T(8,128)(2,1)S(1)} %bitcast.15, f32[1,512]{1,0:T(1,128)S(1)} %bitcast.17, f32[1,2048]{1,0:T(1,128)S(1)} %bitcast.19, ...), custom_call_target="tpu_custom_call" | custom-call | flops 7000000000 | bytes 18000000 | tf_op jit(solution)/shard_map/block/pallas_call | solution.py:413
  46.7 2.6 %collective-permute-done.3 = bf16[16,16,2048]{2,1,0:T(8,128)(2,1)S(1)} collective-permute-done((bf16[16,16,2048]{2,1,0:T(8,128)(2,1)S(1)}, bf16[16,16,2048]{2,1,0:T(8,128)(2,1)S(1)}, u32[]{:S(2)}, u32[]{:S(2)}) %collective-permute-start.3) | collective-permute-done | bytes 1048608 | tf_op jit(solution)/shard_map/ppermute | solution.py:504
  49.4 1.4 %add.3 = bf16[16,16,2048]{2,1,0:T(8,128)(2,1)} add(bf16[16,16,2048]{2,1,0:T(8,128)(2,1)S(1)} %get-tuple-element.37, bf16[16,16,2048]{2,1,0:T(8,128)(2,1)S(1)} %collective-permute-done.3) | non-fusion elementwise | flops 524288 | bytes 3145728 | tf_op jit(solution)/shard_map/add | solution.py:505
  50.7 5.8 %all-to-all-start = ((bf16[16,16,2048]{2,1,0:T(8,128)(2,1)}), bf16[16,16,2048]{2,1,0:T(8,128)(2,1)S(1)}, u32[]{:S(2)}, u32[]{:S(2)}) async-start(bf16[16,16,2048]{2,1,0:T(8,128)(2,1)} %add.3), calls=%async_computation | async-start | bytes 2097152 | tf_op jit(solution)/shard_map/all_to_all | solution.py:506
  56.5 1.5 %copy-done.1 = bf16[640,1536]{1,0:T(8,128)(2,1)S(1)} copy-done((bf16[640,1536]{1,0:T(8,128)(2,1)S(1)}, bf16[640,1536]{1,0:T(8,128)(2,1)}, u32[]{:S(2)}) %copy-start.1) | copy-done | bytes 1966104
  58.1 1.4 %copy-done.3 = bf16[512,1536]{1,0:T(8,128)(2,1)S(1)} copy-done((bf16[512,1536]{1,0:T(8,128)(2,1)S(1)}, bf16[512,1536]{1,0:T(8,128)(2,1)}, u32[]{:S(2)}) %copy-start.3) | copy-done | bytes 1572888
  59.5 3.1 %block_tokens.1 = bf16[576,512]{1,0:T(8,128)(2,1)S(1)} custom-call(bf16[432,512]{1,0:T(8,128)(2,1)S(1)} %bitcast.12, bf16[432,512]{1,0:T(8,128)(2,1)S(1)} %bitcast.14, bf16[640,512]{1,0:T(8,128)(2,1)S(1)} %get-tuple-element.41.gn_ref, bf16[640,1536]{1,0:T(8,128)(2,1)S(1)} %copy-done.1, bf16[512,1536]{1,0:T(8,128)(2,1)S(1)} %copy-done.3, ...), custom_call_target="tpu_custom_call" | custom-call | flops 1200000000 | bytes 6000000 | tf_op jit(solution)/shard_map/block_tokens/pallas_call | solution.py:440
  62.6 2.8 %collective-permute-start.4 = (bf16[3,18,512]{2,1,0:T(8,128)(2,1)S(1)}, bf16[3,18,512]{2,1,0:T(8,128)(2,1)S(1)}, u32[]{:S(2)}, u32[]{:S(2)}) collective-permute-start(bf16[3,18,512]{2,1,0:T(8,128)(2,1)S(1)} %slice.83), channel_id=1, source_target_pairs={{0,32},{1,33},{2,34},{3,35},{4,36},{5,37},{6,38},{7,39},{8,40},{9,... | collective-permute-start | bytes 165896 | tf_op jit(solution)/shard_map/ppermute | solution.py:483
  65.6 19.6 %collective-permute-done.5 = bf16[3,6,512]{2,1,0:T(8,128)(2,1)S(1)} collective-permute-done((bf16[3,6,512]{2,1,0:T(8,128)(2,1)S(1)}, bf16[3,6,512]{2,1,0:T(8,128)(2,1)S(1)}, u32[]{:S(2)}, u32[]{:S(2)}) %collective-permute-start.5) | collective-permute-done | bytes 18464 | tf_op jit(solution)/shard_map/ppermute | solution.py:483
  85.2 0.9 share_copies.1
  86.1 4.2 %all-to-all-start.1 = ((bf16[8,16,2048]{2,1,0:T(8,128)(2,1)}), bf16[8,16,2048]{2,1,0:T(8,128)(2,1)S(1)}, u32[]{:S(2)}, u32[]{:S(2)}) async-start(bf16[8,16,2048]{2,1,0:T(8,128)(2,1)} %share_copies.1), calls=%async_computation.1 | async-start | bytes 1048576 | tf_op jit(solution)/shard_map/all_to_all | solution.py:519
  90.3 6.9 %collective-permute-done.6 = bf16[21,6,512]{2,1,0:T(8,128)(2,1)S(1)} collective-permute-done((bf16[21,6,512]{2,1,0:T(8,128)(2,1)S(1)}, bf16[21,6,512]{2,1,0:T(8,128)(2,1)S(1)}, u32[]{:S(2)}, u32[]{:S(2)}) %collective-permute-start.6) | collective-permute-done | bytes 129056 | tf_op jit(solution)/shard_map/ppermute | solution.py:483
  97.2 1.0 maximum_maximum_fusion
  98.2 4.1 %all-to-all-done.1 = bf16[8,16,2048]{2,1,0:T(8,128)(2,1)S(1)} async-done(((bf16[8,16,2048]{2,1,0:T(8,128)(2,1)}), bf16[8,16,2048]{2,1,0:T(8,128)(2,1)S(1)}, u32[]{:S(2)}, u32[]{:S(2)}) %all-to-all-start.1) | async-done | bytes 524320 | tf_op jit(solution)/shard_map/all_to_all | solution.py:519
  102.3 0.6 convert_reduce_fusion.1
  102.9 0.7 convert_reduce_fusion
  (54 shorter events, 2.0 us)
Async XLA Ops:
  0.6 6.7 %copy-start.15 = (bf16[24,24,512]{2,1,0:T(8,128)(2,1)S(1)}, bf16[24,24,512]{2,1,0:T(8,128)(2,1)}, u32[]{:S(2)}) copy-start(bf16[24,24,512]{2,1,0:T(8,128)(2,1)} %param.18) | copy-start | bytes 1769476
  0.6 6.8 %copy-start.16 = (bf16[24,24,512]{2,1,0:T(8,128)(2,1)S(1)}, bf16[24,24,512]{2,1,0:T(8,128)(2,1)}, u32[]{:S(2)}) copy-start(bf16[24,24,512]{2,1,0:T(8,128)(2,1)} %param.19) | copy-start | bytes 1769476
  2.7 9.9 %collective-permute-start = (bf16[48,6,512]{2,1,0:T(8,128)(2,1)S(1)}, bf16[48,6,512]{2,1,0:T(8,128)(2,1)S(1)}, u32[]{:S(2)}, u32[]{:S(2)}) collective-permute-start(bf16[48,6,512]{2,1,0:T(8,128)(2,1)S(1)} %pad_maximum_fusion.2), channel_id=1, source_target_pairs={{0,31},{1,0},{2,1},{3,2},{4,3},{5,4},{6,5},{7,6},{8,7},{9,8},{10,9... | collective-permute-start | bytes 884744 | tf_op jit(solution)/shard_map/ppermute | solution.py:483
  12.7 5.5 %copy-start.7 = (bf16[512,512]{1,0:T(8,128)(2,1)S(1)}, bf16[512,512]{1,0:T(8,128)(2,1)}, u32[]{:S(2)}) copy-start(bf16[512,512]{1,0:T(8,128)(2,1)} %wproj_hbm.1) | copy-start | bytes 1572868
  12.7 5.5 %copy-start.2 = (bf16[512,1536]{1,0:T(8,128)(2,1)S(1)}, bf16[512,1536]{1,0:T(8,128)(2,1)}, u32[]{:S(2)}) copy-start(bf16[512,1536]{1,0:T(8,128)(2,1)} %wqkv_ref.1) | copy-start | bytes 4718596
  12.7 5.5 %copy-start.4 = (bf16[160,144]{1,0:T(8,128)(2,1)S(1)}, bf16[160,144]{1,0:T(8,128)(2,1)}, u32[]{:S(2)}) copy-start(bf16[160,144]{1,0:T(8,128)(2,1)} %constant.16.clone.px_ref) | copy-start | bytes 138244
  12.7 5.5 %copy-start.6 = (f32[512]{0:T(512)S(1)}, f32[512]{0:T(512)}, u32[]{:S(2)}) copy-start(f32[512]{0:T(512)} %param.20) | copy-start | bytes 6148
  12.7 13.3 %collective-permute-start.1 = (bf16[13,24,512]{2,1,0:T(8,128)(2,1)S(1)}, bf16[13,24,512]{2,1,0:T(8,128)(2,1)S(1)}, u32[]{:S(2)}, u32[]{:S(2)}) collective-permute-start(bf16[13,24,512]{2,1,0:T(8,128)(2,1)S(1)} %fusion.2), channel_id=1, source_target_pairs={{0,224},{1,225},{2,226},{3,227},{4,228},{5,229},{6,230},{7,231},{8... | collective-permute-start | bytes 958472 | tf_op jit(solution)/shard_map/ppermute | solution.py:483
  18.0 8.0 %collective-permute-start.2 = (bf16[3,24,512]{2,1,0:T(8,128)(2,1)S(1)}, bf16[3,24,512]{2,1,0:T(8,128)(2,1)S(1)}, u32[]{:S(2)}, u32[]{:S(2)}) collective-permute-start(bf16[3,24,512]{2,1,0:T(8,128)(2,1)S(1)} %pad_maximum_fusion.4), channel_id=1, source_target_pairs={{0,32},{1,33},{2,34},{3,35},{4,36},{5,37},{6,38},{7,39},{8,40},{9,... | collective-permute-start | bytes 221192 | tf_op jit(solution)/shard_map/ppermute | solution.py:483
  26.1 1.2 %copy-start.10 = (bf16[9,192,160]{2,1,0:T(8,128)(2,1)S(1)}, bf16[9,192,160]{2,1,0:T(8,128)(2,1)}, u32[]{:S(2)}) copy-start(bf16[9,192,160]{2,1,0:T(8,128)(2,1)} %constant.18.clone.pf_ref) | copy-start | bytes 1658884
  26.1 1.2 %copy-start.11 = (bf16[4,160,256]{2,1,0:T(8,128)(2,1)S(1)}, bf16[4,160,256]{2,1,0:T(8,128)(2,1)}, u32[]{:S(2)}) copy-start(bf16[4,160,256]{2,1,0:T(8,128)(2,1)} %constant.21.clone.pi_ref) | copy-start | bytes 983044
  26.2 1.2 %copy-start.12 = (bf16[192,192]{1,0:T(8,128)(2,1)S(1)}, bf16[192,192]{1,0:T(8,128)(2,1)}, u32[]{:S(2)}) copy-start(bf16[192,192]{1,0:T(8,128)(2,1)} %constant.19.clone.pc_ref) | copy-start | bytes 221188
  26.2 1.3 %copy-start.13 = (bf16[160,144]{1,0:T(8,128)(2,1)S(1)}, bf16[160,144]{1,0:T(8,128)(2,1)}, u32[]{:S(2)}) copy-start(bf16[160,144]{1,0:T(8,128)(2,1)} %constant.17.clone.pxu_ref) | copy-start | bytes 138244
  26.2 1.2 %copy-start.14 = (bf16[64,48]{1,0:T(8,128)(2,1)S(1)}, bf16[64,48]{1,0:T(8,128)(2,1)}, u32[]{:S(2)}) copy-start(bf16[64,48]{1,0:T(8,128)(2,1)} %constant.20.clone.pc3_ref) | copy-start | bytes 18436
  46.4 4.3 %copy-start = (bf16[640,1536]{1,0:T(8,128)(2,1)}, bf16[640,1536]{1,0:T(8,128)(2,1)S(1)}, u32[]{:S(2)}) copy-start(bf16[640,1536]{1,0:T(8,128)(2,1)S(1)} %get-tuple-element.42.dqkv_ref) | copy-start | bytes 5898244
  46.4 3.0 %collective-permute-start.3 = (bf16[16,16,2048]{2,1,0:T(8,128)(2,1)S(1)}, bf16[16,16,2048]{2,1,0:T(8,128)(2,1)S(1)}, u32[]{:S(2)}, u32[]{:S(2)}) collective-permute-start(bf16[16,16,2048]{2,1,0:T(8,128)(2,1)S(1)} %get-tuple-element.38), channel_id=1, source_target_pairs={{0,1},{1,0},{2,3},{3,2},{4,5},{5,4},{6,7},{7,6},{8,9},{9,8},{10,11... | collective-permute-start | bytes 3145736 | tf_op jit(solution)/shard_map/ppermute | solution.py:504
  50.7 5.8 %copy-start.5 = (bf16[144,160]{1,0:T(8,128)(2,1)S(1)}, bf16[144,160]{1,0:T(8,128)(2,1)}, u32[]{:S(2)}) copy-start(bf16[144,160]{1,0:T(8,128)(2,1)} %constant.22.clone.pxt_ref) | copy-start | bytes 138244
  50.7 34.4 %all-to-all-start = ((bf16[16,16,2048]{2,1,0:T(8,128)(2,1)}), bf16[16,16,2048]{2,1,0:T(8,128)(2,1)S(1)}, u32[]{:S(2)}, u32[]{:S(2)}) async-start(bf16[16,16,2048]{2,1,0:T(8,128)(2,1)} %add.3), calls=%async_computation | async-start | bytes 2097152 | tf_op jit(solution)/shard_map/all_to_all | solution.py:506
  56.5 1.5 %copy-start.1 = (bf16[640,1536]{1,0:T(8,128)(2,1)S(1)}, bf16[640,1536]{1,0:T(8,128)(2,1)}, u32[]{:S(2)}) copy-start(bf16[640,1536]{1,0:T(8,128)(2,1)} %copy-done) | copy-start | bytes 5898244
  58.1 1.4 %copy-start.3 = (bf16[512,1536]{1,0:T(8,128)(2,1)S(1)}, bf16[512,1536]{1,0:T(8,128)(2,1)}, u32[]{:S(2)}) copy-start(bf16[512,1536]{1,0:T(8,128)(2,1)} %wqkv_ref.1) | copy-start | bytes 4718596
  62.6 22.5 %collective-permute-start.4 = (bf16[3,18,512]{2,1,0:T(8,128)(2,1)S(1)}, bf16[3,18,512]{2,1,0:T(8,128)(2,1)S(1)}, u32[]{:S(2)}, u32[]{:S(2)}) collective-permute-start(bf16[3,18,512]{2,1,0:T(8,128)(2,1)S(1)} %slice.83), channel_id=1, source_target_pairs={{0,32},{1,33},{2,34},{3,35},{4,36},{5,37},{6,38},{7,39},{8,40},{9,... | collective-permute-start | bytes 165896 | tf_op jit(solution)/shard_map/ppermute | solution.py:483
  65.4 19.7 %collective-permute-start.5 = (bf16[3,6,512]{2,1,0:T(8,128)(2,1)S(1)}, bf16[3,6,512]{2,1,0:T(8,128)(2,1)S(1)}, u32[]{:S(2)}, u32[]{:S(2)}) collective-permute-start(bf16[3,6,512]{2,1,0:T(8,128)(2,1)S(1)} %slice.84), channel_id=1, source_target_pairs={{0,33},{1,34},{2,35},{3,36},{4,37},{5,38},{6,39},{7,40},{8,41},{9,... | collective-permute-start | bytes 55304 | tf_op jit(solution)/shard_map/ppermute | solution.py:483
  86.1 16.2 %all-to-all-start.1 = ((bf16[8,16,2048]{2,1,0:T(8,128)(2,1)}), bf16[8,16,2048]{2,1,0:T(8,128)(2,1)S(1)}, u32[]{:S(2)}, u32[]{:S(2)}) async-start(bf16[8,16,2048]{2,1,0:T(8,128)(2,1)} %share_copies.1), calls=%async_computation.1 | async-start | bytes 1048576 | tf_op jit(solution)/shard_map/all_to_all | solution.py:519
  90.3 6.9 %collective-permute-start.6 = (bf16[21,6,512]{2,1,0:T(8,128)(2,1)S(1)}, bf16[21,6,512]{2,1,0:T(8,128)(2,1)S(1)}, u32[]{:S(2)}, u32[]{:S(2)}) collective-permute-start(bf16[21,6,512]{2,1,0:T(8,128)(2,1)S(1)} %slice.85), channel_id=1, source_target_pairs={{0,1},{1,2},{2,3},{3,4},{4,5},{5,6},{6,7},{7,8},{8,9},{9,10},{10,1... | collective-permute-start | bytes 387080 | tf_op jit(solution)/shard_map/ppermute | solution.py:483
  (2 other events, 1.4 us)

commit v7 on v6

--- a/solution.py
+++ b/solution.py
@@ -219,7 +219,7 @@
     lat_size, x_ref, c_ref, ng_ref, mg_ref, eg_ref, px_ref, pxu_ref, pf_ref, pc_ref, pc3_ref, pi_ref,
     wqkv_hbm, wproj_hbm, wm_hbm, we_hbm, normed_hbm, qkv_hbm, probs_hbm, attn_hbm, fine_hbm,
     mine_hbm, other_hbm, gn_hbm, dqkv_hbm,
-    wqkv, wproj, wm, we, xw, normed, qkv, probs, attn, fine, fq, cq, mg, dw, gq, gn, d_attn, dqkv, mine, other, sems,
+    wqkv, wproj, wm, we, xw, normed, qkv, probs, attn, fine, fq, hats, cq, mg, dw, gq, gn, d_attn, dqkv, mine, other, sems,
 ):
     lat = lax.axis_index("lat")
     core = lax.axis_index("core")
@@ -275,11 +275,14 @@
             total = total + jnp.sum(centred * centred, axis=-1, keepdims=True)
         return average, lax.rsqrt(total * (1.0 / (4 * D)) + EPSILON)
 
+    scales = []
     for r in range(QROWS // 32):
         rows = slice(32 * r, 32 * r + 32)
         average, scale = merge_stats(rows)
+        scales.append(scale)
         for q in range(4):
             hat = (fq[q, rows, :].astype(F32) - average) * scale
+            hats[q, rows, :] = hat
             mg[rows, D * q : D * q + D] = (hat * mg_ref[:, D * q : D * q + D]).astype(BF)
 
     loads[3].wait()
@@ -296,18 +299,18 @@
 
     for r in range(QROWS // 32):
         rows = slice(32 * r, 32 * r + 32)
-        average, scale = merge_stats(rows)
+        scale = scales[r]
         sum_dy = jnp.zeros((32, 1), F32)
         sum_dyh = jnp.zeros((32, 1), F32)
         for q in range(4):
-            hat = (fq[q, rows, :].astype(F32) - average) * scale
+            hat = hats[q, rows, :]
             dy = mg[rows, D * q : D * q + D].astype(F32) * mg_ref[:, D * q : D * q + D]
             sum_dy = sum_dy + jnp.sum(dy, axis=-1, keepdims=True)
             sum_dyh = sum_dyh + jnp.sum(dy * hat, axis=-1, keepdims=True)
         mean_dy = sum_dy * (1.0 / (4 * D))
         mean_dyh = sum_dyh * (1.0 / (4 * D))
         for q in range(4):
-            hat = (fq[q, rows, :].astype(F32) - average) * scale
+            hat = hats[q, rows, :]
             dy = mg[rows, D * q : D * q + D].astype(F32) * mg_ref[:, D * q : D * q + D]
             back = (scale * (dy - mean_dy - hat * mean_dyh)).astype(BF)
             gq[q, rows, :] = (cq[q, rows, :].astype(F32) + back.astype(F32)).astype(BF)
@@ -366,7 +369,7 @@
             dqkv[win, 2 * D + lanes.start : 2 * D + lanes.stop] = dv[i].astype(BF)
         return carry
 
-    lax.fori_loop(0, 4, backward, 0)
+    lax.fori_loop(0, 4, backward, 0, unroll=2)
     store(dqkv, dqkv_hbm)
     for j in range(3):
         put(j, dot_tn(normed[inner, :], dqkv[:, D * j : D * j + D]))
@@ -421,7 +424,7 @@
             bf(D, 3 * D), bf(D, D), bf(4 * D, 2 * D), bf(2 * D, 4 * D),
             bf((NWR - EARLY) * WRP, D), bf(NWR * WRP, D), bf(NWR * WRP, 3 * D), pltpu.VMEM((EARLY + 1, HEADS, WIN, 256), F32),
             bf(NWR * WRP, D), bf(NWR * WRP, D),
-            bf(4, QROWS, D), bf(4, QROWS, D), bf(QROWS, 4 * D), bf(QROWS, 4 * D), bf(4, QROWS, D),
+            bf(4, QROWS, D), pltpu.VMEM((4, QROWS, D), F32), bf(4, QROWS, D), bf(QROWS, 4 * D), bf(QROWS, 4 * D), bf(4, QROWS, D),
             bf(4 * WRP, D), bf(4 * WRP, D), bf(4 * WRP, 3 * D), bf(*share), bf(*share),
             pltpu.SemaphoreType.DMA((19,)),
         ],

time: 104 us -> 104 us (level)
  no operation moved by 1% of the time
where the time goes in v7:
time: 104 us; the launch traced here: 103 us
  waiting for transfers between devices  41.9 us (40%)
  Pallas kernels  27.1 us (26%)
  starting transfers between devices  22.8 us (22%)
  local copies, waits for them, and re-layouts  6.53 us (6%)
  other arithmetic  4.11 us (4%)
    ppermute x6, waiting for transfers between devices, moved(): return lax.ppermute(value, names, pairs)  35.2 us
    pallas_call x1, Pallas kernels, compute(): pl.pallas_call(functools.partial(kernel, lats), out_shape=tuple((jax.Shap...  19 us
    ppermute x6, starting transfers between devices, moved(): return lax.ppermute(value, names, pairs)  12.8 us
    all_to_all x1, starting transfers between devices, body(): spread = lax.all_to_all(pair, 'tile', 0, 0, tiled=True)  5.79 us
    all_to_all x1, starting transfers between devices, body(): lax.all_to_all(share_copies(spread, lats), 'lat', 0, 0, tiled=True)  4.15 us
    unnamed x34, local copies, waits for them, and re-layouts  4.09 us
    all_to_all x1, waiting for transfers between devices, body(): lax.all_to_all(share_copies(spread, lats), 'lat', 0, 0, tiled=True)  4.06 us
    pallas_call x1, Pallas kernels, start_early(): pl.pallas_call(early_kernel, out_shape=tuple((jax.ShapeDtypeStruct(*one)...  4.01 us
  transfers between devices with their start and end apart: 9, of which 6 were waited for; matrix products, arithmetic and copies ran while one was open for 1% of the time, Pallas kernels for 7%

profile of v7, /device:TPU:0, one launch (start us, length us, event | category | flops | bytes accessed | tf_op | source)
XLA Modules:
  0.0 103.4 jit_solution(16985124490840888439)
XLA Ops:
  0.7 1.0 %slice.59 = bf16[24,6,512]{2,1,0:T(8,128)(2,1)S(1)} slice(bf16[24,24,512]{2,1,0:T(8,128)(2,1)} %param.18), slice={[0:24], [0:6], [0:512]} | slice | bytes 294912 | tf_op jit(solution)/shard_map/slice | solution.py:488
  1.7 0.9 slice.60
  2.7 4.6 %collective-permute-start = (bf16[48,6,512]{2,1,0:T(8,128)(2,1)S(1)}, bf16[48,6,512]{2,1,0:T(8,128)(2,1)S(1)}, u32[]{:S(2)}, u32[]{:S(2)}) collective-permute-start(bf16[48,6,512]{2,1,0:T(8,128)(2,1)S(1)} %pad_maximum_fusion.2), channel_id=1, source_target_pairs={{0,31},{1,0},{2,1},{3,2},{4,3},{5,4},{6,5},{7,6},{8,7},{9,8},{10,9... | collective-permute-start | bytes 884744 | tf_op jit(solution)/shard_map/ppermute | solution.py:486
  7.6 5.0 %collective-permute-done = bf16[48,6,512]{2,1,0:T(8,128)(2,1)S(1)} collective-permute-done((bf16[48,6,512]{2,1,0:T(8,128)(2,1)S(1)}, bf16[48,6,512]{2,1,0:T(8,128)(2,1)S(1)}, u32[]{:S(2)}, u32[]{:S(2)}) %collective-permute-start) | collective-permute-done | bytes 294944 | tf_op jit(solution)/shard_map/ppermute | solution.py:486
  12.7 5.3 %collective-permute-start.1 = (bf16[13,24,512]{2,1,0:T(8,128)(2,1)S(1)}, bf16[13,24,512]{2,1,0:T(8,128)(2,1)S(1)}, u32[]{:S(2)}, u32[]{:S(2)}) collective-permute-start(bf16[13,24,512]{2,1,0:T(8,128)(2,1)S(1)} %fusion.2), channel_id=1, source_target_pairs={{0,224},{1,225},{2,226},{3,227},{4,228},{5,229},{6,230},{7,231},{8... | collective-permute-start | bytes 958472 | tf_op jit(solution)/shard_map/ppermute | solution.py:486
  18.2 4.0 %block_early.1 = (bf16[480,512]{1,0:T(8,128)(2,1)S(1)}, bf16[480,1536]{1,0:T(8,128)(2,1)S(1)}, f32[3,8,72,256]{3,2,1,0:T(8,128)S(1)}, bf16[480,512]{1,0:T(8,128)(2,1)S(1)}, bf16[480,512]{1,0:T(8,128)(2,1)S(1)}) custom-call(bf16[432,512]{1,0:T(8,128)(2,1)S(1)} %bitcast.11, bf16[160,144]{1,0:T(8,128)(2,1)S(1)} %copy-done.4, f32[1,512]{1,0:T(1,128)S(1)} %bitcast.16, ...), custom_call_target="tpu_custom_call" | custom-call | flops 1400000000 | bytes 8000000 | tf_op jit(solution)/shard_map/block_early/pallas_call | solution.py:401
  22.3 3.8 %collective-permute-done.2 = bf16[3,24,512]{2,1,0:T(8,128)(2,1)S(1)} collective-permute-done((bf16[3,24,512]{2,1,0:T(8,128)(2,1)S(1)}, bf16[3,24,512]{2,1,0:T(8,128)(2,1)S(1)}, u32[]{:S(2)}, u32[]{:S(2)}) %collective-permute-start.2) | collective-permute-done | bytes 73760 | tf_op jit(solution)/shard_map/ppermute | solution.py:486
  26.8 0.5 copy-done.10
  27.4 19.0 %block.1 = (bf16[16,16,2048]{2,1,0:T(8,128)(2,1)S(1)}, bf16[16,16,2048]{2,1,0:T(8,128)(2,1)S(1)}, bf16[640,512]{1,0:T(8,128)(2,1)S(1)}, bf16[640,1536]{1,0:T(8,128)(2,1)S(1)}) custom-call(bf16[432,512]{1,0:T(8,128)(2,1)S(1)} %bitcast.13, bf16[672,512]{1,0:T(8,128)(2,1)S(1)} %bitcast.15, f32[1,512]{1,0:T(1,128)S(1)} %bitcast.17, f32[1,2048]{1,0:T(1,128)S(1)} %bitcast.19, ...), custom_call_target="tpu_custom_call" | custom-call | flops 7000000000 | bytes 18000000 | tf_op jit(solution)/shard_map/block/pallas_call | solution.py:416
  46.5 2.6 %collective-permute-done.3 = bf16[16,16,2048]{2,1,0:T(8,128)(2,1)S(1)} collective-permute-done((bf16[16,16,2048]{2,1,0:T(8,128)(2,1)S(1)}, bf16[16,16,2048]{2,1,0:T(8,128)(2,1)S(1)}, u32[]{:S(2)}, u32[]{:S(2)}) %collective-permute-start.3) | collective-permute-done | bytes 1048608 | tf_op jit(solution)/shard_map/ppermute | solution.py:507
  49.2 1.4 %add.3 = bf16[16,16,2048]{2,1,0:T(8,128)(2,1)} add(bf16[16,16,2048]{2,1,0:T(8,128)(2,1)S(1)} %get-tuple-element.37, bf16[16,16,2048]{2,1,0:T(8,128)(2,1)S(1)} %collective-permute-done.3) | non-fusion elementwise | flops 524288 | bytes 3145728 | tf_op jit(solution)/shard_map/add | solution.py:508
  50.5 5.8 %all-to-all-start = ((bf16[16,16,2048]{2,1,0:T(8,128)(2,1)}), bf16[16,16,2048]{2,1,0:T(8,128)(2,1)S(1)}, u32[]{:S(2)}, u32[]{:S(2)}) async-start(bf16[16,16,2048]{2,1,0:T(8,128)(2,1)} %add.3), calls=%async_computation | async-start | bytes 2097152 | tf_op jit(solution)/shard_map/all_to_all | solution.py:509
  56.3 1.5 %copy-done.1 = bf16[640,1536]{1,0:T(8,128)(2,1)S(1)} copy-done((bf16[640,1536]{1,0:T(8,128)(2,1)S(1)}, bf16[640,1536]{1,0:T(8,128)(2,1)}, u32[]{:S(2)}) %copy-start.1) | copy-done | bytes 1966104
  57.9 1.4 %copy-done.3 = bf16[512,1536]{1,0:T(8,128)(2,1)S(1)} copy-done((bf16[512,1536]{1,0:T(8,128)(2,1)S(1)}, bf16[512,1536]{1,0:T(8,128)(2,1)}, u32[]{:S(2)}) %copy-start.3) | copy-done | bytes 1572888
  59.3 3.1 %block_tokens.1 = bf16[576,512]{1,0:T(8,128)(2,1)S(1)} custom-call(bf16[432,512]{1,0:T(8,128)(2,1)S(1)} %bitcast.12, bf16[432,512]{1,0:T(8,128)(2,1)S(1)} %bitcast.14, bf16[640,512]{1,0:T(8,128)(2,1)S(1)} %get-tuple-element.41.gn_ref, bf16[640,1536]{1,0:T(8,128)(2,1)S(1)} %copy-done.1, bf16[512,1536]{1,0:T(8,128)(2,1)S(1)} %copy-done.3, ...), custom_call_target="tpu_custom_call" | custom-call | flops 1200000000 | bytes 6000000 | tf_op jit(solution)/shard_map/block_tokens/pallas_call | solution.py:443
  62.4 2.8 %collective-permute-start.4 = (bf16[3,18,512]{2,1,0:T(8,128)(2,1)S(1)}, bf16[3,18,512]{2,1,0:T(8,128)(2,1)S(1)}, u32[]{:S(2)}, u32[]{:S(2)}) collective-permute-start(bf16[3,18,512]{2,1,0:T(8,128)(2,1)S(1)} %slice.83), channel_id=1, source_target_pairs={{0,32},{1,33},{2,34},{3,35},{4,36},{5,37},{6,38},{7,39},{8,40},{9,... | collective-permute-start | bytes 165896 | tf_op jit(solution)/shard_map/ppermute | solution.py:486
  65.4 19.6 %collective-permute-done.5 = bf16[3,6,512]{2,1,0:T(8,128)(2,1)S(1)} collective-permute-done((bf16[3,6,512]{2,1,0:T(8,128)(2,1)S(1)}, bf16[3,6,512]{2,1,0:T(8,128)(2,1)S(1)}, u32[]{:S(2)}, u32[]{:S(2)}) %collective-permute-start.5) | collective-permute-done | bytes 18464 | tf_op jit(solution)/shard_map/ppermute | solution.py:486
  85.0 0.9 share_copies.1
  85.9 4.2 %all-to-all-start.1 = ((bf16[8,16,2048]{2,1,0:T(8,128)(2,1)}), bf16[8,16,2048]{2,1,0:T(8,128)(2,1)S(1)}, u32[]{:S(2)}, u32[]{:S(2)}) async-start(bf16[8,16,2048]{2,1,0:T(8,128)(2,1)} %share_copies.1), calls=%async_computation.1 | async-start | bytes 1048576 | tf_op jit(solution)/shard_map/all_to_all | solution.py:522
  90.1 6.9 %collective-permute-done.6 = bf16[21,6,512]{2,1,0:T(8,128)(2,1)S(1)} collective-permute-done((bf16[21,6,512]{2,1,0:T(8,128)(2,1)S(1)}, bf16[21,6,512]{2,1,0:T(8,128)(2,1)S(1)}, u32[]{:S(2)}, u32[]{:S(2)}) %collective-permute-start.6) | collective-permute-done | bytes 129056 | tf_op jit(solution)/shard_map/ppermute | solution.py:486
  97.0 1.0 maximum_maximum_fusion
  98.0 4.1 %all-to-all-done.1 = bf16[8,16,2048]{2,1,0:T(8,128)(2,1)S(1)} async-done(((bf16[8,16,2048]{2,1,0:T(8,128)(2,1)}), bf16[8,16,2048]{2,1,0:T(8,128)(2,1)S(1)}, u32[]{:S(2)}, u32[]{:S(2)}) %all-to-all-start.1) | async-done | bytes 524320 | tf_op jit(solution)/shard_map/all_to_all | solution.py:522
  102.1 0.6 convert_reduce_fusion.1
  102.7 0.7 convert_reduce_fusion
  (54 shorter events, 1.8 us)
Async XLA Ops:
  0.6 6.7 %copy-start.15 = (bf16[24,24,512]{2,1,0:T(8,128)(2,1)S(1)}, bf16[24,24,512]{2,1,0:T(8,128)(2,1)}, u32[]{:S(2)}) copy-start(bf16[24,24,512]{2,1,0:T(8,128)(2,1)} %param.18) | copy-start | bytes 1769476
  0.6 6.8 %copy-start.16 = (bf16[24,24,512]{2,1,0:T(8,128)(2,1)S(1)}, bf16[24,24,512]{2,1,0:T(8,128)(2,1)}, u32[]{:S(2)}) copy-start(bf16[24,24,512]{2,1,0:T(8,128)(2,1)} %param.19) | copy-start | bytes 1769476
  2.7 9.9 %collective-permute-start = (bf16[48,6,512]{2,1,0:T(8,128)(2,1)S(1)}, bf16[48,6,512]{2,1,0:T(8,128)(2,1)S(1)}, u32[]{:S(2)}, u32[]{:S(2)}) collective-permute-start(bf16[48,6,512]{2,1,0:T(8,128)(2,1)S(1)} %pad_maximum_fusion.2), channel_id=1, source_target_pairs={{0,31},{1,0},{2,1},{3,2},{4,3},{5,4},{6,5},{7,6},{8,7},{9,8},{10,9... | collective-permute-start | bytes 884744 | tf_op jit(solution)/shard_map/ppermute | solution.py:486
  12.7 5.5 %copy-start.7 = (bf16[512,512]{1,0:T(8,128)(2,1)S(1)}, bf16[512,512]{1,0:T(8,128)(2,1)}, u32[]{:S(2)}) copy-start(bf16[512,512]{1,0:T(8,128)(2,1)} %wproj_hbm.1) | copy-start | bytes 1572868
  12.7 5.5 %copy-start.2 = (bf16[512,1536]{1,0:T(8,128)(2,1)S(1)}, bf16[512,1536]{1,0:T(8,128)(2,1)}, u32[]{:S(2)}) copy-start(bf16[512,1536]{1,0:T(8,128)(2,1)} %wqkv_ref.1) | copy-start | bytes 4718596
  12.7 5.5 %copy-start.4 = (bf16[160,144]{1,0:T(8,128)(2,1)S(1)}, bf16[160,144]{1,0:T(8,128)(2,1)}, u32[]{:S(2)}) copy-start(bf16[160,144]{1,0:T(8,128)(2,1)} %constant.16.clone.px_ref) | copy-start | bytes 138244
  12.7 5.5 %copy-start.6 = (f32[512]{0:T(512)S(1)}, f32[512]{0:T(512)}, u32[]{:S(2)}) copy-start(f32[512]{0:T(512)} %param.20) | copy-start | bytes 6148
  12.7 13.3 %collective-permute-start.1 = (bf16[13,24,512]{2,1,0:T(8,128)(2,1)S(1)}, bf16[13,24,512]{2,1,0:T(8,128)(2,1)S(1)}, u32[]{:S(2)}, u32[]{:S(2)}) collective-permute-start(bf16[13,24,512]{2,1,0:T(8,128)(2,1)S(1)} %fusion.2), channel_id=1, source_target_pairs={{0,224},{1,225},{2,226},{3,227},{4,228},{5,229},{6,230},{7,231},{8... | collective-permute-start | bytes 958472 | tf_op jit(solution)/shard_map/ppermute | solution.py:486
  18.0 8.0 %collective-permute-start.2 = (bf16[3,24,512]{2,1,0:T(8,128)(2,1)S(1)}, bf16[3,24,512]{2,1,0:T(8,128)(2,1)S(1)}, u32[]{:S(2)}, u32[]{:S(2)}) collective-permute-start(bf16[3,24,512]{2,1,0:T(8,128)(2,1)S(1)} %pad_maximum_fusion.4), channel_id=1, source_target_pairs={{0,32},{1,33},{2,34},{3,35},{4,36},{5,37},{6,38},{7,39},{8,40},{9,... | collective-permute-start | bytes 221192 | tf_op jit(solution)/shard_map/ppermute | solution.py:486
  26.1 1.2 %copy-start.10 = (bf16[9,192,160]{2,1,0:T(8,128)(2,1)S(1)}, bf16[9,192,160]{2,1,0:T(8,128)(2,1)}, u32[]{:S(2)}) copy-start(bf16[9,192,160]{2,1,0:T(8,128)(2,1)} %constant.18.clone.pf_ref) | copy-start | bytes 1658884
  26.1 1.2 %copy-start.11 = (bf16[4,160,256]{2,1,0:T(8,128)(2,1)S(1)}, bf16[4,160,256]{2,1,0:T(8,128)(2,1)}, u32[]{:S(2)}) copy-start(bf16[4,160,256]{2,1,0:T(8,128)(2,1)} %constant.21.clone.pi_ref) | copy-start | bytes 983044
  26.2 1.2 %copy-start.12 = (bf16[192,192]{1,0:T(8,128)(2,1)S(1)}, bf16[192,192]{1,0:T(8,128)(2,1)}, u32[]{:S(2)}) copy-start(bf16[192,192]{1,0:T(8,128)(2,1)} %constant.19.clone.pc_ref) | copy-start | bytes 221188
  26.2 1.3 %copy-start.13 = (bf16[160,144]{1,0:T(8,128)(2,1)S(1)}, bf16[160,144]{1,0:T(8,128)(2,1)}, u32[]{:S(2)}) copy-start(bf16[160,144]{1,0:T(8,128)(2,1)} %constant.17.clone.pxu_ref) | copy-start | bytes 138244
  26.2 1.2 %copy-start.14 = (bf16[64,48]{1,0:T(8,128)(2,1)S(1)}, bf16[64,48]{1,0:T(8,128)(2,1)}, u32[]{:S(2)}) copy-start(bf16[64,48]{1,0:T(8,128)(2,1)} %constant.20.clone.pc3_ref) | copy-start | bytes 18436
  46.4 4.1 %copy-start = (bf16[640,1536]{1,0:T(8,128)(2,1)}, bf16[640,1536]{1,0:T(8,128)(2,1)S(1)}, u32[]{:S(2)}) copy-start(bf16[640,1536]{1,0:T(8,128)(2,1)S(1)} %get-tuple-element.42.dqkv_ref) | copy-start | bytes 5898244
  46.4 2.7 %collective-permute-start.3 = (bf16[16,16,2048]{2,1,0:T(8,128)(2,1)S(1)}, bf16[16,16,2048]{2,1,0:T(8,128)(2,1)S(1)}, u32[]{:S(2)}, u32[]{:S(2)}) collective-permute-start(bf16[16,16,2048]{2,1,0:T(8,128)(2,1)S(1)} %get-tuple-element.38), channel_id=1, source_target_pairs={{0,1},{1,0},{2,3},{3,2},{4,5},{5,4},{6,7},{7,6},{8,9},{9,8},{10,11... | collective-permute-start | bytes 3145736 | tf_op jit(solution)/shard_map/ppermute | solution.py:507
  50.5 5.8 %copy-start.5 = (bf16[144,160]{1,0:T(8,128)(2,1)S(1)}, bf16[144,160]{1,0:T(8,128)(2,1)}, u32[]{:S(2)}) copy-start(bf16[144,160]{1,0:T(8,128)(2,1)} %constant.22.clone.pxt_ref) | copy-start | bytes 138244
  50.5 34.4 %all-to-all-start = ((bf16[16,16,2048]{2,1,0:T(8,128)(2,1)}), bf16[16,16,2048]{2,1,0:T(8,128)(2,1)S(1)}, u32[]{:S(2)}, u32[]{:S(2)}) async-start(bf16[16,16,2048]{2,1,0:T(8,128)(2,1)} %add.3), calls=%async_computation | async-start | bytes 2097152 | tf_op jit(solution)/shard_map/all_to_all | solution.py:509
  56.3 1.5 %copy-start.1 = (bf16[640,1536]{1,0:T(8,128)(2,1)S(1)}, bf16[640,1536]{1,0:T(8,128)(2,1)}, u32[]{:S(2)}) copy-start(bf16[640,1536]{1,0:T(8,128)(2,1)} %copy-done) | copy-start | bytes 5898244
  57.9 1.4 %copy-start.3 = (bf16[512,1536]{1,0:T(8,128)(2,1)S(1)}, bf16[512,1536]{1,0:T(8,128)(2,1)}, u32[]{:S(2)}) copy-start(bf16[512,1536]{1,0:T(8,128)(2,1)} %wqkv_ref.1) | copy-start | bytes 4718596
  62.4 22.5 %collective-permute-start.4 = (bf16[3,18,512]{2,1,0:T(8,128)(2,1)S(1)}, bf16[3,18,512]{2,1,0:T(8,128)(2,1)S(1)}, u32[]{:S(2)}, u32[]{:S(2)}) collective-permute-start(bf16[3,18,512]{2,1,0:T(8,128)(2,1)S(1)} %slice.83), channel_id=1, source_target_pairs={{0,32},{1,33},{2,34},{3,35},{4,36},{5,37},{6,38},{7,39},{8,40},{9,... | collective-permute-start | bytes 165896 | tf_op jit(solution)/shard_map/ppermute | solution.py:486
  65.2 19.7 %collective-permute-start.5 = (bf16[3,6,512]{2,1,0:T(8,128)(2,1)S(1)}, bf16[3,6,512]{2,1,0:T(8,128)(2,1)S(1)}, u32[]{:S(2)}, u32[]{:S(2)}) collective-permute-start(bf16[3,6,512]{2,1,0:T(8,128)(2,1)S(1)} %slice.84), channel_id=1, source_target_pairs={{0,33},{1,34},{2,35},{3,36},{4,37},{5,38},{6,39},{7,40},{8,41},{9,... | collective-permute-start | bytes 55304 | tf_op jit(solution)/shard_map/ppermute | solution.py:486
  85.9 16.2 %all-to-all-start.1 = ((bf16[8,16,2048]{2,1,0:T(8,128)(2,1)}), bf16[8,16,2048]{2,1,0:T(8,128)(2,1)S(1)}, u32[]{:S(2)}, u32[]{:S(2)}) async-start(bf16[8,16,2048]{2,1,0:T(8,128)(2,1)} %share_copies.1), calls=%async_computation.1 | async-start | bytes 1048576 | tf_op jit(solution)/shard_map/all_to_all | solution.py:522
  90.1 6.9 %collective-permute-start.6 = (bf16[21,6,512]{2,1,0:T(8,128)(2,1)S(1)}, bf16[21,6,512]{2,1,0:T(8,128)(2,1)S(1)}, u32[]{:S(2)}, u32[]{:S(2)}) collective-permute-start(bf16[21,6,512]{2,1,0:T(8,128)(2,1)S(1)} %slice.85), channel_id=1, source_target_pairs={{0,1},{1,2},{2,3},{3,4},{4,5},{5,6},{6,7},{7,8},{8,9},{9,10},{10,1... | collective-permute-start | bytes 387080 | tf_op jit(solution)/shard_map/ppermute | solution.py:486
  (2 other events, 1.4 us)

commit v8 on v7

--- a/solution.py
+++ b/solution.py
@@ -452,6 +452,45 @@
     )(x_early, x, gn, dqkv, w_qkv, norm_gain[None], jnp.asarray(to_windows()), jnp.asarray(to_windows().T))
 
 
+def add_kernel(a_ref, b_ref, out_ref):
+    out_ref[...] = a_ref[...] + b_ref[...]
+
+
+def pair_sum(a, b):
+    return pl.pallas_call(
+        add_kernel,
+        out_shape=jax.ShapeDtypeStruct(a.shape, BF),
+        in_specs=[VMEM, VMEM],
+        out_specs=VMEM,
+        compiler_params=pltpu.CompilerParams(vmem_limit_bytes=SMALL_GRANT),
+        name="pair_sum",
+    )(a, b)
+
+
+def total_kernel(in_ref, qkv_ref, proj_ref):
+    for j in range(4):
+        columns = slice(D * j, D * j + D)
+        total = in_ref[0, :, columns].astype(F32)
+        for i in range(1, in_ref.shape[0]):
+            total = total + in_ref[i, :, columns].astype(F32)
+        if j < 3:
+            qkv_ref[:, columns] = total
+        else:
+            proj_ref[...] = total
+
+
+def total_sum(gathered):
+    rows = gathered.shape[1]
+    return pl.pallas_call(
+        total_kernel,
+        out_shape=(jax.ShapeDtypeStruct((rows, 3 * D), F32), jax.ShapeDtypeStruct((rows, D), F32)),
+        in_specs=[VMEM],
+        out_specs=(VMEM, VMEM),
+        compiler_params=pltpu.CompilerParams(vmem_limit_bytes=SMALL_GRANT),
+        name="total_sum",
+    )(gathered)
+
+
 def copies_kernel(in_ref, out_ref):
     for j in range(in_ref.shape[2] // D):
         columns = slice(D * j, D * j + D)
@@ -505,7 +544,7 @@
     )
 
     theirs = lax.ppermute(other, "core", [(i, cores - 1 - i) for i in range(cores)])
-    pair, dqkv = lax.optimization_barrier((mine + theirs, dqkv))
+    pair, dqkv = lax.optimization_barrier((pair_sum(mine, theirs), dqkv))
     spread = lax.all_to_all(pair, "tile", 0, 0, tiled=True)
 
     d_work = finish_tokens(x_early, x, gn, dqkv, w_qkv, norm_gain).reshape(ROWS, COLS, D)
@@ -520,8 +559,7 @@
     d_tokens = jnp.concatenate([top, rest], axis=0)
 
     gathered = lax.all_to_all(share_copies(spread, lats), "lat", 0, 0, tiled=True)
-    grad_qkv = jnp.sum(gathered[:, :, : 3 * D].astype(F32), axis=0)
-    grad_proj = jnp.sum(gathered[:, :, 3 * D :].astype(F32), axis=0)
+    grad_qkv, grad_proj = total_sum(gathered)
     return (d_tokens, grad_qkv, grad_proj)
 
 

time: 104 us -> 103 us (level)
  other arithmetic: 4.11 us -> 1.44 us
  Pallas kernels: 27.1 us -> 28.9 us
    pallas_call x0 -> x2, Pallas kernels: none -> 1.79 us  [the longest x1 1.09 us: pair_sum(): pl.pallas_call(add_kernel, out_shape=jax.ShapeDtypeStruct(a.shape, BF), i...]
    add x1 -> x0, other arithmetic: 1.35 us -> none  [body(): pair, dqkv = lax.optimization_barrier((mine + theirs, dqkv))]
    reduce_sum x2 -> x0, other arithmetic: 1.33 us -> none  [the longest x1 0.69 us: body(): grad_qkv = jnp.sum(gathered[:, :, :3 * D].astype(F32), axis=0)]
  transfers between devices with their start and end apart: 9 -> 9, of which waited for: 6 -> 6; matrix products, arithmetic and copies ran while one was open for 1% -> 2% of each run, Pallas kernels for 7% -> 7%
where the time goes in v8:
time: 103 us
  waiting for transfers between devices  41.9 us (41%)
  Pallas kernels  28.9 us (28%)
  starting transfers between devices  22.8 us (22%)
  local copies, waits for them, and re-layouts  6.52 us (6%)
  other arithmetic  1.44 us (1%)
    ppermute x6, waiting for transfers between devices, moved(): return lax.ppermute(value, names, pairs)  35.2 us
    pallas_call x1, Pallas kernels, compute(): pl.pallas_call(functools.partial(kernel, lats), out_shape=tuple((jax.Shap...  19 us
    ppermute x6, starting transfers between devices, moved(): return lax.ppermute(value, names, pairs)  12.8 us
    all_to_all x1, starting transfers between devices, body(): spread = lax.all_to_all(pair, 'tile', 0, 0, tiled=True)  5.78 us
    all_to_all x1, starting transfers between devices, body(): lax.all_to_all(share_copies(spread, lats), 'lat', 0, 0, tiled=True)  4.15 us
    unnamed x34, local copies, waits for them, and re-layouts  4.08 us
    all_to_all x1, waiting for transfers between devices, body(): lax.all_to_all(share_copies(spread, lats), 'lat', 0, 0, tiled=True)  4.06 us
    pallas_call x1, Pallas kernels, start_early(): pl.pallas_call(early_kernel, out_shape=tuple((jax.ShapeDtypeStruct(*one)...  4.02 us
  transfers between devices with their start and end apart: 9, of which 6 were waited for; matrix products, arithmetic and copies ran while one was open for 2% of the time, Pallas kernels for 7%

profile of v8, /device:TPU:0, one launch (start us, length us, event | category | flops | bytes accessed | tf_op | source)
XLA Modules:
  0.0 102.6 jit_solution(7837810972746158162)
XLA Ops:
  0.7 1.0 %slice.53 = bf16[24,6,512]{2,1,0:T(8,128)(2,1)S(1)} slice(bf16[24,24,512]{2,1,0:T(8,128)(2,1)} %param.18), slice={[0:24], [0:6], [0:512]} | slice | bytes 294912 | tf_op jit(solution)/shard_map/slice | solution.py:527
  1.7 0.9 slice.54
  2.7 4.6 %collective-permute-start = (bf16[48,6,512]{2,1,0:T(8,128)(2,1)S(1)}, bf16[48,6,512]{2,1,0:T(8,128)(2,1)S(1)}, u32[]{:S(2)}, u32[]{:S(2)}) collective-permute-start(bf16[48,6,512]{2,1,0:T(8,128)(2,1)S(1)} %pad_maximum_fusion.2), channel_id=1, source_target_pairs={{0,31},{1,0},{2,1},{3,2},{4,3},{5,4},{6,5},{7,6},{8,7},{9,8},{10,9... | collective-permute-start | bytes 884744 | tf_op jit(solution)/shard_map/ppermute | solution.py:525
  7.6 5.0 %collective-permute-done = bf16[48,6,512]{2,1,0:T(8,128)(2,1)S(1)} collective-permute-done((bf16[48,6,512]{2,1,0:T(8,128)(2,1)S(1)}, bf16[48,6,512]{2,1,0:T(8,128)(2,1)S(1)}, u32[]{:S(2)}, u32[]{:S(2)}) %collective-permute-start) | collective-permute-done | bytes 294944 | tf_op jit(solution)/shard_map/ppermute | solution.py:525
  12.7 5.3 %collective-permute-start.1 = (bf16[13,24,512]{2,1,0:T(8,128)(2,1)S(1)}, bf16[13,24,512]{2,1,0:T(8,128)(2,1)S(1)}, u32[]{:S(2)}, u32[]{:S(2)}) collective-permute-start(bf16[13,24,512]{2,1,0:T(8,128)(2,1)S(1)} %fusion.2), channel_id=1, source_target_pairs={{0,224},{1,225},{2,226},{3,227},{4,228},{5,229},{6,230},{7,231},{8... | collective-permute-start | bytes 958472 | tf_op jit(solution)/shard_map/ppermute | solution.py:525
  18.2 4.0 %block_early.1 = (bf16[480,512]{1,0:T(8,128)(2,1)S(1)}, bf16[480,1536]{1,0:T(8,128)(2,1)S(1)}, f32[3,8,72,256]{3,2,1,0:T(8,128)S(1)}, bf16[480,512]{1,0:T(8,128)(2,1)S(1)}, bf16[480,512]{1,0:T(8,128)(2,1)S(1)}) custom-call(bf16[432,512]{1,0:T(8,128)(2,1)S(1)} %bitcast.11, bf16[160,144]{1,0:T(8,128)(2,1)S(1)} %copy-done.4, f32[1,512]{1,0:T(1,128)S(1)} %bitcast.16, ...), custom_call_target="tpu_custom_call" | custom-call | flops 1400000000 | bytes 8000000 | tf_op jit(solution)/shard_map/block_early/pallas_call | solution.py:401
  22.3 3.8 %collective-permute-done.2 = bf16[3,24,512]{2,1,0:T(8,128)(2,1)S(1)} collective-permute-done((bf16[3,24,512]{2,1,0:T(8,128)(2,1)S(1)}, bf16[3,24,512]{2,1,0:T(8,128)(2,1)S(1)}, u32[]{:S(2)}, u32[]{:S(2)}) %collective-permute-start.2) | collective-permute-done | bytes 73760 | tf_op jit(solution)/shard_map/ppermute | solution.py:525
  26.4 0.4 copy-done.8
  26.8 0.5 copy-done.10
  27.4 19.0 %block.1 = (bf16[16,16,2048]{2,1,0:T(8,128)(2,1)S(1)}, bf16[16,16,2048]{2,1,0:T(8,128)(2,1)S(1)}, bf16[640,512]{1,0:T(8,128)(2,1)S(1)}, bf16[640,1536]{1,0:T(8,128)(2,1)S(1)}) custom-call(bf16[432,512]{1,0:T(8,128)(2,1)S(1)} %bitcast.13, bf16[672,512]{1,0:T(8,128)(2,1)S(1)} %bitcast.15, f32[1,512]{1,0:T(1,128)S(1)} %bitcast.17, f32[1,2048]{1,0:T(1,128)S(1)} %bitcast.19, ...), custom_call_target="tpu_custom_call" | custom-call | flops 7000000000 | bytes 18000000 | tf_op jit(solution)/shard_map/block/pallas_call | solution.py:416
  46.6 2.6 %collective-permute-done.3.b_ref = bf16[16,16,2048]{2,1,0:T(8,128)(2,1)S(1)} collective-permute-done((bf16[16,16,2048]{2,1,0:T(8,128)(2,1)S(1)}, bf16[16,16,2048]{2,1,0:T(8,128)(2,1)S(1)}, u32[]{:S(2)}, u32[]{:S(2)}) %collective-permute-start.3) | collective-permute-done | bytes 1048608 | tf_op jit(solution)/shard_map/ppermute | solution.py:546
  49.2 1.1 %pair_sum.1 = bf16[16,16,2048]{2,1,0:T(8,128)(2,1)} custom-call(bf16[16,16,2048]{2,1,0:T(8,128)(2,1)S(1)} %get-tuple-element.39.a_ref, bf16[16,16,2048]{2,1,0:T(8,128)(2,1)S(1)} %collective-permute-done.3.b_ref), custom_call_target="tpu_custom_call" | custom-call | tf_op jit(solution)/shard_map/pair_sum/pallas_call | solution.py:460
  50.3 5.8 %all-to-all-start = ((bf16[16,16,2048]{2,1,0:T(8,128)(2,1)}), bf16[16,16,2048]{2,1,0:T(8,128)(2,1)S(1)}, u32[]{:S(2)}, u32[]{:S(2)}) async-start(bf16[16,16,2048]{2,1,0:T(8,128)(2,1)} %pair_sum.1), calls=%async_computation | async-start | bytes 2097152 | tf_op jit(solution)/shard_map/all_to_all | solution.py:548
  56.1 1.5 %copy-done.1 = bf16[640,1536]{1,0:T(8,128)(2,1)S(1)} copy-done((bf16[640,1536]{1,0:T(8,128)(2,1)S(1)}, bf16[640,1536]{1,0:T(8,128)(2,1)}, u32[]{:S(2)}) %copy-start.1) | copy-done | bytes 1966104
  57.6 1.4 %copy-done.3 = bf16[512,1536]{1,0:T(8,128)(2,1)S(1)} copy-done((bf16[512,1536]{1,0:T(8,128)(2,1)S(1)}, bf16[512,1536]{1,0:T(8,128)(2,1)}, u32[]{:S(2)}) %copy-start.3) | copy-done | bytes 1572888
  59.1 3.1 %block_tokens.1 = bf16[576,512]{1,0:T(8,128)(2,1)S(1)} custom-call(bf16[432,512]{1,0:T(8,128)(2,1)S(1)} %bitcast.12, bf16[432,512]{1,0:T(8,128)(2,1)S(1)} %bitcast.14, bf16[640,512]{1,0:T(8,128)(2,1)S(1)} %get-tuple-element.43.gn_ref, bf16[640,1536]{1,0:T(8,128)(2,1)S(1)} %copy-done.1, bf16[512,1536]{1,0:T(8,128)(2,1)S(1)} %copy-done.3, ...), custom_call_target="tpu_custom_call" | custom-call | flops 1200000000 | bytes 6000000 | tf_op jit(solution)/shard_map/block_tokens/pallas_call | solution.py:443
  62.2 2.8 %collective-permute-start.4 = (bf16[3,18,512]{2,1,0:T(8,128)(2,1)S(1)}, bf16[3,18,512]{2,1,0:T(8,128)(2,1)S(1)}, u32[]{:S(2)}, u32[]{:S(2)}) collective-permute-start(bf16[3,18,512]{2,1,0:T(8,128)(2,1)S(1)} %slice.75), channel_id=1, source_target_pairs={{0,32},{1,33},{2,34},{3,35},{4,36},{5,37},{6,38},{7,39},{8,40},{9,... | collective-permute-start | bytes 165896 | tf_op jit(solution)/shard_map/ppermute | solution.py:525
  65.2 19.6 %collective-permute-done.5 = bf16[3,6,512]{2,1,0:T(8,128)(2,1)S(1)} collective-permute-done((bf16[3,6,512]{2,1,0:T(8,128)(2,1)S(1)}, bf16[3,6,512]{2,1,0:T(8,128)(2,1)S(1)}, u32[]{:S(2)}, u32[]{:S(2)}) %collective-permute-start.5) | collective-permute-done | bytes 18464 | tf_op jit(solution)/shard_map/ppermute | solution.py:525
  84.8 1.0 share_copies.1
  85.7 4.2 %all-to-all-start.1 = ((bf16[8,16,2048]{2,1,0:T(8,128)(2,1)}), bf16[8,16,2048]{2,1,0:T(8,128)(2,1)S(1)}, u32[]{:S(2)}, u32[]{:S(2)}) async-start(bf16[8,16,2048]{2,1,0:T(8,128)(2,1)} %share_copies.1), calls=%async_computation.1 | async-start | bytes 1048576 | tf_op jit(solution)/shard_map/all_to_all | solution.py:561
  89.9 6.9 %collective-permute-done.6 = bf16[21,6,512]{2,1,0:T(8,128)(2,1)S(1)} collective-permute-done((bf16[21,6,512]{2,1,0:T(8,128)(2,1)S(1)}, bf16[21,6,512]{2,1,0:T(8,128)(2,1)S(1)}, u32[]{:S(2)}, u32[]{:S(2)}) %collective-permute-start.6) | collective-permute-done | bytes 129056 | tf_op jit(solution)/shard_map/ppermute | solution.py:525
  96.8 1.0 %maximum_maximum_fusion = bf16[24,24,512]{2,1,0:T(8,128)(2,1)} fusion(bf16[21,18,512]{2,1,0:T(8,128)(2,1)S(1)} %slice.78, bf16[21,6,512]{2,1,0:T(8,128)(2,1)S(1)} %collective-permute-done.6, bf16[3,18,512]{2,1,0:T(8,128)(2,1)S(1)} %collective-permute-done.4, bf16[3,6,512]{2,1,0:T(8,128)(2,1)S(1)} %collective-permute-done.5), kind=kLoop, calls=%fused_computation.3 | loop fusion | flops 2359296 | bytes 1179648 | tf_op jit(solution)/shard_map/concatenate | solution.py:559
  97.8 4.1 %all-to-all-done.1.in_ref = bf16[8,16,2048]{2,1,0:T(8,128)(2,1)S(1)} async-done(((bf16[8,16,2048]{2,1,0:T(8,128)(2,1)}), bf16[8,16,2048]{2,1,0:T(8,128)(2,1)S(1)}, u32[]{:S(2)}, u32[]{:S(2)}) %all-to-all-start.1) | async-done | bytes 524320 | tf_op jit(solution)/shard_map/all_to_all | solution.py:561
  101.9 0.7 total_sum.1
  (53 shorter events, 1.3 us)
Async XLA Ops:
  0.6 6.7 %copy-start.15 = (bf16[24,24,512]{2,1,0:T(8,128)(2,1)S(1)}, bf16[24,24,512]{2,1,0:T(8,128)(2,1)}, u32[]{:S(2)}) copy-start(bf16[24,24,512]{2,1,0:T(8,128)(2,1)} %param.18) | copy-start | bytes 1769476
  0.6 6.8 %copy-start.16 = (bf16[24,24,512]{2,1,0:T(8,128)(2,1)S(1)}, bf16[24,24,512]{2,1,0:T(8,128)(2,1)}, u32[]{:S(2)}) copy-start(bf16[24,24,512]{2,1,0:T(8,128)(2,1)} %param.19) | copy-start | bytes 1769476
  2.7 9.9 %collective-permute-start = (bf16[48,6,512]{2,1,0:T(8,128)(2,1)S(1)}, bf16[48,6,512]{2,1,0:T(8,128)(2,1)S(1)}, u32[]{:S(2)}, u32[]{:S(2)}) collective-permute-start(bf16[48,6,512]{2,1,0:T(8,128)(2,1)S(1)} %pad_maximum_fusion.2), channel_id=1, source_target_pairs={{0,31},{1,0},{2,1},{3,2},{4,3},{5,4},{6,5},{7,6},{8,7},{9,8},{10,9... | collective-permute-start | bytes 884744 | tf_op jit(solution)/shard_map/ppermute | solution.py:525
  12.7 5.5 %copy-start.7 = (bf16[512,512]{1,0:T(8,128)(2,1)S(1)}, bf16[512,512]{1,0:T(8,128)(2,1)}, u32[]{:S(2)}) copy-start(bf16[512,512]{1,0:T(8,128)(2,1)} %wproj_hbm.1) | copy-start | bytes 1572868
  12.7 5.5 %copy-start.2 = (bf16[512,1536]{1,0:T(8,128)(2,1)S(1)}, bf16[512,1536]{1,0:T(8,128)(2,1)}, u32[]{:S(2)}) copy-start(bf16[512,1536]{1,0:T(8,128)(2,1)} %wqkv_ref.1) | copy-start | bytes 4718596
  12.7 5.5 %copy-start.4 = (bf16[160,144]{1,0:T(8,128)(2,1)S(1)}, bf16[160,144]{1,0:T(8,128)(2,1)}, u32[]{:S(2)}) copy-start(bf16[160,144]{1,0:T(8,128)(2,1)} %constant.14.clone.px_ref) | copy-start | bytes 138244
  12.7 5.5 %copy-start.6 = (f32[512]{0:T(512)S(1)}, f32[512]{0:T(512)}, u32[]{:S(2)}) copy-start(f32[512]{0:T(512)} %param.20) | copy-start | bytes 6148
  12.7 13.3 %collective-permute-start.1 = (bf16[13,24,512]{2,1,0:T(8,128)(2,1)S(1)}, bf16[13,24,512]{2,1,0:T(8,128)(2,1)S(1)}, u32[]{:S(2)}, u32[]{:S(2)}) collective-permute-start(bf16[13,24,512]{2,1,0:T(8,128)(2,1)S(1)} %fusion.2), channel_id=1, source_target_pairs={{0,224},{1,225},{2,226},{3,227},{4,228},{5,229},{6,230},{7,231},{8... | collective-permute-start | bytes 958472 | tf_op jit(solution)/shard_map/ppermute | solution.py:525
  18.0 8.0 %collective-permute-start.2 = (bf16[3,24,512]{2,1,0:T(8,128)(2,1)S(1)}, bf16[3,24,512]{2,1,0:T(8,128)(2,1)S(1)}, u32[]{:S(2)}, u32[]{:S(2)}) collective-permute-start(bf16[3,24,512]{2,1,0:T(8,128)(2,1)S(1)} %pad_maximum_fusion.4), channel_id=1, source_target_pairs={{0,32},{1,33},{2,34},{3,35},{4,36},{5,37},{6,38},{7,39},{8,40},{9,... | collective-permute-start | bytes 221192 | tf_op jit(solution)/shard_map/ppermute | solution.py:525
  26.1 1.2 %copy-start.10 = (bf16[9,192,160]{2,1,0:T(8,128)(2,1)S(1)}, bf16[9,192,160]{2,1,0:T(8,128)(2,1)}, u32[]{:S(2)}) copy-start(bf16[9,192,160]{2,1,0:T(8,128)(2,1)} %constant.16.clone.pf_ref) | copy-start | bytes 1658884
  26.1 1.2 %copy-start.11 = (bf16[4,160,256]{2,1,0:T(8,128)(2,1)S(1)}, bf16[4,160,256]{2,1,0:T(8,128)(2,1)}, u32[]{:S(2)}) copy-start(bf16[4,160,256]{2,1,0:T(8,128)(2,1)} %constant.19.clone.pi_ref) | copy-start | bytes 983044
  26.2 1.2 %copy-start.12 = (bf16[192,192]{1,0:T(8,128)(2,1)S(1)}, bf16[192,192]{1,0:T(8,128)(2,1)}, u32[]{:S(2)}) copy-start(bf16[192,192]{1,0:T(8,128)(2,1)} %constant.17.clone.pc_ref) | copy-start | bytes 221188
  26.2 1.3 %copy-start.13 = (bf16[160,144]{1,0:T(8,128)(2,1)S(1)}, bf16[160,144]{1,0:T(8,128)(2,1)}, u32[]{:S(2)}) copy-start(bf16[160,144]{1,0:T(8,128)(2,1)} %constant.15.clone.pxu_ref) | copy-start | bytes 138244
  26.2 1.2 %copy-start.14 = (bf16[64,48]{1,0:T(8,128)(2,1)S(1)}, bf16[64,48]{1,0:T(8,128)(2,1)}, u32[]{:S(2)}) copy-start(bf16[64,48]{1,0:T(8,128)(2,1)} %constant.18.clone.pc3_ref) | copy-start | bytes 18436
  46.5 3.8 %copy-start = (bf16[640,1536]{1,0:T(8,128)(2,1)}, bf16[640,1536]{1,0:T(8,128)(2,1)S(1)}, u32[]{:S(2)}) copy-start(bf16[640,1536]{1,0:T(8,128)(2,1)S(1)} %get-tuple-element.44.dqkv_ref) | copy-start | bytes 5898244
  46.5 2.7 %collective-permute-start.3 = (bf16[16,16,2048]{2,1,0:T(8,128)(2,1)S(1)}, bf16[16,16,2048]{2,1,0:T(8,128)(2,1)S(1)}, u32[]{:S(2)}, u32[]{:S(2)}) collective-permute-start(bf16[16,16,2048]{2,1,0:T(8,128)(2,1)S(1)} %get-tuple-element.40), channel_id=1, source_target_pairs={{0,1},{1,0},{2,3},{3,2},{4,5},{5,4},{6,7},{7,6},{8,9},{9,8},{10,11... | collective-permute-start | bytes 3145736 | tf_op jit(solution)/shard_map/ppermute | solution.py:546
  50.3 5.8 %copy-start.5 = (bf16[144,160]{1,0:T(8,128)(2,1)S(1)}, bf16[144,160]{1,0:T(8,128)(2,1)}, u32[]{:S(2)}) copy-start(bf16[144,160]{1,0:T(8,128)(2,1)} %constant.20.clone.pxt_ref) | copy-start | bytes 138244
  50.3 34.5 %all-to-all-start = ((bf16[16,16,2048]{2,1,0:T(8,128)(2,1)}), bf16[16,16,2048]{2,1,0:T(8,128)(2,1)S(1)}, u32[]{:S(2)}, u32[]{:S(2)}) async-start(bf16[16,16,2048]{2,1,0:T(8,128)(2,1)} %pair_sum.1), calls=%async_computation | async-start | bytes 2097152 | tf_op jit(solution)/shard_map/all_to_all | solution.py:548
  56.1 1.5 %copy-start.1 = (bf16[640,1536]{1,0:T(8,128)(2,1)S(1)}, bf16[640,1536]{1,0:T(8,128)(2,1)}, u32[]{:S(2)}) copy-start(bf16[640,1536]{1,0:T(8,128)(2,1)} %copy-done) | copy-start | bytes 5898244
  57.6 1.4 %copy-start.3 = (bf16[512,1536]{1,0:T(8,128)(2,1)S(1)}, bf16[512,1536]{1,0:T(8,128)(2,1)}, u32[]{:S(2)}) copy-start(bf16[512,1536]{1,0:T(8,128)(2,1)} %wqkv_ref.1) | copy-start | bytes 4718596
  62.2 22.6 %collective-permute-start.4 = (bf16[3,18,512]{2,1,0:T(8,128)(2,1)S(1)}, bf16[3,18,512]{2,1,0:T(8,128)(2,1)S(1)}, u32[]{:S(2)}, u32[]{:S(2)}) collective-permute-start(bf16[3,18,512]{2,1,0:T(8,128)(2,1)S(1)} %slice.75), channel_id=1, source_target_pairs={{0,32},{1,33},{2,34},{3,35},{4,36},{5,37},{6,38},{7,39},{8,40},{9,... | collective-permute-start | bytes 165896 | tf_op jit(solution)/shard_map/ppermute | solution.py:525
  65.0 19.7 %collective-permute-start.5 = (bf16[3,6,512]{2,1,0:T(8,128)(2,1)S(1)}, bf16[3,6,512]{2,1,0:T(8,128)(2,1)S(1)}, u32[]{:S(2)}, u32[]{:S(2)}) collective-permute-start(bf16[3,6,512]{2,1,0:T(8,128)(2,1)S(1)} %slice.76), channel_id=1, source_target_pairs={{0,33},{1,34},{2,35},{3,36},{4,37},{5,38},{6,39},{7,40},{8,41},{9,... | collective-permute-start | bytes 55304 | tf_op jit(solution)/shard_map/ppermute | solution.py:525
  85.7 16.2 %all-to-all-start.1 = ((bf16[8,16,2048]{2,1,0:T(8,128)(2,1)}), bf16[8,16,2048]{2,1,0:T(8,128)(2,1)S(1)}, u32[]{:S(2)}, u32[]{:S(2)}) async-start(bf16[8,16,2048]{2,1,0:T(8,128)(2,1)} %share_copies.1), calls=%async_computation.1 | async-start | bytes 1048576 | tf_op jit(solution)/shard_map/all_to_all | solution.py:561
  89.9 6.9 %collective-permute-start.6 = (bf16[21,6,512]{2,1,0:T(8,128)(2,1)S(1)}, bf16[21,6,512]{2,1,0:T(8,128)(2,1)S(1)}, u32[]{:S(2)}, u32[]{:S(2)}) collective-permute-start(bf16[21,6,512]{2,1,0:T(8,128)(2,1)S(1)} %slice.77), channel_id=1, source_target_pairs={{0,1},{1,2},{2,3},{3,4},{4,5},{5,6},{6,7},{7,8},{8,9},{9,10},{10,1... | collective-permute-start | bytes 387080 | tf_op jit(solution)/shard_map/ppermute | solution.py:525
  (2 other events, 1.4 us)

commit v9 on v8

--- a/solution.py
+++ b/solution.py
@@ -216,10 +216,10 @@
 
 
 def kernel(
-    lat_size, x_ref, c_ref, ng_ref, mg_ref, eg_ref, px_ref, pxu_ref, pf_ref, pc_ref, pc3_ref, pi_ref,
+    lat_size, x_ref, c_ref, ng_ref, mg_ref, eg_ref, px_ref, pxu_ref, pf_hbm, pc_ref, pc3_ref, pi_ref,
     wqkv_hbm, wproj_hbm, wm_hbm, we_hbm, normed_hbm, qkv_hbm, probs_hbm, attn_hbm, fine_hbm,
     mine_hbm, other_hbm, gn_hbm, dqkv_hbm,
-    wqkv, wproj, wm, we, xw, normed, qkv, probs, attn, fine, fq, hats, cq, mg, dw, gq, gn, d_attn, dqkv, mine, other, sems,
+    pf_ref, wqkv, wproj, wm, we, xw, normed, qkv, probs, attn, fine, fq, hats, cq, mg, dw, gq, gn, d_attn, dqkv, mine, other, sems,
 ):
     lat = lax.axis_index("lat")
     core = lax.axis_index("core")
@@ -227,7 +227,7 @@
     sources = (
         (wqkv_hbm, wqkv), (wproj_hbm, wproj), (fine_hbm, fine.at[done]), (wm_hbm, wm), (we_hbm, we),
         (probs_hbm, probs.at[0:EARLY]), (qkv_hbm, qkv.at[done]),
-        (attn_hbm, attn.at[done]), (normed_hbm, normed.at[done]),
+        (attn_hbm, attn.at[done]), (normed_hbm, normed.at[done]), (pf_hbm, pf_ref),
     )
     loads = [pltpu.make_async_copy(src, dst, sems.at[i]) for i, (src, dst) in enumerate(sources)]
     for load in loads:
@@ -248,6 +248,7 @@
     loads[1].wait()
     attention(EARLY, 1, masked_at, upper, x_ref, (px_ref, px_ref, pxu_ref), ng_ref, wqkv, wproj, xw, normed, qkv, probs, attn, fine)
     loads[2].wait()
+    loads[9].wait()
 
     for g in range(4):
         n = 48 if g < 3 else 16
@@ -322,7 +323,7 @@
     stores = []
 
     def store(src, dst):
-        copy = pltpu.make_async_copy(src, dst, sems.at[9 + len(stores)])
+        copy = pltpu.make_async_copy(src, dst, sems.at[10 + len(stores)])
         copy.start()
         stores.append(copy)
 
@@ -335,7 +336,7 @@
         store(other.at[:, :, columns], other_hbm.at[:, :, columns])
         store(mine.at[:, :, columns], mine_hbm.at[:, :, columns])
 
-    for load in loads[5:]:
+    for load in loads[5:9]:
         load.wait()
     inner = slice(0, 4 * WRP)
     store(gn, gn_hbm)
@@ -418,15 +419,16 @@
         out_shape=tuple(
             jax.ShapeDtypeStruct(shape, BF) for shape in (share, share, (4 * WRP, D), (4 * WRP, 3 * D))
         ),
-        in_specs=[VMEM] * 11 + [HBM] * 9,
+        in_specs=[VMEM] * 7 + [HBM] + [VMEM] * 3 + [HBM] * 9,
         out_specs=(HBM,) * 4,
         scratch_shapes=[
+            bf(len(FINE_PARTS), 4 * 48, WRP),
             bf(D, 3 * D), bf(D, D), bf(4 * D, 2 * D), bf(2 * D, 4 * D),
             bf((NWR - EARLY) * WRP, D), bf(NWR * WRP, D), bf(NWR * WRP, 3 * D), pltpu.VMEM((EARLY + 1, HEADS, WIN, 256), F32),
             bf(NWR * WRP, D), bf(NWR * WRP, D),
             bf(4, QROWS, D), pltpu.VMEM((4, QROWS, D), F32), bf(4, QROWS, D), bf(QROWS, 4 * D), bf(QROWS, 4 * D), bf(4, QROWS, D),
             bf(4 * WRP, D), bf(4 * WRP, D), bf(4 * WRP, 3 * D), bf(*share), bf(*share),
-            pltpu.SemaphoreType.DMA((19,)),
+            pltpu.SemaphoreType.DMA((20,)),
         ],
         compiler_params=pltpu.CompilerParams(vmem_limit_bytes=GRANT),
         cost_estimate=pl.CostEstimate(flops=7_000_000_000, bytes_accessed=18_000_000, transcendentals=0),

time: 103 us -> 103 us (level)
  transfers between devices with their start and end apart: 9 -> 9, of which waited for: 6 -> 6; matrix products, arithmetic and copies ran while one was open for 2% -> 1% of each run, Pallas kernels for 7% -> 7%
where the time goes in v9:
time: 103 us
  waiting for transfers between devices  41.9 us (41%)
  Pallas kernels  29.1 us (28%)
  starting transfers between devices  22.9 us (22%)
  local copies, waits for them, and re-layouts  6.52 us (6%)
  other arithmetic  1.44 us (1%)
    ppermute x6, waiting for transfers between devices, moved(): return lax.ppermute(value, names, pairs)  35.2 us
    pallas_call x1, Pallas kernels, compute(): pl.pallas_call(functools.partial(kernel, lats), out_shape=tuple((jax.Shap...  19.2 us
    ppermute x6, starting transfers between devices, moved(): return lax.ppermute(value, names, pairs)  12.8 us
    all_to_all x1, starting transfers between devices, body(): spread = lax.all_to_all(pair, 'tile', 0, 0, tiled=True)  5.78 us
    all_to_all x1, starting transfers between devices, body(): lax.all_to_all(share_copies(spread, lats), 'lat', 0, 0, tiled=True)  4.15 us
    unnamed x34, local copies, waits for them, and re-layouts  4.08 us
    all_to_all x1, waiting for transfers between devices, body(): lax.all_to_all(share_copies(spread, lats), 'lat', 0, 0, tiled=True)  4.06 us
    pallas_call x1, Pallas kernels, start_early(): pl.pallas_call(early_kernel, out_shape=tuple((jax.ShapeDtypeStruct(*one)...  4.02 us
  transfers between devices with their start and end apart: 9, of which 6 were waited for; matrix products, arithmetic and copies ran while one was open for 1% of the time, Pallas kernels for 7%

profile of v9, /device:TPU:0, one launch (start us, length us, event | category | flops | bytes accessed | tf_op | source)
XLA Modules:
  0.0 102.8 jit_solution(2075158887236553256)
XLA Ops:
  0.7 1.0 %slice.53 = bf16[24,6,512]{2,1,0:T(8,128)(2,1)S(1)} slice(bf16[24,24,512]{2,1,0:T(8,128)(2,1)} %param.18), slice={[0:24], [0:6], [0:512]} | slice | bytes 294912 | tf_op jit(solution)/shard_map/slice | solution.py:529
  1.7 0.9 slice.54
  2.7 4.6 %collective-permute-start = (bf16[48,6,512]{2,1,0:T(8,128)(2,1)S(1)}, bf16[48,6,512]{2,1,0:T(8,128)(2,1)S(1)}, u32[]{:S(2)}, u32[]{:S(2)}) collective-permute-start(bf16[48,6,512]{2,1,0:T(8,128)(2,1)S(1)} %pad_maximum_fusion.2), channel_id=1, source_target_pairs={{0,31},{1,0},{2,1},{3,2},{4,3},{5,4},{6,5},{7,6},{8,7},{9,8},{10,9... | collective-permute-start | bytes 884744 | tf_op jit(solution)/shard_map/ppermute | solution.py:527
  7.6 5.0 %collective-permute-done = bf16[48,6,512]{2,1,0:T(8,128)(2,1)S(1)} collective-permute-done((bf16[48,6,512]{2,1,0:T(8,128)(2,1)S(1)}, bf16[48,6,512]{2,1,0:T(8,128)(2,1)S(1)}, u32[]{:S(2)}, u32[]{:S(2)}) %collective-permute-start) | collective-permute-done | bytes 294944 | tf_op jit(solution)/shard_map/ppermute | solution.py:527
  12.7 5.3 %collective-permute-start.1 = (bf16[13,24,512]{2,1,0:T(8,128)(2,1)S(1)}, bf16[13,24,512]{2,1,0:T(8,128)(2,1)S(1)}, u32[]{:S(2)}, u32[]{:S(2)}) collective-permute-start(bf16[13,24,512]{2,1,0:T(8,128)(2,1)S(1)} %fusion.2), channel_id=1, source_target_pairs={{0,224},{1,225},{2,226},{3,227},{4,228},{5,229},{6,230},{7,231},{8... | collective-permute-start | bytes 958472 | tf_op jit(solution)/shard_map/ppermute | solution.py:527
  18.2 4.0 %block_early.1 = (bf16[480,512]{1,0:T(8,128)(2,1)S(1)}, bf16[480,1536]{1,0:T(8,128)(2,1)S(1)}, f32[3,8,72,256]{3,2,1,0:T(8,128)S(1)}, bf16[480,512]{1,0:T(8,128)(2,1)S(1)}, bf16[480,512]{1,0:T(8,128)(2,1)S(1)}) custom-call(bf16[432,512]{1,0:T(8,128)(2,1)S(1)} %bitcast.11, bf16[160,144]{1,0:T(8,128)(2,1)S(1)} %copy-done.4, f32[1,512]{1,0:T(1,128)S(1)} %bitcast.16, ...), custom_call_target="tpu_custom_call" | custom-call | flops 1400000000 | bytes 8000000 | tf_op jit(solution)/shard_map/block_early/pallas_call | solution.py:402
  22.3 3.8 %collective-permute-done.2 = bf16[3,24,512]{2,1,0:T(8,128)(2,1)S(1)} collective-permute-done((bf16[3,24,512]{2,1,0:T(8,128)(2,1)S(1)}, bf16[3,24,512]{2,1,0:T(8,128)(2,1)S(1)}, u32[]{:S(2)}, u32[]{:S(2)}) %collective-permute-start.2) | collective-permute-done | bytes 73760 | tf_op jit(solution)/shard_map/ppermute | solution.py:527
  26.4 0.4 copy-done.8
  26.8 0.5 copy-done.10
  27.4 19.2 %block.1 = (bf16[16,16,2048]{2,1,0:T(8,128)(2,1)S(1)}, bf16[16,16,2048]{2,1,0:T(8,128)(2,1)S(1)}, bf16[640,512]{1,0:T(8,128)(2,1)S(1)}, bf16[640,1536]{1,0:T(8,128)(2,1)S(1)}) custom-call(bf16[432,512]{1,0:T(8,128)(2,1)S(1)} %bitcast.13, bf16[672,512]{1,0:T(8,128)(2,1)S(1)} %bitcast.15, f32[1,512]{1,0:T(1,128)S(1)} %bitcast.17, f32[1,2048]{1,0:T(1,128)S(1)} %bitcast.19, ...), custom_call_target="tpu_custom_call" | custom-call | flops 7000000000 | bytes 18000000 | tf_op jit(solution)/shard_map/block/pallas_call | solution.py:417
  46.8 2.6 %collective-permute-done.3.b_ref = bf16[16,16,2048]{2,1,0:T(8,128)(2,1)S(1)} collective-permute-done((bf16[16,16,2048]{2,1,0:T(8,128)(2,1)S(1)}, bf16[16,16,2048]{2,1,0:T(8,128)(2,1)S(1)}, u32[]{:S(2)}, u32[]{:S(2)}) %collective-permute-start.3) | collective-permute-done | bytes 1048608 | tf_op jit(solution)/shard_map/ppermute | solution.py:548
  49.4 1.1 %pair_sum.1 = bf16[16,16,2048]{2,1,0:T(8,128)(2,1)} custom-call(bf16[16,16,2048]{2,1,0:T(8,128)(2,1)S(1)} %get-tuple-element.39.a_ref, bf16[16,16,2048]{2,1,0:T(8,128)(2,1)S(1)} %collective-permute-done.3.b_ref), custom_call_target="tpu_custom_call" | custom-call | tf_op jit(solution)/shard_map/pair_sum/pallas_call | solution.py:462
  50.5 5.8 %all-to-all-start = ((bf16[16,16,2048]{2,1,0:T(8,128)(2,1)}), bf16[16,16,2048]{2,1,0:T(8,128)(2,1)S(1)}, u32[]{:S(2)}, u32[]{:S(2)}) async-start(bf16[16,16,2048]{2,1,0:T(8,128)(2,1)} %pair_sum.1), calls=%async_computation | async-start | bytes 2097152 | tf_op jit(solution)/shard_map/all_to_all | solution.py:550
  56.3 1.5 %copy-done.1 = bf16[640,1536]{1,0:T(8,128)(2,1)S(1)} copy-done((bf16[640,1536]{1,0:T(8,128)(2,1)S(1)}, bf16[640,1536]{1,0:T(8,128)(2,1)}, u32[]{:S(2)}) %copy-start.1) | copy-done | bytes 1966104
  57.9 1.4 %copy-done.3 = bf16[512,1536]{1,0:T(8,128)(2,1)S(1)} copy-done((bf16[512,1536]{1,0:T(8,128)(2,1)S(1)}, bf16[512,1536]{1,0:T(8,128)(2,1)}, u32[]{:S(2)}) %copy-start.3) | copy-done | bytes 1572888
  59.3 3.1 %block_tokens.1 = bf16[576,512]{1,0:T(8,128)(2,1)S(1)} custom-call(bf16[432,512]{1,0:T(8,128)(2,1)S(1)} %bitcast.12, bf16[432,512]{1,0:T(8,128)(2,1)S(1)} %bitcast.14, bf16[640,512]{1,0:T(8,128)(2,1)S(1)} %get-tuple-element.43.gn_ref, bf16[640,1536]{1,0:T(8,128)(2,1)S(1)} %copy-done.1, bf16[512,1536]{1,0:T(8,128)(2,1)S(1)} %copy-done.3, ...), custom_call_target="tpu_custom_call" | custom-call | flops 1200000000 | bytes 6000000 | tf_op jit(solution)/shard_map/block_tokens/pallas_call | solution.py:445
  62.4 2.8 %collective-permute-start.4 = (bf16[3,18,512]{2,1,0:T(8,128)(2,1)S(1)}, bf16[3,18,512]{2,1,0:T(8,128)(2,1)S(1)}, u32[]{:S(2)}, u32[]{:S(2)}) collective-permute-start(bf16[3,18,512]{2,1,0:T(8,128)(2,1)S(1)} %slice.75), channel_id=1, source_target_pairs={{0,32},{1,33},{2,34},{3,35},{4,36},{5,37},{6,38},{7,39},{8,40},{9,... | collective-permute-start | bytes 165896 | tf_op jit(solution)/shard_map/ppermute | solution.py:527
  65.4 19.6 %collective-permute-done.5 = bf16[3,6,512]{2,1,0:T(8,128)(2,1)S(1)} collective-permute-done((bf16[3,6,512]{2,1,0:T(8,128)(2,1)S(1)}, bf16[3,6,512]{2,1,0:T(8,128)(2,1)S(1)}, u32[]{:S(2)}, u32[]{:S(2)}) %collective-permute-start.5) | collective-permute-done | bytes 18464 | tf_op jit(solution)/shard_map/ppermute | solution.py:527
  85.0 1.0 share_copies.1
  85.9 4.2 %all-to-all-start.1 = ((bf16[8,16,2048]{2,1,0:T(8,128)(2,1)}), bf16[8,16,2048]{2,1,0:T(8,128)(2,1)S(1)}, u32[]{:S(2)}, u32[]{:S(2)}) async-start(bf16[8,16,2048]{2,1,0:T(8,128)(2,1)} %share_copies.1), calls=%async_computation.1 | async-start | bytes 1048576 | tf_op jit(solution)/shard_map/all_to_all | solution.py:563
  90.2 6.9 %collective-permute-done.6 = bf16[21,6,512]{2,1,0:T(8,128)(2,1)S(1)} collective-permute-done((bf16[21,6,512]{2,1,0:T(8,128)(2,1)S(1)}, bf16[21,6,512]{2,1,0:T(8,128)(2,1)S(1)}, u32[]{:S(2)}, u32[]{:S(2)}) %collective-permute-start.6) | collective-permute-done | bytes 129056 | tf_op jit(solution)/shard_map/ppermute | solution.py:527
  97.0 1.0 %maximum_maximum_fusion = bf16[24,24,512]{2,1,0:T(8,128)(2,1)} fusion(bf16[21,18,512]{2,1,0:T(8,128)(2,1)S(1)} %slice.78, bf16[21,6,512]{2,1,0:T(8,128)(2,1)S(1)} %collective-permute-done.6, bf16[3,18,512]{2,1,0:T(8,128)(2,1)S(1)} %collective-permute-done.4, bf16[3,6,512]{2,1,0:T(8,128)(2,1)S(1)} %collective-permute-done.5), kind=kLoop, calls=%fused_computation.3 | loop fusion | flops 2359296 | bytes 1179648 | tf_op jit(solution)/shard_map/concatenate | solution.py:561
  98.1 4.1 %all-to-all-done.1.in_ref = bf16[8,16,2048]{2,1,0:T(8,128)(2,1)S(1)} async-done(((bf16[8,16,2048]{2,1,0:T(8,128)(2,1)}), bf16[8,16,2048]{2,1,0:T(8,128)(2,1)S(1)}, u32[]{:S(2)}, u32[]{:S(2)}) %all-to-all-start.1) | async-done | bytes 524320 | tf_op jit(solution)/shard_map/all_to_all | solution.py:563
  102.1 0.7 total_sum.1
  (53 shorter events, 1.3 us)
Async XLA Ops:
  0.6 6.7 %copy-start.15 = (bf16[24,24,512]{2,1,0:T(8,128)(2,1)S(1)}, bf16[24,24,512]{2,1,0:T(8,128)(2,1)}, u32[]{:S(2)}) copy-start(bf16[24,24,512]{2,1,0:T(8,128)(2,1)} %param.18) | copy-start | bytes 1769476
  0.6 6.8 %copy-start.16 = (bf16[24,24,512]{2,1,0:T(8,128)(2,1)S(1)}, bf16[24,24,512]{2,1,0:T(8,128)(2,1)}, u32[]{:S(2)}) copy-start(bf16[24,24,512]{2,1,0:T(8,128)(2,1)} %param.19) | copy-start | bytes 1769476
  2.7 9.9 %collective-permute-start = (bf16[48,6,512]{2,1,0:T(8,128)(2,1)S(1)}, bf16[48,6,512]{2,1,0:T(8,128)(2,1)S(1)}, u32[]{:S(2)}, u32[]{:S(2)}) collective-permute-start(bf16[48,6,512]{2,1,0:T(8,128)(2,1)S(1)} %pad_maximum_fusion.2), channel_id=1, source_target_pairs={{0,31},{1,0},{2,1},{3,2},{4,3},{5,4},{6,5},{7,6},{8,7},{9,8},{10,9... | collective-permute-start | bytes 884744 | tf_op jit(solution)/shard_map/ppermute | solution.py:527
  12.7 5.5 %copy-start.7 = (bf16[512,512]{1,0:T(8,128)(2,1)S(1)}, bf16[512,512]{1,0:T(8,128)(2,1)}, u32[]{:S(2)}) copy-start(bf16[512,512]{1,0:T(8,128)(2,1)} %wproj_hbm.1) | copy-start | bytes 1572868
  12.7 5.5 %copy-start.2 = (bf16[512,1536]{1,0:T(8,128)(2,1)S(1)}, bf16[512,1536]{1,0:T(8,128)(2,1)}, u32[]{:S(2)}) copy-start(bf16[512,1536]{1,0:T(8,128)(2,1)} %wqkv_ref.1) | copy-start | bytes 4718596
  12.7 5.5 %copy-start.4 = (bf16[160,144]{1,0:T(8,128)(2,1)S(1)}, bf16[160,144]{1,0:T(8,128)(2,1)}, u32[]{:S(2)}) copy-start(bf16[160,144]{1,0:T(8,128)(2,1)} %constant.14.clone.px_ref) | copy-start | bytes 138244
  12.7 5.5 %copy-start.6 = (f32[512]{0:T(512)S(1)}, f32[512]{0:T(512)}, u32[]{:S(2)}) copy-start(f32[512]{0:T(512)} %param.20) | copy-start | bytes 6148
  12.7 13.3 %collective-permute-start.1 = (bf16[13,24,512]{2,1,0:T(8,128)(2,1)S(1)}, bf16[13,24,512]{2,1,0:T(8,128)(2,1)S(1)}, u32[]{:S(2)}, u32[]{:S(2)}) collective-permute-start(bf16[13,24,512]{2,1,0:T(8,128)(2,1)S(1)} %fusion.2), channel_id=1, source_target_pairs={{0,224},{1,225},{2,226},{3,227},{4,228},{5,229},{6,230},{7,231},{8... | collective-permute-start | bytes 958472 | tf_op jit(solution)/shard_map/ppermute | solution.py:527
  18.0 8.0 %collective-permute-start.2 = (bf16[3,24,512]{2,1,0:T(8,128)(2,1)S(1)}, bf16[3,24,512]{2,1,0:T(8,128)(2,1)S(1)}, u32[]{:S(2)}, u32[]{:S(2)}) collective-permute-start(bf16[3,24,512]{2,1,0:T(8,128)(2,1)S(1)} %pad_maximum_fusion.4), channel_id=1, source_target_pairs={{0,32},{1,33},{2,34},{3,35},{4,36},{5,37},{6,38},{7,39},{8,40},{9,... | collective-permute-start | bytes 221192 | tf_op jit(solution)/shard_map/ppermute | solution.py:527
  26.1 1.2 %copy-start.10 = (bf16[9,192,160]{2,1,0:T(8,128)(2,1)S(1)}, bf16[9,192,160]{2,1,0:T(8,128)(2,1)}, u32[]{:S(2)}) copy-start(bf16[9,192,160]{2,1,0:T(8,128)(2,1)} %constant.16.clone.pf_hbm) | copy-start | bytes 1658884
  26.1 1.2 %copy-start.11 = (bf16[4,160,256]{2,1,0:T(8,128)(2,1)S(1)}, bf16[4,160,256]{2,1,0:T(8,128)(2,1)}, u32[]{:S(2)}) copy-start(bf16[4,160,256]{2,1,0:T(8,128)(2,1)} %constant.19.clone.pi_ref) | copy-start | bytes 983044
  26.2 1.2 %copy-start.12 = (bf16[192,192]{1,0:T(8,128)(2,1)S(1)}, bf16[192,192]{1,0:T(8,128)(2,1)}, u32[]{:S(2)}) copy-start(bf16[192,192]{1,0:T(8,128)(2,1)} %constant.17.clone.pc_ref) | copy-start | bytes 221188
  26.2 1.3 %copy-start.13 = (bf16[160,144]{1,0:T(8,128)(2,1)S(1)}, bf16[160,144]{1,0:T(8,128)(2,1)}, u32[]{:S(2)}) copy-start(bf16[160,144]{1,0:T(8,128)(2,1)} %constant.15.clone.pxu_ref) | copy-start | bytes 138244
  26.2 1.2 %copy-start.14 = (bf16[64,48]{1,0:T(8,128)(2,1)S(1)}, bf16[64,48]{1,0:T(8,128)(2,1)}, u32[]{:S(2)}) copy-start(bf16[64,48]{1,0:T(8,128)(2,1)} %constant.18.clone.pc3_ref) | copy-start | bytes 18436
  46.7 3.8 %copy-start = (bf16[640,1536]{1,0:T(8,128)(2,1)}, bf16[640,1536]{1,0:T(8,128)(2,1)S(1)}, u32[]{:S(2)}) copy-start(bf16[640,1536]{1,0:T(8,128)(2,1)S(1)} %get-tuple-element.44.dqkv_ref) | copy-start | bytes 5898244
  46.7 2.7 %collective-permute-start.3 = (bf16[16,16,2048]{2,1,0:T(8,128)(2,1)S(1)}, bf16[16,16,2048]{2,1,0:T(8,128)(2,1)S(1)}, u32[]{:S(2)}, u32[]{:S(2)}) collective-permute-start(bf16[16,16,2048]{2,1,0:T(8,128)(2,1)S(1)} %get-tuple-element.40), channel_id=1, source_target_pairs={{0,1},{1,0},{2,3},{3,2},{4,5},{5,4},{6,7},{7,6},{8,9},{9,8},{10,11... | collective-permute-start | bytes 3145736 | tf_op jit(solution)/shard_map/ppermute | solution.py:548
  50.5 5.8 %copy-start.5 = (bf16[144,160]{1,0:T(8,128)(2,1)S(1)}, bf16[144,160]{1,0:T(8,128)(2,1)}, u32[]{:S(2)}) copy-start(bf16[144,160]{1,0:T(8,128)(2,1)} %constant.20.clone.pxt_ref) | copy-start | bytes 138244
  50.5 34.5 %all-to-all-start = ((bf16[16,16,2048]{2,1,0:T(8,128)(2,1)}), bf16[16,16,2048]{2,1,0:T(8,128)(2,1)S(1)}, u32[]{:S(2)}, u32[]{:S(2)}) async-start(bf16[16,16,2048]{2,1,0:T(8,128)(2,1)} %pair_sum.1), calls=%async_computation | async-start | bytes 2097152 | tf_op jit(solution)/shard_map/all_to_all | solution.py:550
  56.3 1.5 %copy-start.1 = (bf16[640,1536]{1,0:T(8,128)(2,1)S(1)}, bf16[640,1536]{1,0:T(8,128)(2,1)}, u32[]{:S(2)}) copy-start(bf16[640,1536]{1,0:T(8,128)(2,1)} %copy-done) | copy-start | bytes 5898244
  57.9 1.4 %copy-start.3 = (bf16[512,1536]{1,0:T(8,128)(2,1)S(1)}, bf16[512,1536]{1,0:T(8,128)(2,1)}, u32[]{:S(2)}) copy-start(bf16[512,1536]{1,0:T(8,128)(2,1)} %wqkv_ref.1) | copy-start | bytes 4718596
  62.4 22.6 %collective-permute-start.4 = (bf16[3,18,512]{2,1,0:T(8,128)(2,1)S(1)}, bf16[3,18,512]{2,1,0:T(8,128)(2,1)S(1)}, u32[]{:S(2)}, u32[]{:S(2)}) collective-permute-start(bf16[3,18,512]{2,1,0:T(8,128)(2,1)S(1)} %slice.75), channel_id=1, source_target_pairs={{0,32},{1,33},{2,34},{3,35},{4,36},{5,37},{6,38},{7,39},{8,40},{9,... | collective-permute-start | bytes 165896 | tf_op jit(solution)/shard_map/ppermute | solution.py:527
  65.3 19.7 %collective-permute-start.5 = (bf16[3,6,512]{2,1,0:T(8,128)(2,1)S(1)}, bf16[3,6,512]{2,1,0:T(8,128)(2,1)S(1)}, u32[]{:S(2)}, u32[]{:S(2)}) collective-permute-start(bf16[3,6,512]{2,1,0:T(8,128)(2,1)S(1)} %slice.76), channel_id=1, source_target_pairs={{0,33},{1,34},{2,35},{3,36},{4,37},{5,38},{6,39},{7,40},{8,41},{9,... | collective-permute-start | bytes 55304 | tf_op jit(solution)/shard_map/ppermute | solution.py:527
  85.9 16.2 %all-to-all-start.1 = ((bf16[8,16,2048]{2,1,0:T(8,128)(2,1)}), bf16[8,16,2048]{2,1,0:T(8,128)(2,1)S(1)}, u32[]{:S(2)}, u32[]{:S(2)}) async-start(bf16[8,16,2048]{2,1,0:T(8,128)(2,1)} %share_copies.1), calls=%async_computation.1 | async-start | bytes 1048576 | tf_op jit(solution)/shard_map/all_to_all | solution.py:563
  90.1 6.9 %collective-permute-start.6 = (bf16[21,6,512]{2,1,0:T(8,128)(2,1)S(1)}, bf16[21,6,512]{2,1,0:T(8,128)(2,1)S(1)}, u32[]{:S(2)}, u32[]{:S(2)}) collective-permute-start(bf16[21,6,512]{2,1,0:T(8,128)(2,1)S(1)} %slice.77), channel_id=1, source_target_pairs={{0,1},{1,2},{2,3},{3,4},{4,5},{5,6},{6,7},{7,8},{8,9},{9,10},{10,1... | collective-permute-start | bytes 387080 | tf_op jit(solution)/shard_map/ppermute | solution.py:527
  (2 other events, 1.4 us)
